TPU v7x, 128 devices: a whole 4x4x4 slice. The times are simulated.
128 devices in a mesh: blk: 16 (over z, x_lo, core), head: 8 (over y, x_hi).
Axes of the slice: x: 4 (x_hi: 2, x_lo: 2; x = x_hi * 2 + x_lo), y: 4, z: 4, core: 2. Of those that a mesh axis runs over, the one named last changes fastest.
Arguments:
- inputs: bfloat16 [2, 8192, 1280], P(None, ('blk', 'head')), may hold values from -6 to 6
- segment_ids: int32 [2, 8192], replicated, may hold values from 0 to 8, as said below
- norm1_gain: bfloat16 [1280], P(('blk', 'head')), may hold values from 0.099609375 to 1.8984375
- w_query: bfloat16 [1280, 1280], P(('blk', 'head')), may hold values from -0.15625 to 0.15625
- w_key: bfloat16 [1280, 1280], P(('blk', 'head')), may hold values from -0.15625 to 0.15625
- w_value: bfloat16 [1280, 1280], P(('blk', 'head')), may hold values from -0.15625 to 0.15625
- query_bias: bfloat16 [1280], P(('blk', 'head')), may hold values from -3 to 3
- value_bias: bfloat16 [1280], P(('blk', 'head')), may hold values from -3 to 3
- w_out: bfloat16 [1280, 1280], P(('blk', 'head')), may hold values from -1.25 to 1.25
- out_bias: bfloat16 [1280], P(('blk', 'head')), may hold values from -3 to 3
- norm2_gain: bfloat16 [1280], P(('blk', 'head')), may hold values from 0.099609375 to 1.8984375
- w_hidden: bfloat16 [1280, 1280], P(('blk', 'head')), may hold values from -0.15625 to 0.15625
- hidden_bias: bfloat16 [1280], P(('blk', 'head')), may hold values from -3 to 3
- w_proj: bfloat16 [1280, 1280], P(('blk', 'head')), may hold values from -0.15625 to 0.15625
- proj_bias: bfloat16 [1280], P(('blk', 'head')), may hold values from -3 to 3
- dim_scale: float32 [80], replicated, may hold values from -1 to 1
- cotangent: bfloat16 [2, 8192, 1280], P(None, ('blk', 'head')), may hold values from -6 to 6
Outputs:
- layer_out: bfloat16 [2, 8192, 1280], P(None, ('blk', 'head'))
- input_grad: bfloat16 [2, 8192, 1280], P(None, ('blk', 'head'))
- norm1_gain_grad: float32 [1280], P(('blk', 'head'))
- w_query_grad: float32 [1280, 1280], P(('blk', 'head'))
- w_key_grad: float32 [1280, 1280], P(('blk', 'head'))
- w_value_grad: float32 [1280, 1280], P(('blk', 'head'))
- query_bias_grad: float32 [1280], P(('blk', 'head'))
- value_bias_grad: float32 [1280], P(('blk', 'head'))
- w_out_grad: float32 [1280, 1280], P(('blk', 'head'))
- out_bias_grad: float32 [1280], P(('blk', 'head'))
- norm2_gain_grad: float32 [1280], P(('blk', 'head'))
- w_hidden_grad: float32 [1280, 1280], P(('blk', 'head'))
- hidden_bias_grad: float32 [1280], P(('blk', 'head'))
- w_proj_grad: float32 [1280, 1280], P(('blk', 'head'))
- proj_bias_grad: float32 [1280], P(('blk', 'head'))
- dim_scale_grad: float32 [80], replicated
Inputs may be any that keep to these rules, and one draw needn't show every extreme that they name: `segment_ids`: ids never fall along a sequence. In each micro-batch one document starts before position 512 and ends at or after position 7680; the others are short and lie at the two ends.
All inputs are finite; a program needn't handle non-finite values.
Results may differ from a plain program's by a relative error of at most 0.024.
Values may be sent and summed in bfloat16 or wider, within the bound.
A program may use at most 256 MiB of HBM per device.

v0:
```python
import functools
import math

import jax
import jax.numpy as jnp
import numpy as np
from jax import lax
from jax.experimental import pallas as pl
from jax.experimental.pallas import tpu as pltpu
from jax.sharding import PartitionSpec as P

D = 1280
H = 16
HD = 80
FF = 1280
B = 512
TOK = 64
PAIRS = 32
LANES = 256
ROWS = 32
WIDE = H * LANES
OUT_WIDE = H * 128
GROUP = 80
EPSILON = 1e-06
LOG2E = 1.442695041
NEGATIVE = -1e30
MESH = pl.DeviceIdType.MESH
f32 = jnp.float32
bf16 = jnp.bfloat16

PARTS = (((0, 512), "xyz"), ((512, 384), "yzx"), ((896, 384), "zxy"))
PARTS_TWO = (((0, 640), "xyz"), ((640, 640), "xzy"))


def inverse_rms(values):
    return lax.rsqrt(jnp.mean(values * values, axis=-1, keepdims=True) + EPSILON)


def norm_back(upstream, values, inverse):
    return inverse * upstream - values * inverse**3 * jnp.mean(
        upstream * values, axis=-1, keepdims=True
    )


def nn(a, b):
    return lax.dot_general(a, b, (((1,), (0,)), ((), ())), preferred_element_type=f32)


def nt(a, b):
    return lax.dot_general(a, b, (((1,), (1,)), ((), ())), preferred_element_type=f32)


def tn(a, b):
    return lax.dot_general(a, b, (((0,), (0,)), ((), ())), preferred_element_type=f32)


def my_place():
    blk = lax.axis_index("blk")
    head = lax.axis_index("head")
    return {
        "x": (head % 2) * 2 + (blk // 2) % 2,
        "y": head // 2,
        "z": blk // 4,
        "c": blk % 2,
    }


def device_at(place):
    x, y, z, c = place["x"], place["y"], place["z"], place["c"]
    return (z * 4 + (x % 2) * 2 + c, y * 2 + x // 2)


def chunk_of(ref, place, cols, lead=()):
    blk, head = device_at(place)
    return ref.at[(*lead, blk, pl.ds(head * ROWS, ROWS), cols)]


def moved(place, axis, value):
    other = dict(place)
    other[axis] = value
    return other


def greet(peers):
    barrier = pltpu.get_barrier_semaphore()
    for peer in peers:
        pl.semaphore_signal(barrier, inc=1, device_id=peer, device_id_type=MESH)
    pl.semaphore_wait(barrier, len(peers))


def greet_all():
    barrier = pltpu.get_barrier_semaphore()
    me = lax.axis_index("blk") * 8 + lax.axis_index("head")

    @pl.loop(1, 128)
    def _(k):
        other = (me + k) % 128
        pl.semaphore_signal(
            barrier, inc=1, device_id=(other // 8, other % 8), device_id_type=MESH
        )

    pl.semaphore_wait(barrier, 127)


def ring_peers(place):
    peers = [device_at(moved(place, "c", 1 - place["c"]))]
    for axis in "xyz":
        for step in (1, 3, 2):
            peers.append(device_at(moved(place, axis, (place[axis] + step) % 4)))
    return peers


def wait_bytes(ref, sem):
    pltpu.make_async_copy(ref, ref, sem).wait()


def remote(src, dst, send, recv, device):
    return pltpu.make_async_remote_copy(
        src_ref=src, dst_ref=dst, send_sem=send, recv_sem=recv, device_id=device, device_id_type=MESH
    )


def varied(place, axes, number):
    other = dict(place)
    for axis in axes:
        other[axis] = number % 4
        number = number // 4
    return other


def selections():
    take = np.zeros((3, GROUP, 256), np.float32)
    last = np.zeros((5, GROUP, 256), np.float32)
    for i in range(8):
        for j in range(10):
            for w in range(3):
                take[w, i * 10 + j, i * ROWS + w * 10 + j] = 1
            last[j % 5, i * 10 + j, i * ROWS + 30 + j // 5] = 1
    spread = np.zeros((128, 256), np.float32)
    spread[32:112] = take[0]
    return take, last, spread


TAKE, LAST, SPREAD = selections()
LANE_OF = np.zeros((128, D), np.float32)
LANE_OF[112 + np.arange(D) % 10, np.arange(D)] = 1
ROW_OF = np.zeros((16, D), np.float32)
ROW_OF[np.arange(D) % 10, np.arange(D)] = 1
TENTH = (np.arange(D) // 10).astype(np.int32)
SCALE_ROWS = np.zeros((256, 16), np.float32)
for _i in range(8):
    for _j in range(8):
        SCALE_ROWS[_i * ROWS + _j, _j] = 1


class Gather:
    def __init__(self, parts, buf, send, recv, place):
        self.parts, self.place = parts, place
        self.buf, self.send, self.recv = buf, send, recv
        self.sibling = device_at(moved(place, "c", 1 - place["c"]))

    def begin(self, pack, sem):
        own = pltpu.make_async_copy(
            pack, chunk_of(self.buf, self.place, pl.ds(0, D)), sem
        )
        own.start()
        return own

    def forward(self, part, axes, fixed, count):
        first, width = self.parts[part][0]
        cols = pl.ds(first, width)

        @pl.loop(0, count)
        def _(number):
            where = dict(varied(self.place, axes, number), **fixed)
            piece = chunk_of(self.buf, where, cols)
            remote(
                piece, piece, self.send.at[part, 3], self.recv.at[part, 5], self.sibling
            ).start()

    def stage(self, stage):
        for part, ((first, width), order) in enumerate(self.parts):
            cols = pl.ds(first, width)
            if stage:
                wait_bytes(
                    self.buf.at[0, pl.ds(0, 3 * 4 ** (stage - 1) * ROWS), cols]
                    if stage == 1
                    else self.buf.at[pl.ds(0, 3), pl.ds(0, 4 * ROWS), cols],
                    self.recv.at[part, stage - 1],
                )

            @pl.loop(0, 4**stage)
            def _(number, part=part, cols=cols, order=order):
                piece = chunk_of(self.buf, varied(self.place, order[:stage], number), cols)
                axis = order[stage]
                for step in (1, 3, 2):
                    target = moved(self.place, axis, (self.place[axis] + step) % 4)
                    slot = stage if stage < 2 else 1 + step
                    remote(
                        piece,
                        piece,
                        self.send.at[part, stage],
                        self.recv.at[part, slot],
                        device_at(target),
                    ).start()

        for part, (_, order) in enumerate(self.parts):
            if stage == 0:
                self.forward(part, "", {}, 1)
            else:
                axis = order[stage - 1]
                for step in (1, 3, 2):
                    self.forward(
                        part,
                        order[: stage - 1],
                        {axis: (self.place[axis] + 4 - step) % 4},
                        4 ** (stage - 1),
                    )

    def finish(self):
        for step in (1, 3, 2):
            for part, ((first, width), order) in enumerate(self.parts):
                wait_bytes(
                    self.buf.at[pl.ds(0, 2), :, pl.ds(first, width)],
                    self.recv.at[part, 1 + step],
                )
                axis = order[2]
                self.forward(
                    part, order[:2], {axis: (self.place[axis] + 4 - step) % 4}, 16
                )
        for part, ((first, width), order) in enumerate(self.parts):
            cols = pl.ds(first, width)
            half = self.buf.at[pl.ds(0, 8), :, cols]
            wait_bytes(half, self.recv.at[part, 5])
            wait_bytes(half, self.send.at[part, 3])
            wait_bytes(self.buf.at[0, pl.ds(0, 3 * ROWS), cols], self.send.at[part, 0])
            wait_bytes(
                self.buf.at[pl.ds(0, 3), pl.ds(0, 4 * ROWS), cols], self.send.at[part, 1]
            )
            wait_bytes(self.buf.at[pl.ds(0, 6), :, cols], self.send.at[part, 2])


def row_block(ref, g, count):
    return ref.at[pl.ds(pl.multiple_of(g * count, 16), count)]


def gather_kernel(
    pack, take, last, lane_of, row_of, tenth_row, tenth_col, wide, vectors,
    buf, vec_tile, staged, send, recv, own_sem, out_sem,
):
    place = my_place()
    gather = Gather(PARTS, buf, send, recv, place)
    own = gather.begin(pack, own_sem)
    greet(ring_peers(place))
    own.wait()
    for stage in range(3):
        gather.stage(stage)
    gather.finish()

    @pl.loop(0, 16)
    def _(g):
        slot = g % 2
        out = pltpu.make_async_copy(staged.at[slot], row_block(wide, g, GROUP), out_sem.at[slot])

        @pl.when(g >= 2)
        def _():
            out.wait()

        for w in range(3):
            staged[slot, :, w * D : (w + 1) * D] = nn(take[w], buf[g]).astype(bf16)
        head = jnp.zeros((GROUP, LANES), f32)
        for cell in range(5):
            head = head + nn(last[cell], buf[g, :, cell * LANES : (cell + 1) * LANES])
        staged[slot, :, 3 * D :] = head.astype(bf16)
        vec_tile[pl.ds(pl.multiple_of(g * GROUP, 16), GROUP)] = staged[slot, :, 128:256]
        out.start()

    spread_out = nn(vec_tile[...], lane_of[...])
    spread_out = jnp.where(tenth_col[...] == tenth_row[...], spread_out, 0.0).astype(bf16)
    vectors[...] = nn(row_of[...], spread_out)
    for slot in range(2):
        pltpu.make_async_copy(staged.at[slot], row_block(wide, 0, GROUP), out_sem.at[slot]).wait()


VMEM = pl.BlockSpec(memory_space=pltpu.VMEM)
HBM = pl.BlockSpec(memory_space=pl.ANY)


def gather_semaphores(parts):
    return [pltpu.SemaphoreType.DMA((parts, 4)), pltpu.SemaphoreType.DMA((parts, 6))]


def gather_weights(pack):
    return pl.pallas_call(
        gather_kernel,
        out_shape=(
            jax.ShapeDtypeStruct((D, WIDE), bf16),
            jax.ShapeDtypeStruct((16, D), f32),
        ),
        in_specs=[VMEM] * 7,
        out_specs=(HBM, VMEM),
        scratch_shapes=[
            pltpu.VMEM((16, 256, D), bf16),
            pltpu.VMEM((D, 128), bf16),
            pltpu.VMEM((2, GROUP, WIDE), bf16),
        ]
        + gather_semaphores(3)
        + [
            pltpu.SemaphoreType.DMA,
            pltpu.SemaphoreType.DMA((2,)),
        ],
        compiler_params=pltpu.CompilerParams(
            collective_id=0, has_side_effects=True, vmem_limit_bytes=40 * 2**20
        ),
        name="gather_weights",
    )(
        pack,
        jnp.asarray(TAKE, bf16),
        jnp.asarray(LAST, bf16),
        jnp.asarray(LANE_OF, bf16),
        jnp.asarray(ROW_OF, bf16),
        jnp.asarray(TENTH[None, :]),
        jnp.asarray(TENTH[:, None]),
    )


def unpack_two(buf, staged, spread, take, out_w, hidden_w, proj_w, out_sem):
    spans = ((0, 128, out_w), (128, GROUP, hidden_w), (208, GROUP, proj_w))

    @pl.loop(0, 16)
    def _(g):
        slot = g % 2
        outs = [
            pltpu.make_async_copy(
                staged.at[slot, pl.ds(at, count)], row_block(ref, g, count), out_sem.at[i, slot]
            )
            for i, (at, count, ref) in enumerate(spans)
        ]

        @pl.when(g >= 2)
        def _():
            for out in outs:
                out.wait()

        staged[slot, 0:128] = nn(spread[...], buf[g]).astype(bf16)
        staged[slot, 128:208] = nn(take[1], buf[g]).astype(bf16)
        staged[slot, 208:288] = nn(take[2], buf[g]).astype(bf16)
        for out in outs:
            out.start()

    for slot in range(2):
        for i, (at, count, ref) in enumerate(spans):
            pltpu.make_async_copy(
                staged.at[slot, pl.ds(at, count)], row_block(ref, 0, count), out_sem.at[i, slot]
            ).wait()


class Scatter:
    def __init__(self, parts, away, mine, pair, lands, halves, send, recv, place):
        self.parts = parts
        self.away, self.mine, self.pair = away, mine, pair
        self.lands, self.halves = lands, halves
        self.send, self.recv, self.place = send, recv, place
        self.sibling = device_at(moved(place, "c", 1 - place["c"]))

    def swap(self, number):
        return remote(
            self.away.at[number],
            self.pair.at[number],
            self.send.at[len(self.parts), number],
            self.recv.at[len(self.parts), number],
            self.sibling,
        )

    def add_pair(self, number):
        self.swap(number).wait()
        self.mine[number] = (
            self.mine[number].astype(f32) + self.pair[number].astype(f32)
        ).astype(bf16)

    def own_piece(self, where, cols):
        half = where["z"] * 2 + where["x"] % 2
        return self.mine.at[half, pl.ds((where["y"] * 2 + where["x"] // 2) * ROWS, ROWS), cols]

    def start(self, stage):
        for part, ((first, width), order) in enumerate(self.parts):
            cols = pl.ds(first, width)
            axis = order[2 - stage]
            rest = order[: 2 - stage]

            @pl.loop(0, 16 // 4**stage)
            def _(number, part=part, cols=cols, axis=axis, rest=rest):
                for step in (1, 3, 2):
                    target = moved(self.place, axis, (self.place[axis] + step) % 4)
                    if stage == 0:
                        source = self.own_piece(varied(target, rest, number), cols)
                    elif stage == 1:
                        source = self.halves[0].at[target[axis], number, :, cols]
                    else:
                        source = self.halves[1].at[target[axis], :, cols]
                    remote(
                        source,
                        self.lands[stage].at[step - 1, number, :, cols],
                        self.send.at[part, stage],
                        self.recv.at[part, stage],
                        device_at(target),
                    ).start()

    def add(self, stage, out=None):
        for part, ((first, width), order) in enumerate(self.parts):
            cols = pl.ds(first, width)
            axis = order[2 - stage]
            rest = order[: 2 - stage]
            wait_bytes(self.lands[stage].at[:, :, :, cols], self.recv.at[part, stage])

            @pl.loop(0, 16 // 4**stage)
            def _(number, cols=cols, axis=axis, rest=rest):
                if stage == 0:
                    total = self.own_piece(varied(self.place, rest, number), cols)[...]
                elif stage == 1:
                    total = self.halves[0][self.place[axis], number, :, cols]
                else:
                    total = self.halves[1][self.place[axis], :, cols]
                total = total.astype(f32)
                for source in range(3):
                    total = total + self.lands[stage][source, number, :, cols].astype(f32)
                if stage == 0:
                    self.halves[0][number // 4, number % 4, :, cols] = total.astype(bf16)
                elif stage == 1:
                    self.halves[1][number, :, cols] = total.astype(bf16)
                else:
                    out[:, cols] = total

    def finish(self):
        for stage in range(3):
            for part, ((first, width), order) in enumerate(self.parts):
                wait_bytes(
                    self.lands[stage].at[:, :, :, pl.ds(first, width)], self.send.at[part, stage]
                )


def scatter_scratch(parts):
    return [
        pltpu.VMEM((8, 256, D), bf16),
        pltpu.VMEM((8, 256, D), bf16),
        pltpu.VMEM((8, 256, D), bf16),
        pltpu.VMEM((3, 16, ROWS, D), bf16),
        pltpu.VMEM((3, 4, ROWS, D), bf16),
        pltpu.VMEM((3, 1, ROWS, D), bf16),
        pltpu.VMEM((4, 4, ROWS, D), bf16),
        pltpu.VMEM((4, ROWS, D), bf16),
        pltpu.SemaphoreType.DMA((parts + 1, 8)),
        pltpu.SemaphoreType.DMA((parts + 1, 8)),
    ]


def scatter_of(parts, scratch, place):
    away, mine, pair, l0, l1, l2, h0, h1, send, recv = scratch
    return Scatter(parts, away, mine, pair, (l0, l1, l2), (h0, h1), send, recv, place)


def scatter_kernel(
    normed, d_wide, vector_grads, scale_tile,
    take_t, last_t, lane_of_t, row_of_t, scale_rows, tenth_row, tenth_col,
    out, normed_t, right, vec_tile, *scratch,
):
    place = my_place()
    scatter = scatter_of(PARTS, scratch, place)
    for n in range(D // 128):
        lanes = slice(n * 128, n * 128 + 128)
        normed_t[lanes] = normed[:, lanes].T
    for w in range(3):
        right[w * 128 : w * 128 + 128] = d_wide[:, w * D : (w + 1) * D]
    for cell in range(5):
        right[384:512, cell * LANES : (cell + 1) * LANES] = d_wide[:, 3 * D :]
    by_row = nn(row_of_t[...], vector_grads[...])
    by_row = jnp.where(tenth_col[...] == tenth_row[...], by_row, 0.0).astype(bf16)
    vec_tile[...] = nn(by_row, lane_of_t[...]).astype(bf16)
    greet(ring_peers(place))

    def produce(number, core, into):
        group = number * 2 + core
        rows = pl.ds(pl.multiple_of(group * GROUP, 16), GROUP)
        piece = normed_t[rows]
        lefts = [nn(take_t[w], piece).astype(bf16) for w in range(3)]
        for cell in range(5):
            left = jnp.concatenate(lefts + [nn(last_t[cell], piece).astype(bf16)], axis=1)
            lanes = slice(cell * LANES, (cell + 1) * LANES)
            block = nn(left, right[:, lanes])
            if cell == 0:
                block = block + jnp.concatenate(
                    [jnp.zeros((256, 128), f32), nn(take_t[0], vec_tile[rows])], axis=1
                )
            if cell == 1:
                block = block + jnp.concatenate(
                    [jnp.zeros((256, 128), f32), nn(scale_rows[...], scale_tile[...])], axis=1
                )
            into[number, :, lanes] = block.astype(bf16)

    @pl.loop(0, 8)
    def _(number):
        produce(number, 1 - place["c"], scatter.away)
        scatter.swap(number).start()

    @pl.loop(0, 8)
    def _(number):
        produce(number, place["c"], scatter.mine)
        scatter.add_pair(number)

    for stage in range(3):
        scatter.start(stage)
        scatter.add(stage, out)
    scatter.finish()


def scatter_grads(*operands):
    return pl.pallas_call(
        scatter_kernel,
        out_shape=jax.ShapeDtypeStruct((ROWS, D), f32),
        in_specs=[VMEM] * 11,
        out_specs=VMEM,
        scratch_shapes=[
            pltpu.VMEM((D, 128), bf16),
            pltpu.VMEM((512, D), bf16),
            pltpu.VMEM((D, 128), bf16),
        ]
        + scatter_scratch(3),
        compiler_params=pltpu.CompilerParams(
            collective_id=3, has_side_effects=True, vmem_limit_bytes=48 * 2**20
        ),
        name="scatter_grads",
    )(
        *operands,
        jnp.asarray(TAKE.transpose(0, 2, 1), bf16),
        jnp.asarray(LAST.transpose(0, 2, 1), bf16),
        jnp.asarray(LANE_OF.T, bf16),
        jnp.asarray(ROW_OF.T, bf16),
        jnp.asarray(SCALE_ROWS, bf16),
        jnp.asarray(TENTH[None, :]),
        jnp.asarray(TENTH[:, None]),
    )


def quarter_of(blk):
    inner = blk % 4
    return jnp.where((blk // 4) % 2 == 0, inner, 3 - inner)


def query_block(quarter, j):
    return j * 4 + jnp.where(j % 2 == 0, quarter, 3 - quarter)


def chip_block(x_low, n):
    z = n // 2
    return z * 4 + 2 * ((z + x_low) % 2) + n % 2


def cell_of(ref, pair, width):
    return ref.at[pl.ds(pair // H * TOK, TOK), pl.ds(pair % H * width, width)]


def mask_of(key_block, block, start):
    key_at = key_block * B + lax.broadcasted_iota(jnp.int32, (B, B), 0)
    query_at = block * B + lax.broadcasted_iota(jnp.int32, (B, B), 1)
    return (key_at >= start) & (key_at <= query_at)


def has_mask(key_block, block):
    return (key_block == 0) | (key_block == block) | (block == 15)


def shift_matrix(rows, cols, by):
    row = lax.broadcasted_iota(jnp.int32, (rows, cols), 0)
    col = lax.broadcasted_iota(jnp.int32, (rows, cols), 1)
    return jnp.where((row - col == by) & (jnp.minimum(row, col) < HD), 1.0, 0.0).astype(bf16)


def wait_cells(ref, sem, fewer, width):
    wait_bytes(ref.at[:, pl.ds(0, 15 * width)], sem)
    wait_bytes(cell_of(ref, 0, width), sem)

    @pl.when(jnp.logical_not(fewer))
    def _():
        wait_bytes(cell_of(ref, 0, width), sem)


def forward_kernel(
    pack, starts, pack_two, spread, take,
    kv_out, queries, out_t, log_norms, attended, out_w, hidden_w, proj_w,
    kv, value_t, tops, totals, rounded, landed, buf, staged,
    two_send, two_recv, send, recv, core_send, core_recv, x_send, x_recv,
    pass_send, pass_recv, back_send, back_recv, kv_sem, own_sem, out_sem,
):
    blk = lax.axis_index("blk")
    head = lax.axis_index("head")
    core = blk % 2
    x_low = (blk // 2) % 2
    quarter = blk % 4
    pair = (blk // 4) * 8 + head
    to_quarter = quarter_of(blk)
    even = (blk // 4) % 2 == 0
    place = my_place()
    two = Gather(PARTS_TWO, buf, two_send, two_recv, place)
    own = two.begin(pack_two, own_sem)
    greet_all()

    @pl.loop(0, PAIRS)
    def _(k):
        p = (pair + k) % PAIRS
        src = cell_of(pack, p, LANES)
        dst = kv.at[blk, pl.ds(head * TOK, TOK)]
        mine = (k == 0) & even

        @pl.when(mine)
        def _():
            pltpu.make_async_copy(src, dst, recv).start()

        @pl.when(jnp.logical_not(mine))
        def _():
            remote(src, dst, send, recv, ((p // 8) * 4 + to_quarter, p % 8)).start()

    own.wait()
    two.stage(0)
    sibling = (blk + 1 - 2 * core, head)
    partner = (blk + 2 - 4 * x_low, head)
    wait_bytes(kv.at[pl.ds(0, 4)], recv)

    @pl.loop(0, 4)
    def _(j):
        block = kv.at[query_block(quarter, j)]
        remote(block, block, core_send, core_recv, sibling).start()
        remote(block, block, x_send, x_recv, partner).start()

    two.stage(1)
    pick = shift_matrix(LANES, 128, HD)

    @pl.loop(0, 4)
    def _(j):
        queries[j] = nn(kv[query_block(quarter, j)], pick).astype(bf16)
        tops[j] = jnp.full((1, B), NEGATIVE, f32)
        totals[j] = jnp.zeros((1, B), f32)
        out_t[j] = jnp.zeros((128, B), f32)

    wait_bytes(kv.at[pl.ds(0, 4)], core_recv)

    @pl.loop(0, 8)
    def _(n):
        b = chip_block(x_low, n)
        value_t[b] = kv[b, :, 128:].T

    two.stage(2)

    def step(j, block, key_block):
        def tile(masked):
            s = nt(kv[key_block, :, :128], queries[j])
            if masked:
                s = jnp.where(mask_of(key_block, block, starts[j]), s, NEGATIVE)
            top = tops[j]
            new_top = jnp.maximum(top, jnp.max(s, axis=0, keepdims=True))
            p = jnp.exp(s - new_top)
            scale = jnp.exp(top - new_top)
            tops[j] = new_top
            totals[j] = totals[j] * scale + jnp.sum(p, axis=0, keepdims=True)
            out_t[j] = out_t[j] * scale + nn(value_t[key_block], p.astype(bf16))

        masked = has_mask(key_block, block)
        pl.when(masked)(lambda: tile(True))
        pl.when(jnp.logical_not(masked))(lambda: tile(False))

    @pl.loop(0, 4)
    def _(j):
        block = query_block(quarter, j)

        @pl.loop(0, 2 * j + block % 2 + 1)
        def _(n):
            step(j, block, chip_block(x_low, n))

    wait_bytes(kv.at[pl.ds(0, 4)], x_recv)

    @pl.loop(0, 4)
    def _(j):
        block = kv.at[query_block((quarter + 2) % 4, j)]
        remote(block, block, pass_send, pass_recv, sibling).start()

    wait_bytes(kv.at[pl.ds(0, 4)], pass_recv)
    keep = pltpu.make_async_copy(kv, kv_out, kv_sem)
    keep.start()

    @pl.loop(0, 8)
    def _(n):
        b = chip_block(1 - x_low, n)
        value_t[b] = kv[b, :, 128:].T

    @pl.loop(0, 4)
    def _(i):
        j = 3 - i
        block = query_block(quarter, j)

        @pl.loop(0, 2 * j + 2 * ((j + x_low) % 2))
        def _(n):
            step(j, block, chip_block(1 - x_low, n))

        acc = out_t[j]
        result = acc / acc[112:113]
        out_t[j] = result
        log_norms[j] = tops[j] + jnp.log(totals[j])
        rounded[j] = result.T.astype(bf16)

        @pl.loop(0, 8)
        def _(k):
            h = (head + k) % 8
            src = rounded.at[j, pl.ds(h * TOK, TOK)]
            dst = cell_of(landed, pair, 128)
            mine = (k == 0) & (block == blk)

            @pl.when(mine)
            def _():
                pltpu.make_async_copy(src, dst, back_recv).start()

            @pl.when(jnp.logical_not(mine))
            def _():
                remote(src, dst, back_send, back_recv, (block, h)).start()

    two.finish()
    unpack_two(buf, staged, spread, take, out_w, hidden_w, proj_w, out_sem)
    wait_bytes(landed, back_recv)
    attended[...] = landed[...]
    keep.wait()
    for sem in (core_send, x_send, pass_send):
        wait_bytes(kv.at[pl.ds(0, 4)], sem)
    wait_cells(pack, send, even, LANES)
    wait_cells(landed, back_send, even, 128)


def attend(pack, starts, pack_two):
    return pl.pallas_call(
        forward_kernel,
        out_shape=(
            jax.ShapeDtypeStruct((16, B, LANES), bf16),
            jax.ShapeDtypeStruct((4, B, 128), bf16),
            jax.ShapeDtypeStruct((4, 128, B), f32),
            jax.ShapeDtypeStruct((4, 1, B), f32),
            jax.ShapeDtypeStruct((2 * TOK, OUT_WIDE), bf16),
            jax.ShapeDtypeStruct((OUT_WIDE, D), bf16),
            jax.ShapeDtypeStruct((D, D), bf16),
            jax.ShapeDtypeStruct((D, D), bf16),
        ),
        in_specs=[VMEM] * 5,
        out_specs=(HBM, VMEM, VMEM, VMEM, VMEM, HBM, HBM, HBM),
        scratch_shapes=[
            pltpu.VMEM((16, B, LANES), bf16),
            pltpu.VMEM((16, 128, B), bf16),
            pltpu.VMEM((4, 1, B), f32),
            pltpu.VMEM((4, 1, B), f32),
            pltpu.VMEM((4, B, 128), bf16),
            pltpu.VMEM((2 * TOK, OUT_WIDE), bf16),
            pltpu.VMEM((16, 256, D), bf16),
            pltpu.VMEM((2, 288, D), bf16),
        ]
        + gather_semaphores(2)
        + [pltpu.SemaphoreType.DMA] * 12
        + [pltpu.SemaphoreType.DMA((3, 2))],
        compiler_params=pltpu.CompilerParams(
            collective_id=1, has_side_effects=True, vmem_limit_bytes=48 * 2**20
        ),
        name="attend",
    )(pack, starts, pack_two, jnp.asarray(SPREAD, bf16), jnp.asarray(TAKE, bf16))


def backward_kernel(
    pack, kv, queries, starts, out_t, log_norms,
    attended, d_branch, normed_two, d_pre, activated, upstream, take_t,
    wide_out, two_out,
    d_out, key_t, deltas, d_query, d_kv, mine_kv, half, half_in, cross, cross_in, final, landed,
    attended_t, normed_two_t, activated_t, right,
    send, recv, core_send, core_recv, x_send, x_recv, back_send, back_recv,
    *scratch,
):
    blk = lax.axis_index("blk")
    head = lax.axis_index("head")
    core = blk % 2
    x_low = (blk // 2) % 2
    quarter = blk % 4
    pair = (blk // 4) * 8 + head
    to_quarter = quarter_of(blk)
    even = (blk // 4) % 2 == 0
    place = my_place()
    two = scatter_of(PARTS_TWO, scratch, place)
    greet_all()

    @pl.loop(0, PAIRS)
    def _(k):
        p = (pair + k) % PAIRS
        src = cell_of(pack, p, 128)
        dst = d_out.at[blk // 4, pl.ds(head * TOK, TOK)]
        mine = (k == 0) & even

        @pl.when(mine)
        def _():
            pltpu.make_async_copy(src, dst, recv).start()

        @pl.when(jnp.logical_not(mine))
        def _():
            remote(src, dst, send, recv, ((p // 8) * 4 + to_quarter, p % 8)).start()

    for n in range(D // 128):
        lanes = slice(n * 128, n * 128 + 128)
        normed_two_t[lanes] = normed_two[:, lanes].T
        activated_t[lanes] = activated[:, lanes].T
    for n in range(H):
        lanes = slice(n * 128, n * 128 + 128)
        attended_t[lanes] = attended[:, lanes].T
    right[0:128] = d_branch[...]
    right[128:256] = d_pre[...]
    right[256:384] = upstream[...]

    def produce(number, of_core, into):
        group = number * 2 + of_core
        rows = pl.ds(pl.multiple_of(group * GROUP, 16), GROUP)
        out_rows = pl.ds(pl.multiple_of(group * 128 + 32, 16), GROUP)
        left = jnp.concatenate(
            [
                nn(take_t[0], attended_t[out_rows]).astype(bf16),
                nn(take_t[1], normed_two_t[rows]).astype(bf16),
                nn(take_t[2], activated_t[rows]).astype(bf16),
            ],
            axis=1,
        )
        for cell in range(5):
            lanes = slice(cell * LANES, (cell + 1) * LANES)
            into[number, :, lanes] = nn(left, right[:, lanes]).astype(bf16)

    @pl.loop(0, 8)
    def _(number):
        produce(number, 1 - core, two.away)
        two.swap(number).start()

    @pl.loop(0, 8)
    def _(number):
        produce(number, core, two.mine)

    @pl.loop(0, 16)
    def _(b):
        key_t[b] = kv[b, :, :128].T

    @pl.loop(0, 8)
    def _(number):
        two.add_pair(number)

    two.start(0)
    wait_bytes(d_out, recv)

    @pl.loop(0, 4)
    def _(j):
        deltas[j] = jnp.sum(d_out[j].astype(f32).T * out_t[j], axis=0, keepdims=True)
        d_query[j] = jnp.zeros((128, B), f32)

    sibling = (blk + 1 - 2 * core, head)
    partner = (blk + 2 - 4 * x_low, head)

    def step(j, block, key_block):
        def tile(masked):
            q = queries[j]
            do = d_out[j]
            p = jnp.exp(nt(kv[key_block, :, :128], q) - log_norms[j])
            if masked:
                p = jnp.where(mask_of(key_block, block, starts[j]), p, 0.0)
            dp = nt(kv[key_block, :, 128:], do)
            ds = (p * (dp - deltas[j])).astype(bf16)
            d_kv[:, :128] += nn(ds, q)
            d_kv[:, 128:] += nn(p.astype(bf16), do)
            d_query[j] += nn(key_t[key_block], ds)

        masked = has_mask(key_block, block)
        pl.when(masked)(lambda: tile(True))
        pl.when(jnp.logical_not(masked))(lambda: tile(False))

    def swap(n):
        return remote(
            half.at[n], half_in.at[n], core_send.at[n], core_recv.at[n], sibling
        )

    def cross_swap(z):
        return remote(cross.at[z], cross_in.at[z], x_send.at[z], x_recv.at[z], partner)

    def own_number(z):
        return 2 * z + (x_low + z) % 2

    def core_sum(z):
        own = own_number(z)
        other = 4 * z + 1 - own
        swap(other).wait()
        cross[z] = (mine_kv[other] + half_in[other].astype(f32)).astype(bf16)
        cross_swap(z).start()
        swap(own).wait()
        mine_kv[own] = mine_kv[own] + half_in[own].astype(f32)

    shift = shift_matrix(128, LANES, -HD)

    def finish(z):
        block = query_block(quarter, z)
        cross_swap(z).wait()
        final[z] = (
            mine_kv[own_number(z)]
            + cross_in[z].astype(f32)
            + nn(d_query[z].T.astype(bf16), shift)
        ).astype(bf16)

        @pl.loop(0, 8)
        def _(k):
            h = (head + k) % 8
            src = final.at[z, pl.ds(h * TOK, TOK)]
            dst = cell_of(landed, pair, LANES)
            mine = (k == 0) & (block == blk)

            @pl.when(mine)
            def _():
                pltpu.make_async_copy(src, dst, back_recv).start()

            @pl.when(jnp.logical_not(mine))
            def _():
                remote(src, dst, back_send, back_recv, (block, h)).start()

    @pl.loop(0, 8)
    def _(part):
        z = part // 2

        @pl.loop(2 * part, 2 * part + 2)
        def _(key_block):
            d_kv[...] = jnp.zeros((B, LANES), f32)
            first = z + (query_block(quarter, z) < key_block).astype(jnp.int32)

            @pl.loop(first, 4)
            def _(j):
                step(j, query_block(quarter, j), key_block)

            n = 2 * z + (key_block % 4) // 2

            @pl.when((key_block + z + core) % 2 == 0)
            def _():
                mine_kv[n] = d_kv[...]

            @pl.when((key_block + z + core) % 2 == 1)
            def _():
                half[n] = d_kv[...].astype(bf16)
                swap(n).start()

        @pl.when((part % 2 == 0) & (part > 0))
        def _():
            core_sum(z - 1)

        @pl.when((part % 2 == 1) & (part > 1))
        def _():
            finish(z - 1)

        @pl.when(part == 4)
        def _():
            two.add(0)
            two.start(1)

        @pl.when(part == 6)
        def _():
            two.add(1)
            two.start(2)

    core_sum(3)
    two.add(2, two_out)
    finish(3)
    two.finish()
    wait_bytes(landed, back_recv)
    wide_out[...] = landed[...]
    wait_cells(pack, send, even, 128)
    wait_cells(landed, back_send, even, LANES)


def attend_back(*operands):
    return pl.pallas_call(
        backward_kernel,
        out_shape=(
            jax.ShapeDtypeStruct((2 * TOK, WIDE), bf16),
            jax.ShapeDtypeStruct((ROWS, D), f32),
        ),
        in_specs=[VMEM] * 13,
        out_specs=(VMEM, VMEM),
        scratch_shapes=[
            pltpu.VMEM((4, B, 128), bf16),
            pltpu.VMEM((16, 128, B), bf16),
            pltpu.VMEM((4, 1, B), f32),
            pltpu.VMEM((4, 128, B), f32),
            pltpu.VMEM((B, LANES), f32),
            pltpu.VMEM((8, B, LANES), f32),
            pltpu.VMEM((8, B, LANES), bf16),
            pltpu.VMEM((8, B, LANES), bf16),
            pltpu.VMEM((4, B, LANES), bf16),
            pltpu.VMEM((4, B, LANES), bf16),
            pltpu.VMEM((4, B, LANES), bf16),
            pltpu.VMEM((2 * TOK, WIDE), bf16),
            pltpu.VMEM((OUT_WIDE, 128), bf16),
            pltpu.VMEM((D, 128), bf16),
            pltpu.VMEM((D, 128), bf16),
            pltpu.VMEM((384, D), bf16),
            pltpu.SemaphoreType.DMA,
            pltpu.SemaphoreType.DMA,
            pltpu.SemaphoreType.DMA((8,)),
            pltpu.SemaphoreType.DMA((8,)),
            pltpu.SemaphoreType.DMA((4,)),
            pltpu.SemaphoreType.DMA((4,)),
            pltpu.SemaphoreType.DMA,
            pltpu.SemaphoreType.DMA,
        ]
        + scatter_scratch(2),
        compiler_params=pltpu.CompilerParams(
            collective_id=2, has_side_effects=True, vmem_limit_bytes=60 * 2**20
        ),
        name="attend_back",
    )(*operands, jnp.asarray(TAKE.transpose(0, 2, 1), bf16))


def on_device(
    inputs,
    segment_ids,
    norm1_gain,
    w_query,
    w_key,
    w_value,
    query_bias,
    value_bias,
    w_out,
    out_bias,
    norm2_gain,
    w_hidden,
    hidden_bias,
    w_proj,
    proj_bias,
    dim_scale,
    cotangent,
):
    blk = lax.axis_index("blk")
    vectors = jnp.stack(
        [norm1_gain, query_bias, value_bias, out_bias, norm2_gain, hidden_bias, proj_bias]
    )
    spare = jnp.pad(vectors[:, None], ((0, 3), (0, H - 1), (0, 6)))
    rows = jnp.concatenate(
        [w.reshape(10, H, HD) for w in (w_key, w_query, w_value)] + [spare], axis=2
    )
    pack_one = jnp.concatenate(
        [rows[:, w * 5 : w * 5 + 5].reshape(10, D) for w in range(3)]
        + [rows[:, 15].reshape(2, D)],
        axis=0,
    )
    pack_two = jnp.concatenate([w_out, w_hidden, w_proj, jnp.zeros((2, D), bf16)], axis=0)
    wide_w, every = gather_weights(pack_one)
    gain_one, query_b, value_b, out_b, gain_two, hidden_b, proj_b = [every[i] for i in range(7)]

    micro = blk // 8
    segment_row = lax.dynamic_index_in_dim(segment_ids, micro, 0, keepdims=False)
    starts = jnp.zeros_like(segment_row)
    for value in range(1, 9):
        before = jnp.sum((segment_row < value).astype(jnp.int32))
        starts = jnp.where(segment_row == value, before, starts)
    quarter = blk % 4
    starts = starts.reshape(16, 1, B)
    starts = jnp.stack([starts[query_block(quarter, j)] for j in range(4)])

    def lanes_of(key, query, value, spare_lanes):
        parts = [jnp.broadcast_to(part.reshape(-1, HD), (H, HD)) for part in (key, query, value)]
        return jnp.concatenate(parts + [jnp.broadcast_to(spare_lanes, (H, 16))], 1).reshape(WIDE)

    tokens = inputs.reshape(2 * TOK, D).astype(f32)
    inverse_one = inverse_rms(tokens)
    normed = (tokens * inverse_one * gain_one).astype(bf16)
    softplus_scale = LOG2E / math.sqrt(HD) * jax.nn.softplus(dim_scale)
    ones = jnp.ones((HD,), f32)
    zeros = jnp.zeros((HD,), f32)
    none = jnp.zeros((16,), f32)
    wide_bias = lanes_of(zeros, query_b, value_b, none)
    wide_scale = lanes_of(ones, softplus_scale, ones, none)
    wide_one = lanes_of(zeros, zeros, zeros, none.at[0].set(1.0))
    wide_full = nn(normed, wide_w) + wide_bias
    packed = (wide_full * wide_scale + wide_one).astype(bf16)
    kv, queries, out_t, log_norms, attended, out_w, hidden_w, proj_w = attend(
        packed, starts, pack_two
    )

    residual = tokens + nn(attended, out_w) + out_b
    inverse_two = inverse_rms(residual)
    normed_two = (residual * inverse_two * gain_two).astype(bf16)
    pre_act = nn(normed_two, hidden_w) + hidden_b
    gate = jax.nn.sigmoid(pre_act)
    activated = (pre_act * gate).astype(bf16)
    layer_out = (residual + nn(activated, proj_w) + proj_b).astype(bf16)

    upstream_low = cotangent.reshape(2 * TOK, D)
    upstream = upstream_low.astype(f32)
    d_pre = (nt(upstream_low, proj_w) * gate * (1.0 + pre_act * (1.0 - gate))).astype(bf16)
    d_normed_two = nt(d_pre, hidden_w)
    d_residual = upstream + norm_back(d_normed_two * gain_two, residual, inverse_two)
    d_branch = d_residual.astype(bf16)
    d_attended = nt(d_branch, out_w).astype(bf16)
    d_scaled, two = attend_back(
        d_attended, kv, queries, starts, out_t, log_norms,
        attended, d_branch, normed_two, d_pre, activated, upstream_low,
    )
    d_scaled = d_scaled.astype(f32)
    query_lanes = lanes_of(zeros, ones, zeros, none)
    scale_terms = jnp.sum(d_scaled * wide_full, axis=0) * query_lanes
    scale_terms = jnp.sum(scale_terms.reshape(H, LANES), axis=0)[HD : 2 * HD]
    d_wide = (d_scaled * wide_scale).astype(bf16)
    d_normed = nt(d_wide, wide_w)
    input_grad = (
        d_residual + norm_back(d_normed * gain_one, tokens, inverse_one)
    ).astype(bf16)

    def total(values):
        return jnp.sum(values.astype(f32), axis=0)

    d_bias = total(d_wide).reshape(H, LANES)
    vector_grads = jnp.stack(
        [
            total(d_normed * tokens * inverse_one),
            d_bias[:, HD : 2 * HD].reshape(D),
            d_bias[:, 2 * HD : 3 * HD].reshape(D),
            total(d_branch),
            total(d_normed_two * residual * inverse_two),
            total(d_pre),
            total(upstream),
        ]
    )
    vector_grads = jnp.pad(vector_grads, ((0, 9), (0, 0))).astype(bf16)
    scale_tile = jnp.pad(scale_terms.reshape(8, 10), ((0, 8), (112, 6))).astype(bf16)
    one = scatter_grads(normed, d_wide, vector_grads, scale_tile)
    rows = jnp.concatenate(
        [one[w * 10 : w * 10 + 10].reshape(10, 5, LANES) for w in range(3)]
        + [one[30:32].reshape(10, 1, LANES)],
        axis=1,
    )
    d_key_w, d_query_w, d_value_w = [
        rows[:, :, i * HD : (i + 1) * HD].reshape(10, D) for i in range(3)
    ]
    vector = [one[i, 240:250] for i in range(7)]
    scale_grad = one[0:8, 496:506].reshape(HD)
    scale_grad = scale_grad * (LOG2E / math.sqrt(HD)) * jax.nn.sigmoid(dim_scale)
    return (
        layer_out.reshape(2, TOK, D),
        input_grad.reshape(2, TOK, D),
        vector[0],
        d_query_w,
        d_key_w,
        d_value_w,
        vector[1],
        vector[2],
        two[0:10],
        vector[3],
        vector[4],
        two[10:20],
        vector[5],
        two[20:30],
        vector[6],
        scale_grad,
    )


def solution(mesh):
    rows = P(("blk", "head"), None)
    vec = P(("blk", "head"))
    tok = P(None, ("blk", "head"), None)
    in_specs = (
        tok, P(), vec, rows, rows, rows, vec, vec, rows, vec, vec, rows, vec, rows, vec, P(), tok
    )
    out_specs = (
        tok, tok, vec, rows, rows, rows, vec, vec, rows, vec, vec, rows, vec, rows, vec, P()
    )
    return jax.shard_map(
        on_device, mesh=mesh, in_specs=in_specs, out_specs=out_specs, check_vma=False
    )
```

profile of v0, /device:TPU:97, one launch (start us, length us, event | category | flops | bytes accessed | tf_op | source)
XLA Modules:
  0.0 377.8 jit_solution(4379458764751918671)
XLA Ops:
  0.7 1.9 fusion.25
  2.6 6.2 %compare_select_fusion.7 = s32[1,8192]{1,0:T(1,128)S(1)} fusion(s32[]{:T(128)} %get-tuple-element.64, s32[]{:T(128)} %get-tuple-element.66, s32[]{:T(128)} %get-tuple-element.68, s32[]{:T(128)} %get-tuple-element.70, s32[]{:T(128)} %get-tuple-element.67, s32[]{:T(128)} %get-tuple-element.65, s32[]{:T(128)} %get-tuple-element.69, s32[]{:T(128)} %get-tuple-element.63, ...), kind=kLoop, calls=%fused_computation.58 | loop fusion | flops 131072 | bytes 65572 | tf_op jit(solution)/shard_map/jit(_where)/select_n | solution.py:1060
  8.9 0.9 reshape.318
  9.8 0.9 reshape.319
  10.7 0.9 reshape.320
  11.6 0.8 stack.58
  12.4 0.1 fusion.19
  12.8 1.1 copy-done.1
  13.9 0.9 copy-done.7
  14.8 1.0 copy-done.12
  15.8 0.9 copy-done.13
  16.7 0.8 copy-done.17
  17.5 0.7 copy-done.18
  18.2 58.5 %gather_weights.1 = (bf16[1280,4096]{1,0:T(8,128)(2,1)S(1)}, f32[16,1280]{1,0:T(8,128)S(1)}) custom-call(bf16[32,1280]{1,0:T(8,128)(2,1)S(1)} %pad_maximum_fusion.1.pack, bf16[3,80,256]{2,1,0:T(8,128)(2,1)S(1)} %copy-done.7, bf16[5,80,256]{2,1,0:T(8,128)(2,1)S(1)} %copy-done.13, bf16[128,1280]{1,0:T(8,128)(2,1)S(1)} %copy-done.12, ...), custom_call_target="tpu_custom_call" | custom-call | tf_op jit(solution)/shard_map/gather_weights/pallas_call | solution.py:294
  76.7 4.0 %copy-done = bf16[1280,4096]{1,0:T(8,128)(2,1)} copy-done((bf16[1280,4096]{1,0:T(8,128)(2,1)}, bf16[1280,4096]{1,0:T(8,128)(2,1)S(1)}, u32[]{:S(2)}) %copy-start) | copy-done | bytes 10485784
  80.7 0.1 slice_reduce_fusion
  81.2 0.1 maximum_bitcast_fusion.2
  81.3 0.1 fusion.8
  81.5 0.1 rsqrt.26
  81.6 0.2 fusion.10.normed
  81.8 6.0 %add_convert_fusion = (bf16[128,4096]{1,0:T(8,128)(2,1)S(1)}, f32[128,4096]{1,0:T(8,128)S(1)}) fusion(f32[4096]{0:T(1024)S(1)} %bitcast.112, f32[4096]{0:T(1024)S(1)} %bitcast.109, f32[4096]{0:T(1024)S(1)} %bitcast.111, bf16[128,1280]{1,0:T(8,128)(2,1)S(1)} %fusion.10.normed, bf16[1280,4096]{1,0:T(8,128)(2,1)} %copy-done), kind=kOutput, calls=%fused_computation.16 | convolution fusion | flops 1344274432 | bytes 14008320 | tf_op jit(solution)/shard_map/dot_general | solution.py:46
  88.0 90.2 %attend.1 = (bf16[16,512,256]{2,1,0:T(8,128)(2,1)}, bf16[4,512,128]{2,1,0:T(8,128)(2,1)S(1)}, f32[4,128,512]{2,1,0:T(8,128)S(1)}, f32[4,1,512]{2,1,0:T(1,128)S(1...) custom-call(bf16[128,4096]{1,0:T(8,128)(2,1)S(1)} %get-tuple-element, ...), custom_call_target="tpu_custom_call" | custom-call | tf_op jit(solution)/shard_map/attend/pallas_call | solution.py:736
  178.2 4.2 %multiply_reduce_fusion.2 = (f32[128]{0:T(128)S(1)}, f32[128,1280]{1,0:T(8,128)S(1)}) fusion(f32[1280]{0:T(1024)S(1)} %get-tuple-element.59, bf16[128,2048]{1,0:T(8,128)(2,1)S(1)} %get-tuple-element.42.attended, bf16[2048,1280]{1,0:T(8,128)(2,1)} %get-tuple-element.43, bf16[128,1280]{1,0:T(8,128)(2,1)S(1)} %bitcast.98), kind=kOutput, calls=%fused_computation.38 | convolution fusion | flops 671907712 | bytes 6755840 | tf_op jit(solution)/shard_map/dot_general | solution.py:46
  182.5 0.1 multiply_convert_fusion.1.normed_two
  182.7 1.4 multiply_convert_fusion
  184.1 0.8 copy-done.26
  184.9 1.3 fusion.37
  186.2 1.3 multiply_reduce_fusion
  187.5 1.1 fusion.29
  188.6 2.6 convolution_convert_fusion.pack
  191.3 106.6 %attend_back.1 = (bf16[128,4096]{1,0:T(8,128)(2,1)}, f32[32,1280]{1,0:T(8,128)}) custom-call(bf16[128,2048]{1,0:T(8,128)(2,1)} %convolution_convert_fusion.pack, bf16[16,512,256]{2,1,0:T(8,128)(2,1)} %get-tuple-element.46.kv, bf16[4,512,128]{2,1,0:T(8,128)(2,1)} %copy-done.6, s32[4,1,512]{2,1,0:T(1,128)} %copy-done.14, f32[4,128,512]{2,1,0:T(8,128)} %copy-done.4, ...), custom_call_target="tpu_custom_call" | custom-call | tf_op jit(solution)/shard_map/attend_back/pallas_call | solution.py:977
  297.9 1.6 fusion.7
  299.7 0.1 reshape.328
  299.8 0.3 fusion.30
  300.2 8.6 %fusion.17 = (bf16[1280]{0:T(1024)(128)(2,1)S(1)}, f32[128]{0:T(128)S(1)}, f32[128,1280]{1,0:T(8,128)}) fusion(bf16[2,64,1280]{2,1,0:T(8,128)(2,1)} %param.35, f32[128]{0:T(128)S(1)} %rsqrt.26, f32[1280]{0:T(1024)S(1)} %get-tuple-element.62, bf16[128,4096]{1,0:T(8,128)(2,1)S(1)} %get-tuple-element.75.d_wide, bf16[1280,4096]{1,0:T(8,128)(2,1)} %copy-done), kind=kOutput, calls=%fused_computation.31 | convolution fusion | flops 1343322752 | bytes 12526080 | tf_op jit(solution)/shard_map/dot_general | solution.py:50
  308.9 0.1 stack_reshape.8
  309.0 0.1 stack_reshape.9
  309.1 1.0 reduce.14
  310.3 57.2 %scatter_grads.1 = f32[32,1280]{1,0:T(8,128)S(1)} custom-call(bf16[128,1280]{1,0:T(8,128)(2,1)S(1)} %fusion.10.normed, bf16[128,4096]{1,0:T(8,128)(2,1)S(1)} %get-tuple-element.75.d_wide, bf16[16,1280]{1,0:T(8,128)(2,1)S(1)} %pad.17.vector_grads, bf16[16,128]{1,0:T(8,128)(2,1)S(1)} %pad.18.scale_tile, bf16[3,256,80]{2,1,0:T(8,128)(2,1)S(1)} %copy-done.5, ...), custom_call_target="tpu_custom_call" | custom-call | tf_op jit(solution)/shard_map/scatter_grads/pallas_call | solution.py:517
  367.8 0.1 fusion.33
  367.9 0.7 reshape.333
  368.7 0.7 reshape.334
  369.4 0.7 reshape.335
  370.3 0.5 divide_multiply_fusion
  370.8 0.6 slice_bitcast_fusion
  371.4 2.4 fusion.14
  373.8 0.7 fusion.32
  374.5 3.3 fusion.5
  (137 shorter events, 1.8 us)
Async XLA Ops:
  0.6 80.5 %copy-start.37 = (f32[16]{0:T(128)S(1)}, f32[16]{0:T(128)}, u32[]{:S(2)}) copy-start(f32[16]{0:T(128)} %constant.130.clone.1) | copy-start | bytes 196
  0.7 80.3 %copy-start.38 = (f32[80]{0:T(128)S(1)}, f32[80]{0:T(128)}, u32[]{:S(2)}) copy-start(f32[80]{0:T(128)} %param.50) | copy-start | bytes 964
  0.7 80.7 %copy-start.23 = (bf16[2,64,1280]{2,1,0:T(8,128)(2,1)S(1)}, bf16[2,64,1280]{2,1,0:T(8,128)(2,1)}, u32[]{:S(2)}) copy-start(bf16[2,64,1280]{2,1,0:T(8,128)(2,1)} %param.35) | copy-start | bytes 983044
  8.8 79.1 %copy-start.14 = (s32[4,1,512]{2,1,0:T(1,128)}, s32[4,1,512]{2,1,0:T(1,128)S(1)}, u32[]{:S(2)}) copy-start(s32[4,1,512]{2,1,0:T(1,128)S(1)} %pad_add_fusion.starts) | copy-start | bytes 24580
  12.8 1.1 copy-start.1
  13.9 0.9 copy-start.7
  14.8 1.0 copy-start.12
  15.8 0.9 copy-start.13
  16.7 0.8 copy-start.17
  17.5 0.7 copy-start.18
  76.7 4.0 %copy-start = (bf16[1280,4096]{1,0:T(8,128)(2,1)}, bf16[1280,4096]{1,0:T(8,128)(2,1)S(1)}, u32[]{:S(2)}) copy-start(bf16[1280,4096]{1,0:T(8,128)(2,1)S(1)} %get-tuple-element.41) | copy-start | bytes 31457284
  81.7 6.1 %copy-start.33 = (bf16[10,1280]{1,0:T(8,128)(2,1)S(1)}, bf16[10,1280]{1,0:T(8,128)(2,1)}, u32[]{:S(2)}) copy-start(bf16[10,1280]{1,0:T(8,128)(2,1)} %param.48) | copy-start | bytes 76804
  81.7 6.1 %copy-start.34 = (bf16[10,1280]{1,0:T(8,128)(2,1)S(1)}, bf16[10,1280]{1,0:T(8,128)(2,1)}, u32[]{:S(2)}) copy-start(bf16[10,1280]{1,0:T(8,128)(2,1)} %param.46) | copy-start | bytes 76804
  81.8 6.1 %copy-start.35 = (bf16[10,1280]{1,0:T(8,128)(2,1)S(1)}, bf16[10,1280]{1,0:T(8,128)(2,1)}, u32[]{:S(2)}) copy-start(bf16[10,1280]{1,0:T(8,128)(2,1)} %param.43) | copy-start | bytes 76804
  81.8 6.2 %copy-start.8 = (bf16[3,80,256]{2,1,0:T(8,128)(2,1)S(1)}, bf16[3,80,256]{2,1,0:T(8,128)(2,1)}, u32[]{:S(2)}) copy-start(bf16[3,80,256]{2,1,0:T(8,128)(2,1)} %constant.149.clone.take) | copy-start | bytes 368644
  81.8 6.2 %copy-start.16 = (bf16[128,256]{1,0:T(8,128)(2,1)S(1)}, bf16[128,256]{1,0:T(8,128)(2,1)}, u32[]{:S(2)}) copy-start(bf16[128,256]{1,0:T(8,128)(2,1)} %constant.155.clone.spread) | copy-start | bytes 196612
  178.2 4.3 %copy-start.3 = (bf16[128,2048]{1,0:T(8,128)(2,1)}, bf16[128,2048]{1,0:T(8,128)(2,1)S(1)}, u32[]{:S(2)}) copy-start(bf16[128,2048]{1,0:T(8,128)(2,1)S(1)} %get-tuple-element.42.attended) | copy-start | bytes 1572868
  178.2 4.3 %copy-start.4 = (f32[4,128,512]{2,1,0:T(8,128)}, f32[4,128,512]{2,1,0:T(8,128)S(1)}, u32[]{:S(2)}) copy-start(f32[4,128,512]{2,1,0:T(8,128)S(1)} %get-tuple-element.48.out_t) | copy-start | bytes 3145732
  178.2 4.3 %copy-start.6 = (bf16[4,512,128]{2,1,0:T(8,128)(2,1)}, bf16[4,512,128]{2,1,0:T(8,128)(2,1)S(1)}, u32[]{:S(2)}) copy-start(bf16[4,512,128]{2,1,0:T(8,128)(2,1)S(1)} %get-tuple-element.47.queries) | copy-start | bytes 1572868
  178.2 4.3 %copy-start.20 = (f32[4,1,512]{2,1,0:T(1,128)}, f32[4,1,512]{2,1,0:T(1,128)S(1)}, u32[]{:S(2)}) copy-start(f32[4,1,512]{2,1,0:T(1,128)S(1)} %get-tuple-element.49.log_norms) | copy-start | bytes 24580
  178.2 4.5 %copy-start.25 = (bf16[1280,1280]{1,0:T(8,128)(2,1)S(1)}, bf16[1280,1280]{1,0:T(8,128)(2,1)}, u32[]{:S(2)}) copy-start(bf16[1280,1280]{1,0:T(8,128)(2,1)} %get-tuple-element.44) | copy-start | bytes 9830404
  182.5 5.0 %copy-start.21 = (f32[128,1280]{1,0:T(8,128)}, f32[128,1280]{1,0:T(8,128)S(1)}, u32[]{:S(2)}) copy-start(f32[128,1280]{1,0:T(8,128)S(1)} %get-tuple-element.109) | copy-start | bytes 1966084
  182.6 3.5 copy-start.31
  182.6 2.2 copy-start.26
  182.7 2.3 copy-start.28
  184.1 4.5 %slice-start = ((s8[5242880]{0:T(1024)(128)(4,1)}), s8[4194304]{0:T(1024)(128)(4,1)S(1)}, s32[]{:S(2)}) async-start(s8[5242880]{0:T(1024)(128)(4,1)} %bitcast.96), calls=%async_computation | async-start | bytes 8388608
  184.9 3.7 slice-start.1
  186.2 2.4 copy-start.30
  188.6 2.7 copy-start.27
  191.3 108.2 %copy-start.36 = (f32[4096]{0:T(1024)S(1)}, f32[4096]{0:T(1024)}, u32[]{:S(2)}) copy-start(f32[4096]{0:T(1024)} %constant.148.clone.1) | copy-start | bytes 49156
  297.9 1.9 copy-start.24
  300.1 10.1 %copy-start.2 = (s32[1280,1]{1,0:T(8,128)S(1)}, s32[1280,1]{1,0:T(8,128)}, u32[]{:S(2)}) copy-start(s32[1280,1]{1,0:T(8,128)} %constant.154.clone.tenth_col) | copy-start | bytes 15364
  300.1 10.1 %copy-start.5 = (bf16[3,256,80]{2,1,0:T(8,128)(2,1)S(1)}, bf16[3,256,80]{2,1,0:T(8,128)(2,1)}, u32[]{:S(2)}) copy-start(bf16[3,256,80]{2,1,0:T(8,128)(2,1)} %constant.156.clone.take_t) | copy-start | bytes 368644
  300.1 10.1 %copy-start.9 = (bf16[5,256,80]{2,1,0:T(8,128)(2,1)S(1)}, bf16[5,256,80]{2,1,0:T(8,128)(2,1)}, u32[]{:S(2)}) copy-start(bf16[5,256,80]{2,1,0:T(8,128)(2,1)} %constant.157.clone.last_t) | copy-start | bytes 614404
  300.2 10.1 %copy-start.10 = (bf16[1280,128]{1,0:T(8,128)(2,1)S(1)}, bf16[1280,128]{1,0:T(8,128)(2,1)}, u32[]{:S(2)}) copy-start(bf16[1280,128]{1,0:T(8,128)(2,1)} %constant.158.clone.lane_of_t) | copy-start | bytes 983044
  300.2 10.1 %copy-start.11 = (bf16[1280,16]{1,0:T(8,128)(2,1)S(1)}, bf16[1280,16]{1,0:T(8,128)(2,1)}, u32[]{:S(2)}) copy-start(bf16[1280,16]{1,0:T(8,128)(2,1)} %constant.159.clone.row_of_t) | copy-start | bytes 122884
  300.2 10.1 %copy-start.15 = (bf16[256,16]{1,0:T(8,128)(2,1)S(1)}, bf16[256,16]{1,0:T(8,128)(2,1)}, u32[]{:S(2)}) copy-start(bf16[256,16]{1,0:T(8,128)(2,1)} %constant.160.clone.scale_rows) | copy-start | bytes 24580
  300.2 10.1 %copy-start.19 = (s32[1,1280]{1,0:T(1,128)S(1)}, s32[1,1280]{1,0:T(1,128)}, u32[]{:S(2)}) copy-start(s32[1,1280]{1,0:T(1,128)} %constant.153.clone.tenth_row) | copy-start | bytes 15364
  367.6 6.3 %copy-start.32 = (f32[32,1280]{1,0:T(8,128)S(1)}, f32[32,1280]{1,0:T(8,128)}, u32[]{:S(2)}) copy-start(f32[32,1280]{1,0:T(8,128)} %get-tuple-element.51) | copy-start | bytes 491524
  367.6 7.0 %copy-start.22 = (f32[128,1280]{1,0:T(8,128)S(1)}, f32[128,1280]{1,0:T(8,128)}, u32[]{:S(2)}) copy-start(f32[128,1280]{1,0:T(8,128)} %copy-done.21) | copy-start | bytes 1966084
  367.6 7.0 %copy-start.29 = (bf16[128,1280]{1,0:T(8,128)(2,1)S(1)}, bf16[128,1280]{1,0:T(8,128)(2,1)}, u32[]{:S(2)}) copy-start(bf16[128,1280]{1,0:T(8,128)(2,1)} %get-tuple-element.110.activated) | copy-start | bytes 983044
where the time goes:
time: 382 us; the launch traced here: 378 us
  Pallas kernels  312 us (82%)
  matrix products  28.7 us (8%)
  local copies, waits for them, and re-layouts  19.1 us (5%)
  other arithmetic  16 us (4%)
    pallas_call x1, Pallas kernels, attend_back(): pl.pallas_call(backward_kernel, out_shape=(jax.ShapeDtypeStruct((2 * TOK,...  107 us
    pallas_call x1, Pallas kernels, attend(): pl.pallas_call(forward_kernel, out_shape=(jax.ShapeDtypeStruct((16, B, LA...  90.2 us
    pallas_call x1, Pallas kernels, gather_weights(): pl.pallas_call(gather_kernel, out_shape=(jax.ShapeDtypeStruct((D, WIDE),...  58.5 us
    pallas_call x1, Pallas kernels, scatter_grads(): pl.pallas_call(scatter_kernel, out_shape=jax.ShapeDtypeStruct((ROWS, D),...  57.2 us
    dot_general x4, matrix products, nn(): lax.dot_general(a, b, (((1,), (0,)), ((), ())), preferred_element_type=f32)  14.9 us
    dot_general x4, matrix products, nt(): lax.dot_general(a, b, (((1,), (1,)), ((), ())), preferred_element_type=f32)  13.8 us
    unnamed x91, local copies, waits for them, and re-layouts  10.5 us

commit v1 on v0

--- a/solution.py
+++ b/solution.py
@@ -21,6 +21,8 @@
 WIDE = H * LANES
 OUT_WIDE = H * 128
 GROUP = 80
+CHUNK = 96
+MINE = 512
 EPSILON = 1e-06
 LOG2E = 1.442695041
 NEGATIVE = -1e30
@@ -28,8 +30,7 @@
 f32 = jnp.float32
 bf16 = jnp.bfloat16
 
-PARTS = (((0, 512), "xyz"), ((512, 384), "yzx"), ((896, 384), "zxy"))
-PARTS_TWO = (((0, 640), "xyz"), ((640, 640), "xzy"))
+PARTS = (((0, 640), "xyz"), ((640, 640), "xzy"))
 
 
 def inverse_rms(values):
@@ -129,33 +130,35 @@
 
 
 def selections():
-    take = np.zeros((3, GROUP, 256), np.float32)
-    last = np.zeros((5, GROUP, 256), np.float32)
+    spread = np.zeros((288, 256), np.float32)
+    join = np.zeros((CHUNK, 256), np.float32)
+    order = np.zeros((4 * GROUP, 4 * CHUNK), np.float32)
     for i in range(8):
         for j in range(10):
-            for w in range(3):
-                take[w, i * 10 + j, i * ROWS + w * 10 + j] = 1
-            last[j % 5, i * 10 + j, i * ROWS + 30 + j // 5] = 1
-    spread = np.zeros((128, 256), np.float32)
-    spread[32:112] = take[0]
-    return take, last, spread
-
-
-TAKE, LAST, SPREAD = selections()
-LANE_OF = np.zeros((128, D), np.float32)
-LANE_OF[112 + np.arange(D) % 10, np.arange(D)] = 1
-ROW_OF = np.zeros((16, D), np.float32)
-ROW_OF[np.arange(D) % 10, np.arange(D)] = 1
-TENTH = (np.arange(D) // 10).astype(np.int32)
-SCALE_ROWS = np.zeros((256, 16), np.float32)
-for _i in range(8):
-    for _j in range(8):
-        SCALE_ROWS[_i * ROWS + _j, _j] = 1
+            spread[32 + i * 10 + j, i * ROWS + j] = 1
+            spread[128 + i * 10 + j, i * ROWS + 10 + j] = 1
+            spread[208 + i * 10 + j, i * ROWS + 20 + j] = 1
+            join[i * 10 + j, i * ROWS + j] = 1
+            inner, x_high = i // 2, i % 2
+            for y in range(4):
+                order[inner * GROUP + (y * 2 + x_high) * 10 + j, y * CHUNK + i * 10 + j] = 1
+        for v in range(16):
+            join[GROUP + v, i * ROWS + 16 + v] = 1
+    share = join.T.copy()
+    return spread, join, share, order
+
+
+SPREAD, JOIN, SHARE, ORDER = selections()
+TAKE_T = np.stack([SPREAD[32:112].T, SPREAD[128:208].T, SPREAD[208:288].T])
+
+
+def row_block(ref, g, count):
+    return ref.at[pl.ds(pl.multiple_of(g * count, 16), count)]
 
 
 class Gather:
-    def __init__(self, parts, buf, send, recv, place):
-        self.parts, self.place = parts, place
+    def __init__(self, buf, send, recv, place):
+        self.place = place
         self.buf, self.send, self.recv = buf, send, recv
         self.sibling = device_at(moved(place, "c", 1 - place["c"]))
 
@@ -167,7 +170,7 @@
         return own
 
     def forward(self, part, axes, fixed, count):
-        first, width = self.parts[part][0]
+        first, width = PARTS[part][0]
         cols = pl.ds(first, width)
 
         @pl.loop(0, count)
@@ -179,7 +182,7 @@
             ).start()
 
     def stage(self, stage):
-        for part, ((first, width), order) in enumerate(self.parts):
+        for part, ((first, width), order) in enumerate(PARTS):
             cols = pl.ds(first, width)
             if stage:
                 wait_bytes(
@@ -204,7 +207,7 @@
                         device_at(target),
                     ).start()
 
-        for part, (_, order) in enumerate(self.parts):
+        for part, (_, order) in enumerate(PARTS):
             if stage == 0:
                 self.forward(part, "", {}, 1)
             else:
@@ -219,7 +222,7 @@
 
     def finish(self):
         for step in (1, 3, 2):
-            for part, ((first, width), order) in enumerate(self.parts):
+            for part, ((first, width), order) in enumerate(PARTS):
                 wait_bytes(
                     self.buf.at[pl.ds(0, 2), :, pl.ds(first, width)],
                     self.recv.at[part, 1 + step],
@@ -228,7 +231,7 @@
                 self.forward(
                     part, order[:2], {axis: (self.place[axis] + 4 - step) % 4}, 16
                 )
-        for part, ((first, width), order) in enumerate(self.parts):
+        for part, ((first, width), order) in enumerate(PARTS):
             cols = pl.ds(first, width)
             half = self.buf.at[pl.ds(0, 8), :, cols]
             wait_bytes(half, self.recv.at[part, 5])
@@ -240,91 +243,11 @@
             wait_bytes(self.buf.at[pl.ds(0, 6), :, cols], self.send.at[part, 2])
 
 
-def row_block(ref, g, count):
-    return ref.at[pl.ds(pl.multiple_of(g * count, 16), count)]
-
-
-def gather_kernel(
-    pack, take, last, lane_of, row_of, tenth_row, tenth_col, wide, vectors,
-    buf, vec_tile, staged, send, recv, own_sem, out_sem,
-):
-    place = my_place()
-    gather = Gather(PARTS, buf, send, recv, place)
-    own = gather.begin(pack, own_sem)
-    greet(ring_peers(place))
-    own.wait()
-    for stage in range(3):
-        gather.stage(stage)
-    gather.finish()
-
-    @pl.loop(0, 16)
-    def _(g):
-        slot = g % 2
-        out = pltpu.make_async_copy(staged.at[slot], row_block(wide, g, GROUP), out_sem.at[slot])
-
-        @pl.when(g >= 2)
-        def _():
-            out.wait()
-
-        for w in range(3):
-            staged[slot, :, w * D : (w + 1) * D] = nn(take[w], buf[g]).astype(bf16)
-        head = jnp.zeros((GROUP, LANES), f32)
-        for cell in range(5):
-            head = head + nn(last[cell], buf[g, :, cell * LANES : (cell + 1) * LANES])
-        staged[slot, :, 3 * D :] = head.astype(bf16)
-        vec_tile[pl.ds(pl.multiple_of(g * GROUP, 16), GROUP)] = staged[slot, :, 128:256]
-        out.start()
-
-    spread_out = nn(vec_tile[...], lane_of[...])
-    spread_out = jnp.where(tenth_col[...] == tenth_row[...], spread_out, 0.0).astype(bf16)
-    vectors[...] = nn(row_of[...], spread_out)
-    for slot in range(2):
-        pltpu.make_async_copy(staged.at[slot], row_block(wide, 0, GROUP), out_sem.at[slot]).wait()
-
-
 VMEM = pl.BlockSpec(memory_space=pltpu.VMEM)
 HBM = pl.BlockSpec(memory_space=pl.ANY)
 
 
-def gather_semaphores(parts):
-    return [pltpu.SemaphoreType.DMA((parts, 4)), pltpu.SemaphoreType.DMA((parts, 6))]
-
-
-def gather_weights(pack):
-    return pl.pallas_call(
-        gather_kernel,
-        out_shape=(
-            jax.ShapeDtypeStruct((D, WIDE), bf16),
-            jax.ShapeDtypeStruct((16, D), f32),
-        ),
-        in_specs=[VMEM] * 7,
-        out_specs=(HBM, VMEM),
-        scratch_shapes=[
-            pltpu.VMEM((16, 256, D), bf16),
-            pltpu.VMEM((D, 128), bf16),
-            pltpu.VMEM((2, GROUP, WIDE), bf16),
-        ]
-        + gather_semaphores(3)
-        + [
-            pltpu.SemaphoreType.DMA,
-            pltpu.SemaphoreType.DMA((2,)),
-        ],
-        compiler_params=pltpu.CompilerParams(
-            collective_id=0, has_side_effects=True, vmem_limit_bytes=40 * 2**20
-        ),
-        name="gather_weights",
-    )(
-        pack,
-        jnp.asarray(TAKE, bf16),
-        jnp.asarray(LAST, bf16),
-        jnp.asarray(LANE_OF, bf16),
-        jnp.asarray(ROW_OF, bf16),
-        jnp.asarray(TENTH[None, :]),
-        jnp.asarray(TENTH[:, None]),
-    )
-
-
-def unpack_two(buf, staged, spread, take, out_w, hidden_w, proj_w, out_sem):
+def unpack(buf, staged, spread, out_w, hidden_w, proj_w, out_sem):
     spans = ((0, 128, out_w), (128, GROUP, hidden_w), (208, GROUP, proj_w))
 
     @pl.loop(0, 16)
@@ -342,9 +265,7 @@
             for out in outs:
                 out.wait()
 
-        staged[slot, 0:128] = nn(spread[...], buf[g]).astype(bf16)
-        staged[slot, 128:208] = nn(take[1], buf[g]).astype(bf16)
-        staged[slot, 208:288] = nn(take[2], buf[g]).astype(bf16)
+        staged[slot] = nn(spread[...], buf[g]).astype(bf16)
         for out in outs:
             out.start()
 
@@ -356,8 +277,7 @@
 
 
 class Scatter:
-    def __init__(self, parts, away, mine, pair, lands, halves, send, recv, place):
-        self.parts = parts
+    def __init__(self, away, mine, pair, lands, halves, send, recv, place):
         self.away, self.mine, self.pair = away, mine, pair
         self.lands, self.halves = lands, halves
         self.send, self.recv, self.place = send, recv, place
@@ -367,8 +287,8 @@
         return remote(
             self.away.at[number],
             self.pair.at[number],
-            self.send.at[len(self.parts), number],
-            self.recv.at[len(self.parts), number],
+            self.send.at[len(PARTS), number],
+            self.recv.at[len(PARTS), number],
             self.sibling,
         )
 
@@ -383,7 +303,7 @@
         return self.mine.at[half, pl.ds((where["y"] * 2 + where["x"] // 2) * ROWS, ROWS), cols]
 
     def start(self, stage):
-        for part, ((first, width), order) in enumerate(self.parts):
+        for part, ((first, width), order) in enumerate(PARTS):
             cols = pl.ds(first, width)
             axis = order[2 - stage]
             rest = order[: 2 - stage]
@@ -407,7 +327,7 @@
                     ).start()
 
     def add(self, stage, out=None):
-        for part, ((first, width), order) in enumerate(self.parts):
+        for part, ((first, width), order) in enumerate(PARTS):
             cols = pl.ds(first, width)
             axis = order[2 - stage]
             rest = order[: 2 - stage]
@@ -433,13 +353,13 @@
 
     def finish(self):
         for stage in range(3):
-            for part, ((first, width), order) in enumerate(self.parts):
+            for part, ((first, width), order) in enumerate(PARTS):
                 wait_bytes(
                     self.lands[stage].at[:, :, :, pl.ds(first, width)], self.send.at[part, stage]
                 )
 
 
-def scatter_scratch(parts):
+def scatter_scratch():
     return [
         pltpu.VMEM((8, 256, D), bf16),
         pltpu.VMEM((8, 256, D), bf16),
@@ -449,96 +369,67 @@
         pltpu.VMEM((3, 1, ROWS, D), bf16),
         pltpu.VMEM((4, 4, ROWS, D), bf16),
         pltpu.VMEM((4, ROWS, D), bf16),
-        pltpu.SemaphoreType.DMA((parts + 1, 8)),
-        pltpu.SemaphoreType.DMA((parts + 1, 8)),
+        pltpu.SemaphoreType.DMA((3, 8)),
+        pltpu.SemaphoreType.DMA((3, 8)),
     ]
 
 
-def scatter_of(parts, scratch, place):
+def scatter_of(scratch, place):
     away, mine, pair, l0, l1, l2, h0, h1, send, recv = scratch
-    return Scatter(parts, away, mine, pair, (l0, l1, l2), (h0, h1), send, recv, place)
-
-
-def scatter_kernel(
-    normed, d_wide, vector_grads, scale_tile,
-    take_t, last_t, lane_of_t, row_of_t, scale_rows, tenth_row, tenth_col,
-    out, normed_t, right, vec_tile, *scratch,
-):
-    place = my_place()
-    scatter = scatter_of(PARTS, scratch, place)
-    for n in range(D // 128):
-        lanes = slice(n * 128, n * 128 + 128)
-        normed_t[lanes] = normed[:, lanes].T
-    for w in range(3):
-        right[w * 128 : w * 128 + 128] = d_wide[:, w * D : (w + 1) * D]
-    for cell in range(5):
-        right[384:512, cell * LANES : (cell + 1) * LANES] = d_wide[:, 3 * D :]
-    by_row = nn(row_of_t[...], vector_grads[...])
-    by_row = jnp.where(tenth_col[...] == tenth_row[...], by_row, 0.0).astype(bf16)
-    vec_tile[...] = nn(by_row, lane_of_t[...]).astype(bf16)
-    greet(ring_peers(place))
-
-    def produce(number, core, into):
-        group = number * 2 + core
-        rows = pl.ds(pl.multiple_of(group * GROUP, 16), GROUP)
-        piece = normed_t[rows]
-        lefts = [nn(take_t[w], piece).astype(bf16) for w in range(3)]
-        for cell in range(5):
-            left = jnp.concatenate(lefts + [nn(last_t[cell], piece).astype(bf16)], axis=1)
-            lanes = slice(cell * LANES, (cell + 1) * LANES)
-            block = nn(left, right[:, lanes])
-            if cell == 0:
-                block = block + jnp.concatenate(
-                    [jnp.zeros((256, 128), f32), nn(take_t[0], vec_tile[rows])], axis=1
-                )
-            if cell == 1:
-                block = block + jnp.concatenate(
-                    [jnp.zeros((256, 128), f32), nn(scale_rows[...], scale_tile[...])], axis=1
-                )
-            into[number, :, lanes] = block.astype(bf16)
-
-    @pl.loop(0, 8)
-    def _(number):
-        produce(number, 1 - place["c"], scatter.away)
-        scatter.swap(number).start()
-
-    @pl.loop(0, 8)
-    def _(number):
-        produce(number, place["c"], scatter.mine)
-        scatter.add_pair(number)
-
-    for stage in range(3):
-        scatter.start(stage)
-        scatter.add(stage, out)
-    scatter.finish()
-
-
-def scatter_grads(*operands):
-    return pl.pallas_call(
-        scatter_kernel,
-        out_shape=jax.ShapeDtypeStruct((ROWS, D), f32),
-        in_specs=[VMEM] * 11,
-        out_specs=VMEM,
-        scratch_shapes=[
-            pltpu.VMEM((D, 128), bf16),
-            pltpu.VMEM((512, D), bf16),
-            pltpu.VMEM((D, 128), bf16),
-        ]
-        + scatter_scratch(3),
-        compiler_params=pltpu.CompilerParams(
-            collective_id=3, has_side_effects=True, vmem_limit_bytes=48 * 2**20
-        ),
-        name="scatter_grads",
-    )(
-        *operands,
-        jnp.asarray(TAKE.transpose(0, 2, 1), bf16),
-        jnp.asarray(LAST.transpose(0, 2, 1), bf16),
-        jnp.asarray(LANE_OF.T, bf16),
-        jnp.asarray(ROW_OF.T, bf16),
-        jnp.asarray(SCALE_ROWS, bf16),
-        jnp.asarray(TENTH[None, :]),
-        jnp.asarray(TENTH[:, None]),
-    )
+    return Scatter(away, mine, pair, (l0, l1, l2), (h0, h1), send, recv, place)
+
+
+HALVES = ((0, "yz"), (256, "zy"))
+
+
+def ring_devices(place):
+    others = [moved(place, "c", 1 - place["c"])]
+    for step in (1, 3, 2):
+        there = moved(place, "x", (place["x"] + step) % 4)
+        others += [there, moved(there, "c", 1 - place["c"])]
+    return others
+
+
+def ring_number(place):
+    return (place["x"] % 2) * 4 + place["c"] * 2 + place["x"] // 2
+
+
+def tokens_of(ref, place):
+    inner = (place["x"] % 2) * 2 + place["c"]
+    return ref.at[inner, :, pl.ds((place["x"] // 2) * TOK, TOK)]
+
+
+def head_of(place):
+    return (place["x"] // 2) * 8 + (place["z"] % 2) * 4 + place["y"]
+
+
+def pair_device(pair, quarter):
+    micro, h = pair // H, pair % H
+    return ((micro * 2 + (h % 8) // 4) * 4 + quarter, (h % 4) * 2 + h // 8)
+
+
+def gather_columns(buf, send, recv, place, stage):
+    for half, (first, order) in enumerate(HALVES):
+        cols = pl.ds(first, 256)
+        axis = order[stage]
+        if stage:
+            wait_bytes(buf.at[0, pl.ds(0, 3 * CHUNK), cols], recv.at[half, 0])
+        for number in range(4**stage):
+            where = varied(place, order[:stage], number)
+            piece = buf.at[where["z"], pl.ds(where["y"] * CHUNK, CHUNK), cols]
+            for step in (1, 3, 2):
+                target = moved(place, axis, (place[axis] + step) % 4)
+                remote(
+                    piece, piece, send.at[half, stage], recv.at[half, stage], device_at(target)
+                ).start()
+
+
+def finish_columns(buf, send, recv):
+    for half, (first, _) in enumerate(HALVES):
+        cols = pl.ds(first, 256)
+        wait_bytes(buf.at[pl.ds(0, 3), :, cols], recv.at[half, 1])
+        wait_bytes(buf.at[0, pl.ds(0, 3 * CHUNK), cols], send.at[half, 0])
+        wait_bytes(buf.at[pl.ds(0, 3), :, cols], send.at[half, 1])
 
 
 def quarter_of(blk):
@@ -584,45 +475,115 @@
         wait_bytes(cell_of(ref, 0, width), sem)
 
 
-def forward_kernel(
-    pack, starts, pack_two, spread, take,
-    kv_out, queries, out_t, log_norms, attended, out_w, hidden_w, proj_w,
-    kv, value_t, tops, totals, rounded, landed, buf, staged,
-    two_send, two_recv, send, recv, core_send, core_recv, x_send, x_recv,
-    pass_send, pass_recv, back_send, back_recv, kv_sem, own_sem, out_sem,
+def stays_here(place):
+    return (place["z"] % 2 == place["x"] % 2) & (place["y"] // 2 == place["c"])
+
+
+def wait_ring(ref, sem, place):
+    wait_bytes(ref.at[pl.ds(0, 3)], sem)
+    wait_bytes(ref.at[0, pl.ds(0, 384)], sem)
+
+    @pl.when(jnp.logical_not(stays_here(place)))
+    def _():
+        wait_bytes(ref.at[0, pl.ds(0, 128)], sem)
+
+
+def front_kernel(
+    tokens, pieces, pack, scale_row, starts, join, order, spread,
+    normed_out, packed_out, wide_w, vectors, kv_out, queries, out_t, log_norms, attended,
+    out_w, hidden_w, proj_w,
+    ring_tokens, ring_pieces, chunks, kv, value_t, tops, totals, rounded, landed, buf, staged,
+    x_tok_send, x_tok_recv, c_tok_send, c_tok_recv, piece_send, piece_recv, col_send, col_recv,
+    two_send, two_recv, own_sem, send, recv, core_send, core_recv, x_send, x_recv,
+    pass_send, pass_recv, back_send, back_recv, kv_sem, out_sem,
 ):
     blk = lax.axis_index("blk")
     head = lax.axis_index("head")
     core = blk % 2
     x_low = (blk // 2) % 2
     quarter = blk % 4
-    pair = (blk // 4) * 8 + head
-    to_quarter = quarter_of(blk)
     even = (blk // 4) % 2 == 0
     place = my_place()
-    two = Gather(PARTS_TWO, buf, two_send, two_recv, place)
-    own = two.begin(pack_two, own_sem)
+    pair = (place["z"] // 2) * H + head_of(place)
+    turn = place["x"] * 2 + core
+    sibling = (blk + 1 - 2 * core, head)
+    partner = (blk + 2 - 4 * x_low, head)
+    two = Gather(buf, two_send, two_recv, place)
+    own = two.begin(pack, own_sem.at[0])
+    own_tokens = pltpu.make_async_copy(tokens, tokens_of(ring_tokens, place), own_sem.at[1])
+    own_tokens.start()
+    number = ring_number(place)
+    pltpu.make_async_copy(pieces.at[turn], ring_pieces.at[number], piece_recv).start()
     greet_all()
-
-    @pl.loop(0, PAIRS)
-    def _(k):
-        p = (pair + k) % PAIRS
-        src = cell_of(pack, p, LANES)
-        dst = kv.at[blk, pl.ds(head * TOK, TOK)]
-        mine = (k == 0) & even
-
-        @pl.when(mine)
-        def _():
-            pltpu.make_async_copy(src, dst, recv).start()
-
-        @pl.when(jnp.logical_not(mine))
-        def _():
-            remote(src, dst, send, recv, ((p // 8) * 4 + to_quarter, p % 8)).start()
-
+    for there in ring_devices(place):
+        remote(
+            pieces.at[there["x"] * 2 + there["c"]],
+            ring_pieces.at[number],
+            piece_send,
+            piece_recv,
+            device_at(there),
+        ).start()
+    mine = tokens_of(ring_tokens, place)
+    for step in (1, 3, 2):
+        there = moved(place, "x", (place["x"] + step) % 4)
+        remote(
+            tokens, mine, x_tok_send.at[step - 1], x_tok_recv.at[step - 1], device_at(there)
+        ).start()
+    remote(tokens, mine, c_tok_send, c_tok_recv, sibling).start()
     own.wait()
     two.stage(0)
-    sibling = (blk + 1 - 2 * core, head)
-    partner = (blk + 2 - 4 * x_low, head)
+    wait_bytes(ring_pieces, piece_recv)
+    joined = nn(join[...], ring_pieces[...].reshape(256, MINE)).astype(bf16)
+    chunks[place["z"], pl.ds(pl.multiple_of(place["y"] * CHUNK, 32), CHUNK)] = joined
+    gather_columns(chunks, col_send, col_recv, place, 0)
+    gather_columns(chunks, col_send, col_recv, place, 1)
+    for step in (1, 3, 2):
+        wait_bytes(tokens, x_tok_recv.at[step - 1])
+        there = moved(place, "x", (place["x"] + 4 - step) % 4)
+        arrived = tokens_of(ring_tokens, there)
+        remote(arrived, arrived, c_tok_send, c_tok_recv, sibling).start()
+    own_tokens.wait()
+    finish_columns(chunks, col_send, col_recv)
+    vector_rows = jnp.zeros((16, MINE), f32)
+    for z in range(4):
+        wide_w[z * 4 * GROUP : (z + 1) * 4 * GROUP] = nn(order[...], chunks[z]).astype(bf16)
+        for y in range(4):
+            at = y * CHUNK + GROUP
+            vector_rows = vector_rows + chunks[z, at : at + 16].astype(f32)
+    vectors[...] = vector_rows
+    bias = vector_rows[0:1]
+    gain = jnp.concatenate([vector_rows[1:2], vector_rows[2:3], vector_rows[3:4, :256]], axis=1)
+    one_lane = jnp.where(
+        lax.broadcasted_iota(jnp.int32, (1, MINE), 1) % LANES == 3 * HD, 1.0, 0.0
+    )
+    wait_bytes(ring_tokens.at[pl.ds(0, 2)], c_tok_recv)
+
+    @pl.loop(0, 4)
+    def _(inner):
+        values = ring_tokens[inner].reshape(256, D).astype(f32)
+        normed = (values * inverse_rms(values) * gain).astype(bf16)
+        normed_out[inner] = normed
+        full = nn(normed, wide_w[...])
+        packed = ((full + bias) * scale_row[0:1] + one_lane).astype(bf16)
+        packed_out[inner] = packed.reshape(2, 128, MINE)
+        block = place["z"] * 4 + inner
+        to_quarter = quarter_of(block)
+        for m in range(2):
+            for h in range(2):
+                blk_to, head_to = pair_device(m * H + turn * 2 + h, to_quarter)
+                src = packed_out.at[inner, m, :, pl.ds(h * LANES, LANES)]
+                dst = kv.at[block, pl.ds(place["y"] * 128, 128)]
+                stays = (blk_to == blk) & (head_to == head)
+
+                @pl.when(stays)
+                def _():
+                    pltpu.make_async_copy(src, dst, recv).start()
+
+                @pl.when(jnp.logical_not(stays))
+                def _():
+                    remote(src, dst, send, recv, (blk_to, head_to)).start()
+
+    two.stage(1)
     wait_bytes(kv.at[pl.ds(0, 4)], recv)
 
     @pl.loop(0, 4)
@@ -631,7 +592,6 @@
         remote(block, block, core_send, core_recv, sibling).start()
         remote(block, block, x_send, x_recv, partner).start()
 
-    two.stage(1)
     pick = shift_matrix(LANES, 128, HD)
 
     @pl.loop(0, 4)
@@ -722,20 +682,29 @@
                 remote(src, dst, back_send, back_recv, (block, h)).start()
 
     two.finish()
-    unpack_two(buf, staged, spread, take, out_w, hidden_w, proj_w, out_sem)
+    unpack(buf, staged, spread, out_w, hidden_w, proj_w, out_sem)
     wait_bytes(landed, back_recv)
     attended[...] = landed[...]
     keep.wait()
     for sem in (core_send, x_send, pass_send):
         wait_bytes(kv.at[pl.ds(0, 4)], sem)
-    wait_cells(pack, send, even, LANES)
     wait_cells(landed, back_send, even, 128)
-
-
-def attend(pack, starts, pack_two):
+    wait_bytes(ring_pieces.at[pl.ds(0, 7)], piece_send)
+    for step_at in range(3):
+        wait_bytes(tokens, x_tok_send.at[step_at])
+    wait_bytes(ring_tokens.at[pl.ds(0, 2)], c_tok_send)
+    wait_ring(kv, send, place)
+
+
+def front(*operands):
+    dma = pltpu.SemaphoreType.DMA
     return pl.pallas_call(
-        forward_kernel,
+        front_kernel,
         out_shape=(
+            jax.ShapeDtypeStruct((4, 256, D), bf16),
+            jax.ShapeDtypeStruct((4, 2, 128, MINE), bf16),
+            jax.ShapeDtypeStruct((D, MINE), bf16),
+            jax.ShapeDtypeStruct((16, MINE), f32),
             jax.ShapeDtypeStruct((16, B, LANES), bf16),
             jax.ShapeDtypeStruct((4, B, 128), bf16),
             jax.ShapeDtypeStruct((4, 128, B), f32),
@@ -745,9 +714,12 @@
             jax.ShapeDtypeStruct((D, D), bf16),
             jax.ShapeDtypeStruct((D, D), bf16),
         ),
-        in_specs=[VMEM] * 5,
-        out_specs=(HBM, VMEM, VMEM, VMEM, VMEM, HBM, HBM, HBM),
+        in_specs=[VMEM] * 8,
+        out_specs=(VMEM, VMEM, VMEM, VMEM, HBM, VMEM, VMEM, VMEM, VMEM, HBM, HBM, HBM),
         scratch_shapes=[
+            pltpu.VMEM((4, 2, 128, D), bf16),
+            pltpu.VMEM((8, ROWS, MINE), bf16),
+            pltpu.VMEM((4, 4 * CHUNK, MINE), bf16),
             pltpu.VMEM((16, B, LANES), bf16),
             pltpu.VMEM((16, 128, B), bf16),
             pltpu.VMEM((4, 1, B), f32),
@@ -756,24 +728,34 @@
             pltpu.VMEM((2 * TOK, OUT_WIDE), bf16),
             pltpu.VMEM((16, 256, D), bf16),
             pltpu.VMEM((2, 288, D), bf16),
+            dma((3,)), dma((3,)), dma, dma, dma, dma, dma((2, 2)), dma((2, 2)),
+            dma((2, 4)), dma((2, 6)), dma((2,)),
         ]
-        + gather_semaphores(2)
-        + [pltpu.SemaphoreType.DMA] * 12
-        + [pltpu.SemaphoreType.DMA((3, 2))],
+        + [dma] * 11
+        + [dma((3, 2))],
         compiler_params=pltpu.CompilerParams(
-            collective_id=1, has_side_effects=True, vmem_limit_bytes=48 * 2**20
+            collective_id=0, has_side_effects=True, vmem_limit_bytes=56 * 2**20
         ),
-        name="attend",
-    )(pack, starts, pack_two, jnp.asarray(SPREAD, bf16), jnp.asarray(TAKE, bf16))
-
-
-def backward_kernel(
+        name="front",
+    )(
+        *operands,
+        jnp.asarray(JOIN, bf16),
+        jnp.asarray(ORDER, bf16),
+        jnp.asarray(SPREAD, bf16),
+    )
+
+
+def rear_kernel(
     pack, kv, queries, starts, out_t, log_norms,
-    attended, d_branch, normed_two, d_pre, activated, upstream, take_t,
-    wide_out, two_out,
-    d_out, key_t, deltas, d_query, d_kv, mine_kv, half, half_in, cross, cross_in, final, landed,
+    attended, d_branch, normed_two, d_pre, activated, upstream,
+    normed, packed, wide_w, vectors, vector_grads, scale_row, take_t, share, order_t,
+    d_normed, pieces_out, two_out,
+    d_out, key_t, deltas, d_query, d_kv, mine_kv, half, half_in, cross, cross_in, final, d_wide,
     attended_t, normed_two_t, activated_t, right,
+    partial_in, sum_in, grad_chunks, first_in, second_in, first_y, first_z,
+    joined, shares, shares_in,
     send, recv, core_send, core_recv, x_send, x_recv, back_send, back_recv,
+    normed_sem, c_send, c_recv, sum_send, sum_recv, col_send, col_recv, share_send, share_recv,
     *scratch,
 ):
     blk = lax.axis_index("blk")
@@ -781,11 +763,12 @@
     core = blk % 2
     x_low = (blk // 2) % 2
     quarter = blk % 4
-    pair = (blk // 4) * 8 + head
+    place = my_place()
+    my_head = head_of(place)
+    pair = (place["z"] // 2) * H + my_head
     to_quarter = quarter_of(blk)
     even = (blk // 4) % 2 == 0
-    place = my_place()
-    two = scatter_of(PARTS_TWO, scratch, place)
+    two = scatter_of(scratch, place)
     greet_all()
 
     @pl.loop(0, PAIRS)
@@ -801,7 +784,7 @@
 
         @pl.when(jnp.logical_not(mine))
         def _():
-            remote(src, dst, send, recv, ((p // 8) * 4 + to_quarter, p % 8)).start()
+            remote(src, dst, send, recv, pair_device(p, to_quarter)).start()
 
     for n in range(D // 128):
         lanes = slice(n * 128, n * 128 + 128)
@@ -847,6 +830,8 @@
     def _(number):
         two.add_pair(number)
 
+    load_normed = pltpu.make_async_copy(normed, two.pair.at[pl.ds(0, 4)], normed_sem)
+    load_normed.start()
     two.start(0)
     wait_bytes(d_out, recv)
 
@@ -906,20 +891,24 @@
             + nn(d_query[z].T.astype(bf16), shift)
         ).astype(bf16)
 
-        @pl.loop(0, 8)
+        @pl.loop(0, 4)
         def _(k):
-            h = (head + k) % 8
-            src = final.at[z, pl.ds(h * TOK, TOK)]
-            dst = cell_of(landed, pair, LANES)
-            mine = (k == 0) & (block == blk)
-
-            @pl.when(mine)
+            y = (place["y"] + k) % 4
+            there = {"x": my_head // 4, "y": y, "z": z, "c": (my_head // 2) % 2}
+            src = final.at[z, pl.ds(y * 128, 128)]
+            dst = d_wide.at[
+                block % 4, place["z"] // 2, :, pl.ds((my_head % 2) * LANES, LANES)
+            ]
+            blk_to, head_to = device_at(there)
+            stays = (blk_to == blk) & (head_to == head)
+
+            @pl.when(stays)
             def _():
                 pltpu.make_async_copy(src, dst, back_recv).start()
 
-            @pl.when(jnp.logical_not(mine))
+            @pl.when(jnp.logical_not(stays))
             def _():
-                remote(src, dst, back_send, back_recv, (block, h)).start()
+                remote(src, dst, back_send, back_recv, (blk_to, head_to)).start()
 
     @pl.loop(0, 8)
     def _(part):
@@ -967,21 +956,187 @@
     two.add(2, two_out)
     finish(3)
     two.finish()
-    wait_bytes(landed, back_recv)
-    wide_out[...] = landed[...]
+    wait_bytes(d_wide, back_recv)
+
+    load_normed.wait()
+    partial, normed_here = two.away, two.pair
+    scale = scale_row[0:1]
+    gain = jnp.concatenate([vectors[1:2], vectors[2:3], vectors[3:4, :256]], axis=1)
+    bias_sum = jnp.zeros((1, MINE), f32)
+    scale_sum = jnp.zeros((1, MINE), f32)
+    gain_sum = jnp.zeros((1, D), f32)
+    for inner in range(4):
+        grad = d_wide[inner].reshape(256, MINE).astype(f32)
+        scale_sum = scale_sum + jnp.sum(
+            grad * packed[inner].reshape(256, MINE).astype(f32), axis=0, keepdims=True
+        )
+        grad = (grad * scale).astype(bf16)
+        d_wide[inner] = grad.reshape(2, 128, MINE)
+        bias_sum = bias_sum + jnp.sum(grad.astype(f32), axis=0, keepdims=True)
+        back = nt(grad, wide_w[...])
+        gain_sum = gain_sum + jnp.sum(
+            back * normed_here[inner].astype(f32), axis=0, keepdims=True
+        )
+        partial[inner] = back.astype(bf16)
+    sibling_at = (blk + 1 - 2 * core, head)
+    c_swaps = []
+    for low in range(2):
+        c_swaps.append(
+            remote(
+                partial.at[low * 2 + 1 - core],
+                partial_in.at[low],
+                c_send.at[low],
+                c_recv.at[low],
+                sibling_at,
+            )
+        )
+        c_swaps[-1].start()
+    gain_sum = gain_sum / gain
+    scale_sum = scale_sum[:, :LANES] + scale_sum[:, LANES:]
+    rows = vector_grads[...] + jnp.concatenate(
+        [
+            bias_sum,
+            gain_sum[:, :512],
+            gain_sum[:, 512:1024],
+            jnp.concatenate([gain_sum[:, 1024:], scale_sum], axis=1),
+            jnp.zeros((12, MINE), f32),
+        ],
+        axis=0,
+    )
+    rows = rows.astype(bf16)
+    for z in range(4):
+        left = jnp.concatenate(
+            [normed_here[inner, :, z * 320 // 128 * 128 : z * 320 // 128 * 128 + 384]
+             for inner in range(4)],
+            axis=0,
+        )
+        skip = z * 320 % 128
+        grads = tn(left, d_wide[...].reshape(1024, MINE))[skip : skip + 320].astype(bf16)
+        grad_chunks[z] = nn(order_t[...], grads).astype(bf16)
+        for y in range(4):
+            grad_chunks[z, y * CHUNK + GROUP : y * CHUNK + GROUP + 16] = rows
+
+    def chunk_rows(y):
+        return pl.ds(pl.multiple_of(y * CHUNK, 32), CHUNK)
+
+    for step_at in (1, 3, 2):
+        z = (place["z"] + step_at) % 4
+        remote(
+            grad_chunks.at[z, :, pl.ds(0, 256)],
+            first_in.at[0, step_at - 1],
+            col_send.at[0, 0],
+            col_recv.at[0, 0],
+            device_at(moved(place, "z", z)),
+        ).start()
+        y = (place["y"] + step_at) % 4
+        for plane in range(4):
+            remote(
+                grad_chunks.at[plane, chunk_rows(y), pl.ds(256, 256)],
+                first_in.at[1, step_at - 1, chunk_rows(plane)],
+                col_send.at[1, 0],
+                col_recv.at[1, 0],
+                device_at(moved(place, "y", y)),
+            ).start()
+    for low in range(2):
+        c_swaps[low].wait()
+        partial[4 + low] = (
+            partial[low * 2 + core].astype(f32) + partial_in[low].astype(f32)
+        ).astype(bf16)
+    for step_at in (1, 3, 2):
+        there = moved(place, "x", (place["x"] + step_at) % 4)
+        for m in range(2):
+            remote(
+                partial.at[4 + there["x"] % 2, pl.ds(m * 128 + (there["x"] // 2) * TOK, TOK)],
+                sum_in.at[step_at - 1, pl.ds(m * TOK, TOK)],
+                sum_send,
+                sum_recv,
+                device_at(there),
+            ).start()
+    wait_bytes(first_in.at[0], col_recv.at[0, 0])
+    total = grad_chunks[place["z"], :, 0:256].astype(f32)
+    for source in range(3):
+        total = total + first_in[0, source].astype(f32)
+    first_y[...] = total.astype(bf16)
+    wait_bytes(first_in.at[1], col_recv.at[1, 0])
+    for plane in range(4):
+        total = grad_chunks[plane, chunk_rows(place["y"]), 256:512].astype(f32)
+        for source in range(3):
+            total = total + first_in[1, source, chunk_rows(plane)].astype(f32)
+        first_z[plane] = total.astype(bf16)
+    for step_at in (1, 3, 2):
+        y = (place["y"] + step_at) % 4
+        remote(
+            first_y.at[chunk_rows(y)],
+            second_in.at[0, step_at - 1],
+            col_send.at[0, 1],
+            col_recv.at[0, 1],
+            device_at(moved(place, "y", y)),
+        ).start()
+        z = (place["z"] + step_at) % 4
+        remote(
+            first_z.at[z],
+            second_in.at[1, step_at - 1],
+            col_send.at[1, 1],
+            col_recv.at[1, 1],
+            device_at(moved(place, "z", z)),
+        ).start()
+    wait_bytes(second_in.at[0], col_recv.at[0, 1])
+    wait_bytes(second_in.at[1], col_recv.at[1, 1])
+    total_y = first_y[chunk_rows(place["y"])].astype(f32)
+    total_z = first_z[place["z"]].astype(f32)
+    for source in range(3):
+        total_y = total_y + second_in[0, source].astype(f32)
+        total_z = total_z + second_in[1, source].astype(f32)
+    joined[:, 0:256] = total_y.astype(bf16)
+    joined[:, 256:512] = total_z.astype(bf16)
+    shares[...] = nn(share[...], joined[...]).astype(bf16).reshape(8, ROWS, MINE)
+    turn = place["x"] * 2 + core
+    for there in ring_devices(place):
+        remote(
+            shares.at[ring_number(there)],
+            shares_in.at[turn],
+            share_send,
+            share_recv,
+            device_at(there),
+        ).start()
+    pltpu.make_async_copy(
+        shares.at[ring_number(place)], shares_in.at[turn], share_recv
+    ).start()
+    wait_bytes(sum_in, sum_recv)
+    for m in range(2):
+        at = pl.multiple_of(m * 128 + (place["x"] // 2) * TOK, TOK)
+        total = partial[4 + x_low, pl.ds(at, TOK)].astype(f32)
+        for source in range(3):
+            total = total + sum_in[source, m * TOK : (m + 1) * TOK].astype(f32)
+        d_normed[m * TOK : (m + 1) * TOK] = total
+    wait_bytes(shares_in, share_recv)
+    pieces_out[...] = shares_in[...]
     wait_cells(pack, send, even, 128)
-    wait_cells(landed, back_send, even, LANES)
-
-
-def attend_back(*operands):
+    wait_bytes(final.at[pl.ds(0, 3)], back_send)
+    wait_bytes(final.at[0, pl.ds(0, 384)], back_send)
+
+    @pl.when(jnp.logical_not(stays_here(place)))
+    def _():
+        wait_bytes(final.at[0, pl.ds(0, 128)], back_send)
+
+    wait_bytes(sum_in, sum_send)
+    for number in range(2):
+        wait_bytes(first_in.at[number], col_send.at[number, 0])
+        wait_bytes(second_in.at[number], col_send.at[number, 1])
+    wait_bytes(shares.at[pl.ds(0, 7)], share_send)
+
+
+def rear(*operands):
+    dma = pltpu.SemaphoreType.DMA
     return pl.pallas_call(
-        backward_kernel,
+        rear_kernel,
         out_shape=(
-            jax.ShapeDtypeStruct((2 * TOK, WIDE), bf16),
+            jax.ShapeDtypeStruct((2 * TOK, D), f32),
+            jax.ShapeDtypeStruct((8, ROWS, MINE), bf16),
             jax.ShapeDtypeStruct((ROWS, D), f32),
         ),
-        in_specs=[VMEM] * 13,
-        out_specs=(VMEM, VMEM),
+        in_specs=[VMEM] * 12 + [HBM] + [VMEM] * 8,
+        out_specs=(VMEM, VMEM, VMEM),
         scratch_shapes=[
             pltpu.VMEM((4, B, 128), bf16),
             pltpu.VMEM((16, 128, B), bf16),
@@ -994,26 +1149,35 @@
             pltpu.VMEM((4, B, LANES), bf16),
             pltpu.VMEM((4, B, LANES), bf16),
             pltpu.VMEM((4, B, LANES), bf16),
-            pltpu.VMEM((2 * TOK, WIDE), bf16),
+            pltpu.VMEM((4, 2, 128, MINE), bf16),
             pltpu.VMEM((OUT_WIDE, 128), bf16),
             pltpu.VMEM((D, 128), bf16),
             pltpu.VMEM((D, 128), bf16),
             pltpu.VMEM((384, D), bf16),
-            pltpu.SemaphoreType.DMA,
-            pltpu.SemaphoreType.DMA,
-            pltpu.SemaphoreType.DMA((8,)),
-            pltpu.SemaphoreType.DMA((8,)),
-            pltpu.SemaphoreType.DMA((4,)),
-            pltpu.SemaphoreType.DMA((4,)),
-            pltpu.SemaphoreType.DMA,
-            pltpu.SemaphoreType.DMA,
+            pltpu.VMEM((2, 256, D), bf16),
+            pltpu.VMEM((3, 2 * TOK, D), bf16),
+            pltpu.VMEM((4, 4 * CHUNK, MINE), bf16),
+            pltpu.VMEM((2, 3, 4 * CHUNK, 256), bf16),
+            pltpu.VMEM((2, 3, CHUNK, 256), bf16),
+            pltpu.VMEM((4 * CHUNK, 256), bf16),
+            pltpu.VMEM((4, CHUNK, 256), bf16),
+            pltpu.VMEM((CHUNK, MINE), bf16),
+            pltpu.VMEM((8, ROWS, MINE), bf16),
+            pltpu.VMEM((8, ROWS, MINE), bf16),
+            dma, dma, dma((8,)), dma((8,)), dma((4,)), dma((4,)), dma, dma,
+            dma, dma((2,)), dma((2,)), dma, dma, dma((2, 2)), dma((2, 2)), dma, dma,
         ]
-        + scatter_scratch(2),
+        + scatter_scratch(),
         compiler_params=pltpu.CompilerParams(
-            collective_id=2, has_side_effects=True, vmem_limit_bytes=60 * 2**20
+            collective_id=1, has_side_effects=True, vmem_limit_bytes=63 * 2**20
         ),
-        name="attend_back",
-    )(*operands, jnp.asarray(TAKE.transpose(0, 2, 1), bf16))
+        name="rear",
+    )(
+        *operands,
+        jnp.asarray(TAKE_T, bf16),
+        jnp.asarray(SHARE, bf16),
+        jnp.asarray(ORDER.T, bf16),
+    )
 
 
 def on_device(
@@ -1036,21 +1200,37 @@
     cotangent,
 ):
     blk = lax.axis_index("blk")
-    vectors = jnp.stack(
-        [norm1_gain, query_bias, value_bias, out_bias, norm2_gain, hidden_bias, proj_bias]
-    )
-    spare = jnp.pad(vectors[:, None], ((0, 3), (0, H - 1), (0, 6)))
-    rows = jnp.concatenate(
-        [w.reshape(10, H, HD) for w in (w_key, w_query, w_value)] + [spare], axis=2
-    )
-    pack_one = jnp.concatenate(
-        [rows[:, w * 5 : w * 5 + 5].reshape(10, D) for w in range(3)]
-        + [rows[:, 15].reshape(2, D)],
-        axis=0,
-    )
-    pack_two = jnp.concatenate([w_out, w_hidden, w_proj, jnp.zeros((2, D), bf16)], axis=0)
-    wide_w, every = gather_weights(pack_one)
-    gain_one, query_b, value_b, out_b, gain_two, hidden_b, proj_b = [every[i] for i in range(7)]
+    head = lax.axis_index("head")
+    at = (blk * 8 + head) * 10
+    spread_heads = jnp.zeros((H, LANES), bf16)
+    for i, vector in ((1, query_bias), (2, value_bias)):
+        spread_heads = lax.dynamic_update_slice(
+            spread_heads, vector[None], (blk, i * HD + head * 10)
+        )
+    natural = jnp.stack([norm1_gain, out_bias, norm2_gain, hidden_bias, proj_bias])
+    natural = lax.dynamic_update_slice(jnp.zeros((5, 3 * MINE), bf16), natural, (0, at))
+    columns = jnp.concatenate(
+        [w.reshape(10, H, HD) for w in (w_key, w_query, w_value)]
+        + [jnp.zeros((10, H, LANES - 3 * HD), bf16)],
+        axis=2,
+    )
+    columns = columns.reshape(10, 8, MINE).transpose(1, 0, 2)
+    pieces = jnp.concatenate(
+        [
+            columns,
+            jnp.zeros((8, 6, MINE), bf16),
+            spread_heads.reshape(8, 1, MINE),
+            jnp.broadcast_to(natural.reshape(1, 15, MINE), (8, 15, MINE)),
+        ],
+        axis=1,
+    )
+    pack = jnp.concatenate([w_out, w_hidden, w_proj, jnp.zeros((2, D), bf16)], axis=0)
+    softplus_scale = LOG2E / math.sqrt(HD) * jax.nn.softplus(dim_scale)
+    ones = jnp.ones((HD,), f32)
+    scale_row = jnp.concatenate(
+        [ones, softplus_scale, ones, jnp.zeros((LANES - 3 * HD,), f32)] * 2
+    )
+    scale_row = jnp.broadcast_to(scale_row, (8, MINE))
 
     micro = blk // 8
     segment_row = lax.dynamic_index_in_dim(segment_ids, micro, 0, keepdims=False)
@@ -1062,26 +1242,14 @@
     starts = starts.reshape(16, 1, B)
     starts = jnp.stack([starts[query_block(quarter, j)] for j in range(4)])
 
-    def lanes_of(key, query, value, spare_lanes):
-        parts = [jnp.broadcast_to(part.reshape(-1, HD), (H, HD)) for part in (key, query, value)]
-        return jnp.concatenate(parts + [jnp.broadcast_to(spare_lanes, (H, 16))], 1).reshape(WIDE)
+    (
+        ring_normed, packed, wide_w, vectors, kv, queries, out_t, log_norms, attended,
+        out_w, hidden_w, proj_w,
+    ) = front(inputs, pieces, pack, scale_row, starts)
+    every = vectors[1:].reshape(5, 3 * MINE)[:, :D]
+    gain_one, out_b, gain_two, hidden_b, proj_b = [every[i] for i in range(5)]
 
     tokens = inputs.reshape(2 * TOK, D).astype(f32)
-    inverse_one = inverse_rms(tokens)
-    normed = (tokens * inverse_one * gain_one).astype(bf16)
-    softplus_scale = LOG2E / math.sqrt(HD) * jax.nn.softplus(dim_scale)
-    ones = jnp.ones((HD,), f32)
-    zeros = jnp.zeros((HD,), f32)
-    none = jnp.zeros((16,), f32)
-    wide_bias = lanes_of(zeros, query_b, value_b, none)
-    wide_scale = lanes_of(ones, softplus_scale, ones, none)
-    wide_one = lanes_of(zeros, zeros, zeros, none.at[0].set(1.0))
-    wide_full = nn(normed, wide_w) + wide_bias
-    packed = (wide_full * wide_scale + wide_one).astype(bf16)
-    kv, queries, out_t, log_norms, attended, out_w, hidden_w, proj_w = attend(
-        packed, starts, pack_two
-    )
-
     residual = tokens + nn(attended, out_w) + out_b
     inverse_two = inverse_rms(residual)
     normed_two = (residual * inverse_two * gain_two).astype(bf16)
@@ -1097,65 +1265,59 @@
     d_residual = upstream + norm_back(d_normed_two * gain_two, residual, inverse_two)
     d_branch = d_residual.astype(bf16)
     d_attended = nt(d_branch, out_w).astype(bf16)
-    d_scaled, two = attend_back(
-        d_attended, kv, queries, starts, out_t, log_norms,
-        attended, d_branch, normed_two, d_pre, activated, upstream_low,
-    )
-    d_scaled = d_scaled.astype(f32)
-    query_lanes = lanes_of(zeros, ones, zeros, none)
-    scale_terms = jnp.sum(d_scaled * wide_full, axis=0) * query_lanes
-    scale_terms = jnp.sum(scale_terms.reshape(H, LANES), axis=0)[HD : 2 * HD]
-    d_wide = (d_scaled * wide_scale).astype(bf16)
-    d_normed = nt(d_wide, wide_w)
-    input_grad = (
-        d_residual + norm_back(d_normed * gain_one, tokens, inverse_one)
-    ).astype(bf16)
 
     def total(values):
         return jnp.sum(values.astype(f32), axis=0)
 
-    d_bias = total(d_wide).reshape(H, LANES)
     vector_grads = jnp.stack(
         [
-            total(d_normed * tokens * inverse_one),
-            d_bias[:, HD : 2 * HD].reshape(D),
-            d_bias[:, 2 * HD : 3 * HD].reshape(D),
             total(d_branch),
             total(d_normed_two * residual * inverse_two),
             total(d_pre),
             total(upstream),
         ]
     )
-    vector_grads = jnp.pad(vector_grads, ((0, 9), (0, 0))).astype(bf16)
-    scale_tile = jnp.pad(scale_terms.reshape(8, 10), ((0, 8), (112, 6))).astype(bf16)
-    one = scatter_grads(normed, d_wide, vector_grads, scale_tile)
-    rows = jnp.concatenate(
-        [one[w * 10 : w * 10 + 10].reshape(10, 5, LANES) for w in range(3)]
-        + [one[30:32].reshape(10, 1, LANES)],
-        axis=1,
-    )
+    vector_grads = jnp.pad(vector_grads, ((0, 0), (0, 3 * MINE - D))).reshape(12, MINE)
+    vector_grads = jnp.pad(vector_grads, ((4, 0), (0, 0)))
+    d_normed, shares, two = rear(
+        d_attended, kv, queries, starts, out_t, log_norms,
+        attended, d_branch, normed_two, d_pre, activated, upstream_low,
+        ring_normed, packed, wide_w, vectors, vector_grads, scale_row,
+    )
+    inverse_one = inverse_rms(tokens)
+    input_grad = (
+        d_residual + norm_back(d_normed * gain_one, tokens, inverse_one)
+    ).astype(bf16)
+
+    shares = shares.astype(f32)
+    columns = shares[:, :10].transpose(1, 0, 2).reshape(10, H, LANES)
     d_key_w, d_query_w, d_value_w = [
-        rows[:, :, i * HD : (i + 1) * HD].reshape(10, D) for i in range(3)
+        columns[:, :, i * HD : (i + 1) * HD].reshape(10, D) for i in range(3)
     ]
-    vector = [one[i, 240:250] for i in range(7)]
-    scale_grad = one[0:8, 496:506].reshape(HD)
+    by_head = shares[:, 16].reshape(H, LANES)
+    d_query_bias, d_value_bias = [
+        lax.dynamic_slice(by_head, (blk, i * HD + head * 10), (1, 10)).reshape(10) for i in (1, 2)
+    ]
+    summed = jnp.sum(shares[:, 17:], axis=0)
+    scale_grad = summed[2, LANES + HD : LANES + 2 * HD] / softplus_scale
     scale_grad = scale_grad * (LOG2E / math.sqrt(HD)) * jax.nn.sigmoid(dim_scale)
+    natural = lax.dynamic_slice(summed.reshape(5, 3 * MINE), (0, at), (5, 10))
     return (
         layer_out.reshape(2, TOK, D),
         input_grad.reshape(2, TOK, D),
-        vector[0],
+        natural[0],
         d_query_w,
         d_key_w,
         d_value_w,
-        vector[1],
-        vector[2],
+        d_query_bias,
+        d_value_bias,
         two[0:10],
-        vector[3],
-        vector[4],
+        natural[1],
+        natural[2],
         two[10:20],
-        vector[5],
+        natural[3],
         two[20:30],
-        vector[6],
+        natural[4],
         scale_grad,
     )
 

time: 382 us -> 304 us (0.80)
  Pallas kernels: 312 us -> 253 us
  matrix products: 28.7 us -> 11 us
    pallas_call x4 -> x2, Pallas kernels: 312 us -> 253 us  [the longest x1 140 us: rear(): pl.pallas_call(rear_kernel, out_shape=(jax.ShapeDtypeStruct((2 * TOK, D),...]
    dot_general x4 -> x3, matrix products: 14.9 us -> 5.82 us  [nn(): lax.dot_general(a, b, (((1,), (0,)), ((), ())), preferred_element_type=f32)]
    unnamed x91 -> x28, local copies, waits for them, and re-layouts: 10.5 us -> 1.52 us
    dot_general x4 -> x3, matrix products: 13.8 us -> 5.16 us  [nt(): lax.dot_general(a, b, (((1,), (1,)), ((), ())), preferred_element_type=f32)]
where the time goes in v1:
time: 304 us; the launch traced here: 300 us
  Pallas kernels  253 us (83%)
  other arithmetic  19.5 us (6%)
  local copies, waits for them, and re-layouts  15.5 us (5%)
  matrix products  11 us (4%)
    pallas_call x1, Pallas kernels, rear(): pl.pallas_call(rear_kernel, out_shape=(jax.ShapeDtypeStruct((2 * TOK, D),...  140 us
    pallas_call x1, Pallas kernels, front(): pl.pallas_call(front_kernel, out_shape=(jax.ShapeDtypeStruct((4, 256, D),...  113 us
    select_n x1, other arithmetic, on_device(): starts = jnp.where(segment_row == value, before, starts)  6.17 us

profile of v1, /device:TPU:97, one launch (start us, length us, event | category | flops | bytes accessed | tf_op | source)
XLA Modules:
  0.0 300.5 jit_solution(5823456952621000528)
XLA Ops:
  0.7 0.7 fusion.19
  1.4 0.1 pad.21.clone
  1.5 0.1 pad.23.clone
  1.6 0.1 pad.29.clone
  1.7 0.1 concatenate.15
  1.7 1.1 multiply_reduce_fusion.1
  2.9 0.6 rsqrt.27
  3.5 0.7 stack.41
  4.2 1.9 fusion.16
  6.1 1.0 convert_reduce_fusion
  7.2 0.9 dynamic_update_slice.9
  8.1 0.9 dynamic_update_slice.10
  8.9 0.6 broadcast_in_dim.72.scale_row
  9.6 0.2 dynamic_update_slice.11
  9.8 6.2 %compare_select_fusion.7 = s32[1,8192]{1,0:T(1,128)S(1)} fusion(s32[]{:T(128)} %get-tuple-element.49, s32[]{:T(128)} %get-tuple-element.51, s32[]{:T(128)} %get-tuple-element.53, s32[]{:T(128)} %get-tuple-element.55, s32[]{:T(128)} %get-tuple-element.52, s32[]{:T(128)} %get-tuple-element.50, s32[]{:T(128)} %get-tuple-element.54, s32[]{:T(128)} %get-tuple-element.48, ...), kind=kLoop, calls=%fused_computation.48 | loop fusion | flops 131072 | bytes 65572 | tf_op jit(solution)/shard_map/jit(_where)/select_n | solution.py:1240
  16.0 0.6 pad_add_fusion.starts
  16.6 0.9 reshape.281
  17.5 0.9 reshape.280
  18.4 0.9 reshape.282
  19.3 0.1 maximum_maximum_fusion
  19.4 1.5 maximum_maximum_fusion.1.pack
  21.0 0.8 pad_maximum_fusion.pieces
  21.8 113.4 %front.1 = (bf16[4,256,1280]{2,1,0:T(8,128)(2,1)}, bf16[4,2,128,512]{3,2,1,0:T(8,128)(2,1)}, bf16[1280,512]{1,0:T(8,128)(2,1)}, f32[16,512]{1,0:T(8,128)}, bf16[...) custom-call(bf16[2,64,1280]{2,1,0:T(8,128)(2,1)} %tokens.1, ...), custom_call_target="tpu_custom_call" | custom-call | tf_op jit(solution)/shard_map/front/pallas_call | solution.py:701
  135.3 0.8 slice.69
  136.0 0.6 slice_reduce_fusion.2
  136.7 3.7 %multiply_reduce_fusion.3 = (f32[128]{0:T(128)S(1)}, f32[128,1280]{1,0:T(8,128)S(1)}) fusion(f32[1280]{0:T(1024)S(1)} %get-tuple-element.60, bf16[128,2048]{1,0:T(8,128)(2,1)} %get-tuple-element.31.attended, bf16[2048,1280]{1,0:T(8,128)(2,1)} %get-tuple-element.32, bf16[128,1280]{1,0:T(8,128)(2,1)S(1)} %bitcast.74), kind=kOutput, calls=%fused_computation.28 | convolution fusion | flops 671907712 | bytes 6755840 | tf_op jit(solution)/shard_map/dot_general | solution.py:47
  140.4 0.1 multiply_convert_fusion.1.normed_two
  140.6 0.7 multiply_convert_fusion
  141.3 1.4 copy-done.1
  142.8 1.2 convert_reduce_fusion.1
  144.1 1.4 fusion.5
  145.5 1.3 multiply_reduce_fusion
  146.8 1.1 convert_reduce_fusion.2
  147.9 2.6 convolution_convert_fusion.pack
  150.6 0.6 pad.9.vector_grads
  151.2 140.0 %rear.1 = (f32[128,1280]{1,0:T(8,128)}, bf16[8,32,512]{2,1,0:T(8,128)(2,1)}, f32[32,1280]{1,0:T(8,128)}) custom-call(bf16[128,2048]{1,0:T(8,128)(2,1)} %convolution_convert_fusion.pack, bf16[16,512,256]{2,1,0:T(8,128)(2,1)} %get-tuple-element.36.kv, bf16[4,512,128]{2,1,0:T(8,128)(2,1)} %get-tuple-element.37.queries, s32[4,1,512]{2,1,0:T(1,128)} %pad_add_fusion.starts, ...), custom_call_target="tpu_custom_call" | custom-call | tf_op jit(solution)/shard_map/rear/pallas_call | solution.py:1131
  291.3 1.3 fusion.10
  292.6 2.3 fusion.9
  294.9 1.7 fusion.21
  296.6 0.1 convert_element_type.103
  296.7 0.1 copy.41
  296.9 0.6 divide_multiply_fusion
  297.5 0.1 constant_dynamic-slice_fusion
  297.6 0.6 slice_bitcast_fusion.2
  298.2 0.1 fusion.22
  298.3 0.7 reshape.294
  299.0 0.7 reshape.293
  299.8 0.7 reshape.292
  (58 shorter events, 0.5 us)
Async XLA Ops:
  0.6 136.0 %copy-start = (bf16[2,64,1280]{2,1,0:T(8,128)(2,1)S(1)}, bf16[2,64,1280]{2,1,0:T(8,128)(2,1)}, u32[]{:S(2)}) copy-start(bf16[2,64,1280]{2,1,0:T(8,128)(2,1)} %tokens.1) | copy-start | bytes 983044
  136.7 3.9 %copy-start.2 = (bf16[1280,1280]{1,0:T(8,128)(2,1)S(1)}, bf16[1280,1280]{1,0:T(8,128)(2,1)}, u32[]{:S(2)}) copy-start(bf16[1280,1280]{1,0:T(8,128)(2,1)} %get-tuple-element.34) | copy-start | bytes 9830404
  140.6 3.5 %copy-start.6 = (bf16[128,1280]{1,0:T(8,128)(2,1)}, bf16[128,1280]{1,0:T(8,128)(2,1)S(1)}, u32[]{:S(2)}) copy-start(bf16[128,1280]{1,0:T(8,128)(2,1)S(1)} %multiply_convert_fusion.1.normed_two) | copy-start | bytes 983044
  140.6 2.2 copy-start.1
  140.6 2.2 copy-start.4
  141.3 2.7 copy-start.5
  144.1 2.7 copy-start.7
  144.1 3.8 %slice-start = ((s8[5242880]{0:T(1024)(128)(4,1)}), s8[4194304]{0:T(1024)(128)(4,1)S(1)}, s32[]{:S(2)}) async-start(s8[5242880]{0:T(1024)(128)(4,1)} %bitcast.72), calls=%async_computation | async-start | bytes 8388608
  145.5 2.4 slice-start.1
  147.9 3.3 %copy-start.3 = (bf16[128,1280]{1,0:T(8,128)(2,1)}, bf16[128,1280]{1,0:T(8,128)(2,1)S(1)}, u32[]{:S(2)}) copy-start(bf16[128,1280]{1,0:T(8,128)(2,1)S(1)} %get-tuple-element.62.d_branch) | copy-start | bytes 983044
  151.2 140.0 %copy-start.9 = (f32[1280]{0:T(1024)S(1)}, f32[1280]{0:T(1024)}, u32[]{:S(2)}) copy-start(f32[1280]{0:T(1024)} %get-tuple-element.56) | copy-start | bytes 15364
  151.2 141.3 %copy-start.10 = (f32[128]{0:T(128)S(1)}, f32[128]{0:T(128)}, u32[]{:S(2)}) copy-start(f32[128]{0:T(128)} %rsqrt.27) | copy-start | bytes 1540
  291.2 5.3 %copy-start.8 = (bf16[8,32,512]{2,1,0:T(8,128)(2,1)S(1)}, bf16[8,32,512]{2,1,0:T(8,128)(2,1)}, u32[]{:S(2)}) copy-start(bf16[8,32,512]{2,1,0:T(8,128)(2,1)} %get-tuple-element.44) | copy-start | bytes 786436
  291.2 5.7 %copy-start.11 = (f32[80]{0:T(128)S(1)}, f32[80]{0:T(128)}, u32[]{:S(2)}) copy-start(f32[80]{0:T(128)} %param.38) | copy-start | bytes 964

commit v2 on v1

--- a/solution.py
+++ b/solution.py
@@ -30,7 +30,8 @@
 f32 = jnp.float32
 bf16 = jnp.bfloat16
 
-PARTS = (((0, 640), "xyz"), ((640, 640), "xzy"))
+PARTS = (((0, 512), "xyz"), ((512, 384), "yzx"), ((896, 384), "zxy"))
+PARTS_BACK = (((0, 640), "xyz"), ((640, 640), "xzy"))
 
 
 def inverse_rms(values):
@@ -71,9 +72,17 @@
     return (z * 4 + (x % 2) * 2 + c, y * 2 + x // 2)
 
 
-def chunk_of(ref, place, cols, lead=()):
-    blk, head = device_at(place)
-    return ref.at[(*lead, blk, pl.ds(head * ROWS, ROWS), cols)]
+def span(place, free, core=True):
+    x, y, z = place["x"], place["y"], place["z"]
+    whole = slice(None)
+    at = [
+        whole if "z" in free else z,
+        whole if "x" in free else x % 2,
+        place["c"],
+        whole if "y" in free else y,
+        whole if "x" in free else x // 2,
+    ]
+    return tuple(at if core else at[:2] + at[3:])
 
 
 def moved(place, axis, value):
@@ -130,14 +139,13 @@
 
 
 def selections():
-    spread = np.zeros((288, 256), np.float32)
+    take = np.zeros((240, 256), np.float32)
     join = np.zeros((CHUNK, 256), np.float32)
     order = np.zeros((4 * GROUP, 4 * CHUNK), np.float32)
     for i in range(8):
         for j in range(10):
-            spread[32 + i * 10 + j, i * ROWS + j] = 1
-            spread[128 + i * 10 + j, i * ROWS + 10 + j] = 1
-            spread[208 + i * 10 + j, i * ROWS + 20 + j] = 1
+            for w in range(3):
+                take[w * GROUP + i * 10 + j, i * ROWS + w * 10 + j] = 1
             join[i * 10 + j, i * ROWS + j] = 1
             inner, x_high = i // 2, i % 2
             for y in range(4):
@@ -145,11 +153,11 @@
         for v in range(16):
             join[GROUP + v, i * ROWS + 16 + v] = 1
     share = join.T.copy()
-    return spread, join, share, order
-
-
-SPREAD, JOIN, SHARE, ORDER = selections()
-TAKE_T = np.stack([SPREAD[32:112].T, SPREAD[128:208].T, SPREAD[208:288].T])
+    return take, join, share, order
+
+
+TAKE, JOIN, SHARE, ORDER = selections()
+TAKE_T = TAKE.reshape(3, GROUP, 256).transpose(0, 2, 1)
 
 
 def row_block(ref, g, count):
@@ -163,92 +171,97 @@
         self.sibling = device_at(moved(place, "c", 1 - place["c"]))
 
     def begin(self, pack, sem):
-        own = pltpu.make_async_copy(
-            pack, chunk_of(self.buf, self.place, pl.ds(0, D)), sem
-        )
+        own = pltpu.make_async_copy(pack, self.buf.at[span(self.place, "")], sem)
         own.start()
         return own
 
-    def forward(self, part, axes, fixed, count):
+    def piece(self, part, where, free):
         first, width = PARTS[part][0]
-        cols = pl.ds(first, width)
-
-        @pl.loop(0, count)
-        def _(number):
-            where = dict(varied(self.place, axes, number), **fixed)
-            piece = chunk_of(self.buf, where, cols)
-            remote(
-                piece, piece, self.send.at[part, 3], self.recv.at[part, 5], self.sibling
-            ).start()
+        return self.buf.at[(*span(where, free), slice(None), pl.ds(first, width))]
+
+    def pieces(self, part, count):
+        cols = pl.ds(*PARTS[part][0])
+        whole = slice(None)
+        at = {
+            3: (pl.ds(0, 3), 0, 0, 0, 0),
+            12: (pl.ds(0, 3), 0, 0, whole, 0),
+            16: (0, whole, 0, whole, whole),
+            48: (pl.ds(0, 3), whole, 0, whole, whole),
+            64: (whole, whole, 0, whole, whole),
+        }[count]
+        return self.buf.at[(*at, whole, cols)]
+
+    def forward(self, part, where, free):
+        piece = self.piece(part, where, free)
+        remote(piece, piece, self.send.at[part, 3], self.recv.at[part, 5], self.sibling).start()
 
     def stage(self, stage):
-        for part, ((first, width), order) in enumerate(PARTS):
-            cols = pl.ds(first, width)
+        for part, (_, order) in enumerate(PARTS):
             if stage:
-                wait_bytes(
-                    self.buf.at[0, pl.ds(0, 3 * 4 ** (stage - 1) * ROWS), cols]
-                    if stage == 1
-                    else self.buf.at[pl.ds(0, 3), pl.ds(0, 4 * ROWS), cols],
-                    self.recv.at[part, stage - 1],
-                )
-
-            @pl.loop(0, 4**stage)
-            def _(number, part=part, cols=cols, order=order):
-                piece = chunk_of(self.buf, varied(self.place, order[:stage], number), cols)
-                axis = order[stage]
-                for step in (1, 3, 2):
-                    target = moved(self.place, axis, (self.place[axis] + step) % 4)
-                    slot = stage if stage < 2 else 1 + step
-                    remote(
-                        piece,
-                        piece,
-                        self.send.at[part, stage],
-                        self.recv.at[part, slot],
-                        device_at(target),
-                    ).start()
-
+                wait_bytes(self.pieces(part, 3 * 4 ** (stage - 1)), self.recv.at[part, stage - 1])
+            piece = self.piece(part, self.place, order[:stage])
+            axis = order[stage]
+            for step in (1, 3, 2) if stage < 2 else (1, 3):
+                target = moved(self.place, axis, (self.place[axis] + step) % 4)
+                slot = stage if stage < 2 else 1 + step
+                remote(
+                    piece,
+                    piece,
+                    self.send.at[part, stage],
+                    self.recv.at[part, slot],
+                    device_at(target),
+                ).start()
         for part, (_, order) in enumerate(PARTS):
             if stage == 0:
-                self.forward(part, "", {}, 1)
+                self.forward(part, self.place, "")
             else:
                 axis = order[stage - 1]
                 for step in (1, 3, 2):
-                    self.forward(
-                        part,
-                        order[: stage - 1],
-                        {axis: (self.place[axis] + 4 - step) % 4},
-                        4 ** (stage - 1),
-                    )
+                    there = moved(self.place, axis, (self.place[axis] + 4 - step) % 4)
+                    self.forward(part, there, order[: stage - 1])
+
+    def relay(self):
+        for part, ((first, width), order) in enumerate(PARTS):
+            axis, halved = order[2], order[1]
+            here = self.place[axis]
+            for step in (1, 3):
+                wait_bytes(self.pieces(part, 16), self.recv.at[part, 1 + step])
+                there = moved(self.place, axis, (here + 4 - step) % 4)
+                at = list(span(there, order[:2]))
+                half = step // 2
+                if halved == "x":
+                    at[4] = half
+                else:
+                    at[0 if halved == "z" else 3] = pl.ds(half * 2, 2)
+                piece = self.buf.at[(*at, slice(None), pl.ds(first, width))]
+                target = device_at(moved(self.place, axis, (here + step) % 4))
+                remote(
+                    piece, piece, self.send.at[part, 2], self.recv.at[part, 3], target
+                ).start()
+                self.forward(part, there, order[:2])
 
     def finish(self):
-        for step in (1, 3, 2):
-            for part, ((first, width), order) in enumerate(PARTS):
-                wait_bytes(
-                    self.buf.at[pl.ds(0, 2), :, pl.ds(first, width)],
-                    self.recv.at[part, 1 + step],
-                )
-                axis = order[2]
-                self.forward(
-                    part, order[:2], {axis: (self.place[axis] + 4 - step) % 4}, 16
-                )
-        for part, ((first, width), order) in enumerate(PARTS):
-            cols = pl.ds(first, width)
-            half = self.buf.at[pl.ds(0, 8), :, cols]
-            wait_bytes(half, self.recv.at[part, 5])
-            wait_bytes(half, self.send.at[part, 3])
-            wait_bytes(self.buf.at[0, pl.ds(0, 3 * ROWS), cols], self.send.at[part, 0])
-            wait_bytes(
-                self.buf.at[pl.ds(0, 3), pl.ds(0, 4 * ROWS), cols], self.send.at[part, 1]
-            )
-            wait_bytes(self.buf.at[pl.ds(0, 6), :, cols], self.send.at[part, 2])
+        for part, (_, order) in enumerate(PARTS):
+            wait_bytes(self.pieces(part, 16), self.recv.at[part, 3])
+            axis = order[2]
+            there = moved(self.place, axis, (self.place[axis] + 2) % 4)
+            self.forward(part, there, order[:2])
+        for part in range(3):
+            wait_bytes(self.pieces(part, 64), self.recv.at[part, 5])
+            wait_bytes(self.pieces(part, 64), self.send.at[part, 3])
+            wait_bytes(self.pieces(part, 3), self.send.at[part, 0])
+            wait_bytes(self.pieces(part, 12), self.send.at[part, 1])
+            wait_bytes(self.pieces(part, 48), self.send.at[part, 2])
 
 
 VMEM = pl.BlockSpec(memory_space=pltpu.VMEM)
 HBM = pl.BlockSpec(memory_space=pl.ANY)
 
 
-def unpack(buf, staged, spread, out_w, hidden_w, proj_w, out_sem):
+def unpack(buf, staged, take, out_w, hidden_w, proj_w, out_sem):
     spans = ((0, 128, out_w), (128, GROUP, hidden_w), (208, GROUP, proj_w))
+    staged[:, 0:32] = jnp.zeros((2, 32, D), bf16)
+    staged[:, 112:128] = jnp.zeros((2, 16, D), bf16)
 
     @pl.loop(0, 16)
     def _(g):
@@ -265,7 +278,9 @@
             for out in outs:
                 out.wait()
 
-        staged[slot] = nn(spread[...], buf[g]).astype(bf16)
+        rows = nn(take[...], buf[g // 4, (g // 2) % 2, g % 2].reshape(256, D)).astype(bf16)
+        staged[slot, 32:112] = rows[0:80]
+        staged[slot, 128:288] = rows[80:240]
         for out in outs:
             out.start()
 
@@ -284,99 +299,98 @@
         self.sibling = device_at(moved(place, "c", 1 - place["c"]))
 
     def swap(self, number):
+        at = (number // 2, number % 2)
+        sems = (len(PARTS_BACK), number)
         return remote(
-            self.away.at[number],
-            self.pair.at[number],
-            self.send.at[len(PARTS), number],
-            self.recv.at[len(PARTS), number],
-            self.sibling,
+            self.away.at[at], self.pair.at[at], self.send.at[sems], self.recv.at[sems], self.sibling
         )
 
     def add_pair(self, number):
         self.swap(number).wait()
-        self.mine[number] = (
-            self.mine[number].astype(f32) + self.pair[number].astype(f32)
-        ).astype(bf16)
-
-    def own_piece(self, where, cols):
-        half = where["z"] * 2 + where["x"] % 2
-        return self.mine.at[half, pl.ds((where["y"] * 2 + where["x"] // 2) * ROWS, ROWS), cols]
+        at = (number // 2, number % 2)
+        self.mine[at] = (self.mine[at].astype(f32) + self.pair[at].astype(f32)).astype(bf16)
+
+    def source(self, part, stage, where):
+        (first, width), order = PARTS_BACK[part]
+        if stage == 0:
+            at = span(where, order[:2], core=False)
+            return self.mine.at[(*at, slice(None), pl.ds(first, width))]
+        at = [
+            slice(None) if axis in order[: 2 - stage] else value
+            for axis, value in zip("zxyx", span(where, "", core=False))
+            if axis in order[: 3 - stage]
+        ]
+        return self.halves[stage - 1][part].at[tuple(at)]
 
     def start(self, stage):
-        for part, ((first, width), order) in enumerate(PARTS):
-            cols = pl.ds(first, width)
+        for part, (_, order) in enumerate(PARTS_BACK):
             axis = order[2 - stage]
-            rest = order[: 2 - stage]
-
-            @pl.loop(0, 16 // 4**stage)
-            def _(number, part=part, cols=cols, axis=axis, rest=rest):
-                for step in (1, 3, 2):
-                    target = moved(self.place, axis, (self.place[axis] + step) % 4)
-                    if stage == 0:
-                        source = self.own_piece(varied(target, rest, number), cols)
-                    elif stage == 1:
-                        source = self.halves[0].at[target[axis], number, :, cols]
-                    else:
-                        source = self.halves[1].at[target[axis], :, cols]
-                    remote(
-                        source,
-                        self.lands[stage].at[step - 1, number, :, cols],
-                        self.send.at[part, stage],
-                        self.recv.at[part, stage],
-                        device_at(target),
-                    ).start()
+            for step in (1, 3, 2):
+                target = moved(self.place, axis, (self.place[axis] + step) % 4)
+                remote(
+                    self.source(part, stage, target),
+                    self.lands[stage][part].at[step - 1],
+                    self.send.at[part, stage],
+                    self.recv.at[part, stage],
+                    device_at(target),
+                ).start()
 
     def add(self, stage, out=None):
-        for part, ((first, width), order) in enumerate(PARTS):
-            cols = pl.ds(first, width)
-            axis = order[2 - stage]
-            rest = order[: 2 - stage]
-            wait_bytes(self.lands[stage].at[:, :, :, cols], self.recv.at[part, stage])
-
-            @pl.loop(0, 16 // 4**stage)
-            def _(number, cols=cols, axis=axis, rest=rest):
-                if stage == 0:
-                    total = self.own_piece(varied(self.place, rest, number), cols)[...]
-                elif stage == 1:
-                    total = self.halves[0][self.place[axis], number, :, cols]
+        for part, ((first, width), order) in enumerate(PARTS_BACK):
+            land = self.lands[stage][part]
+            wait_bytes(land, self.recv.at[part, stage])
+            own = self.source(part, stage, self.place)
+            lead = land.shape[1:-2]
+
+            @pl.loop(0, math.prod(lead))
+            def _(number):
+                at = []
+                for size in reversed(lead):
+                    at.insert(0, number % size)
+                    number = number // size
+                at = tuple(at)
+                total = own[at].astype(f32)
+                for source in range(3):
+                    total = total + land[(source, *at)].astype(f32)
+                if stage < 2:
+                    self.halves[stage][part][at] = total.astype(bf16)
                 else:
-                    total = self.halves[1][self.place[axis], :, cols]
-                total = total.astype(f32)
-                for source in range(3):
-                    total = total + self.lands[stage][source, number, :, cols].astype(f32)
-                if stage == 0:
-                    self.halves[0][number // 4, number % 4, :, cols] = total.astype(bf16)
-                elif stage == 1:
-                    self.halves[1][number, :, cols] = total.astype(bf16)
-                else:
-                    out[:, cols] = total
+                    out[:, first : first + width] = total
 
     def finish(self):
         for stage in range(3):
-            for part, ((first, width), order) in enumerate(PARTS):
-                wait_bytes(
-                    self.lands[stage].at[:, :, :, pl.ds(first, width)], self.send.at[part, stage]
-                )
+            for part in range(len(PARTS_BACK)):
+                wait_bytes(self.lands[stage][part], self.send.at[part, stage])
+
+
+def lead_of(axes):
+    sizes = {"z": (4,), "x": (2, 2), "y": (4,)}
+    if axes == {"x", "y"}:
+        return (2, 4, 2)
+    if axes == {"x", "z"}:
+        return (4, 2, 2)
+    return sum((sizes[axis] for axis in "zyx" if axis in axes), ())
 
 
 def scatter_scratch():
-    return [
-        pltpu.VMEM((8, 256, D), bf16),
-        pltpu.VMEM((8, 256, D), bf16),
-        pltpu.VMEM((8, 256, D), bf16),
-        pltpu.VMEM((3, 16, ROWS, D), bf16),
-        pltpu.VMEM((3, 4, ROWS, D), bf16),
-        pltpu.VMEM((3, 1, ROWS, D), bf16),
-        pltpu.VMEM((4, 4, ROWS, D), bf16),
-        pltpu.VMEM((4, ROWS, D), bf16),
-        pltpu.SemaphoreType.DMA((3, 8)),
-        pltpu.SemaphoreType.DMA((3, 8)),
-    ]
+    whole = pltpu.VMEM((4, 2, 4, 2, ROWS, D), bf16)
+    lands, halves = [], []
+    for stage in range(3):
+        for (_, width), order in PARTS_BACK:
+            lead = lead_of(set(order[: 2 - stage]))
+            lands.append(pltpu.VMEM((3, *lead, ROWS, width), bf16))
+            if stage < 2:
+                halves.append(pltpu.VMEM((*lead, ROWS, width), bf16))
+    semaphores = [pltpu.SemaphoreType.DMA((3, 8))] * 2
+    return [whole] * 3 + lands + halves + semaphores
 
 
 def scatter_of(scratch, place):
-    away, mine, pair, l0, l1, l2, h0, h1, send, recv = scratch
-    return Scatter(away, mine, pair, (l0, l1, l2), (h0, h1), send, recv, place)
+    away, mine, pair = scratch[:3]
+    parts = len(PARTS_BACK)
+    lands = [scratch[3 + parts * stage : 3 + parts * (stage + 1)] for stage in range(3)]
+    halves = [scratch[3 + parts * stage : 3 + parts * (stage + 1)] for stage in (3, 4)]
+    return Scatter(away, mine, pair, lands, halves, scratch[-2], scratch[-1], place)
 
 
 HALVES = ((0, "yz"), (256, "zy"))
@@ -408,28 +422,30 @@
     return ((micro * 2 + (h % 8) // 4) * 4 + quarter, (h % 4) * 2 + h // 8)
 
 
+def column_pieces(buf, half, place, free):
+    at = [slice(None) if axis in free else place[axis] for axis in "zy"]
+    return buf.at[(*at, slice(None), pl.ds(HALVES[half][0], 256))]
+
+
 def gather_columns(buf, send, recv, place, stage):
     for half, (first, order) in enumerate(HALVES):
-        cols = pl.ds(first, 256)
         axis = order[stage]
         if stage:
-            wait_bytes(buf.at[0, pl.ds(0, 3 * CHUNK), cols], recv.at[half, 0])
-        for number in range(4**stage):
-            where = varied(place, order[:stage], number)
-            piece = buf.at[where["z"], pl.ds(where["y"] * CHUNK, CHUNK), cols]
-            for step in (1, 3, 2):
-                target = moved(place, axis, (place[axis] + step) % 4)
-                remote(
-                    piece, piece, send.at[half, stage], recv.at[half, stage], device_at(target)
-                ).start()
+            wait_bytes(buf.at[0, pl.ds(0, 3), :, pl.ds(first, 256)], recv.at[half, 0])
+        piece = column_pieces(buf, half, place, order[:stage])
+        for step in (1, 3, 2):
+            target = moved(place, axis, (place[axis] + step) % 4)
+            remote(
+                piece, piece, send.at[half, stage], recv.at[half, stage], device_at(target)
+            ).start()
 
 
 def finish_columns(buf, send, recv):
     for half, (first, _) in enumerate(HALVES):
         cols = pl.ds(first, 256)
-        wait_bytes(buf.at[pl.ds(0, 3), :, cols], recv.at[half, 1])
-        wait_bytes(buf.at[0, pl.ds(0, 3 * CHUNK), cols], send.at[half, 0])
-        wait_bytes(buf.at[pl.ds(0, 3), :, cols], send.at[half, 1])
+        wait_bytes(buf.at[pl.ds(0, 3), :, :, cols], recv.at[half, 1])
+        wait_bytes(buf.at[0, pl.ds(0, 3), :, cols], send.at[half, 0])
+        wait_bytes(buf.at[pl.ds(0, 3), :, :, cols], send.at[half, 1])
 
 
 def quarter_of(blk):
@@ -439,11 +455,6 @@
 
 def query_block(quarter, j):
     return j * 4 + jnp.where(j % 2 == 0, quarter, 3 - quarter)
-
-
-def chip_block(x_low, n):
-    z = n // 2
-    return z * 4 + 2 * ((z + x_low) % 2) + n % 2
 
 
 def cell_of(ref, pair, width):
@@ -489,8 +500,8 @@
 
 
 def front_kernel(
-    tokens, pieces, pack, scale_row, starts, join, order, spread,
-    normed_out, packed_out, wide_w, vectors, kv_out, queries, out_t, log_norms, attended,
+    tokens, pieces, pack, scale_row, segments, join, order, take,
+    normed_out, packed_out, wide_w, vectors, starts, kv_out, queries, out_t, log_norms, attended,
     out_w, hidden_w, proj_w,
     ring_tokens, ring_pieces, chunks, kv, value_t, tops, totals, rounded, landed, buf, staged,
     x_tok_send, x_tok_recv, c_tok_send, c_tok_recv, piece_send, piece_recv, col_send, col_recv,
@@ -507,7 +518,6 @@
     pair = (place["z"] // 2) * H + head_of(place)
     turn = place["x"] * 2 + core
     sibling = (blk + 1 - 2 * core, head)
-    partner = (blk + 2 - 4 * x_low, head)
     two = Gather(buf, two_send, two_recv, place)
     own = two.begin(pack, own_sem.at[0])
     own_tokens = pltpu.make_async_copy(tokens, tokens_of(ring_tokens, place), own_sem.at[1])
@@ -532,9 +542,17 @@
     remote(tokens, mine, c_tok_send, c_tok_recv, sibling).start()
     own.wait()
     two.stage(0)
+    ids = segments[place["z"] // 2]
+    before = [jnp.sum((ids < value).astype(jnp.int32)) for value in range(1, 9)]
+    for j in range(4):
+        row = segments[place["z"] // 2, pl.ds(query_block(quarter, j), 1)]
+        start = jnp.zeros_like(row)
+        for value in range(1, 9):
+            start = jnp.where(row == value, before[value - 1], start)
+        starts[j] = start
     wait_bytes(ring_pieces, piece_recv)
     joined = nn(join[...], ring_pieces[...].reshape(256, MINE)).astype(bf16)
-    chunks[place["z"], pl.ds(pl.multiple_of(place["y"] * CHUNK, 32), CHUNK)] = joined
+    chunks[place["z"], place["y"]] = joined
     gather_columns(chunks, col_send, col_recv, place, 0)
     gather_columns(chunks, col_send, col_recv, place, 1)
     for step in (1, 3, 2):
@@ -546,10 +564,9 @@
     finish_columns(chunks, col_send, col_recv)
     vector_rows = jnp.zeros((16, MINE), f32)
     for z in range(4):
-        wide_w[z * 4 * GROUP : (z + 1) * 4 * GROUP] = nn(order[...], chunks[z]).astype(bf16)
+        wide_w[z * 4 * GROUP : (z + 1) * 4 * GROUP] = nn(order[...], chunks[z].reshape(4 * CHUNK, MINE)).astype(bf16)
         for y in range(4):
-            at = y * CHUNK + GROUP
-            vector_rows = vector_rows + chunks[z, at : at + 16].astype(f32)
+            vector_rows = vector_rows + chunks[z, y, GROUP:].astype(f32)
     vectors[...] = vector_rows
     bias = vector_rows[0:1]
     gain = jnp.concatenate([vector_rows[1:2], vector_rows[2:3], vector_rows[3:4, :256]], axis=1)
@@ -558,16 +575,9 @@
     )
     wait_bytes(ring_tokens.at[pl.ds(0, 2)], c_tok_recv)
 
-    @pl.loop(0, 4)
-    def _(inner):
-        values = ring_tokens[inner].reshape(256, D).astype(f32)
-        normed = (values * inverse_rms(values) * gain).astype(bf16)
-        normed_out[inner] = normed
-        full = nn(normed, wide_w[...])
-        packed = ((full + bias) * scale_row[0:1] + one_lane).astype(bf16)
-        packed_out[inner] = packed.reshape(2, 128, MINE)
+    def deliver(inner, aside, send, recv):
         block = place["z"] * 4 + inner
-        to_quarter = quarter_of(block)
+        to_quarter = (quarter_of(block) + aside) % 4
         for m in range(2):
             for h in range(2):
                 blk_to, head_to = pair_device(m * H + turn * 2 + h, to_quarter)
@@ -583,6 +593,20 @@
                 def _():
                     remote(src, dst, send, recv, (blk_to, head_to)).start()
 
+    @pl.loop(0, 4)
+    def _(inner):
+        values = ring_tokens[inner].reshape(256, D).astype(f32)
+        normed = (values * inverse_rms(values) * gain).astype(bf16)
+        normed_out[inner] = normed.reshape(4, 2, ROWS, D)
+        full = nn(normed, wide_w[...])
+        packed = ((full + bias) * scale_row[0:1] + one_lane).astype(bf16)
+        packed_out[inner] = packed.reshape(2, 128, MINE)
+        deliver(inner, 0, send, recv)
+
+    @pl.loop(0, 4)
+    def _(inner):
+        deliver(inner, 2, x_send, x_recv)
+
     two.stage(1)
     wait_bytes(kv.at[pl.ds(0, 4)], recv)
 
@@ -590,7 +614,12 @@
     def _(j):
         block = kv.at[query_block(quarter, j)]
         remote(block, block, core_send, core_recv, sibling).start()
-        remote(block, block, x_send, x_recv, partner).start()
+
+    def turn_values(of_quarter):
+        @pl.loop(0, 4)
+        def _(j):
+            b = query_block(of_quarter, j)
+            value_t[b] = kv[b, :, 128:].T
 
     pick = shift_matrix(LANES, 128, HD)
 
@@ -601,14 +630,7 @@
         totals[j] = jnp.zeros((1, B), f32)
         out_t[j] = jnp.zeros((128, B), f32)
 
-    wait_bytes(kv.at[pl.ds(0, 4)], core_recv)
-
-    @pl.loop(0, 8)
-    def _(n):
-        b = chip_block(x_low, n)
-        value_t[b] = kv[b, :, 128:].T
-
-    two.stage(2)
+    turn_values(quarter)
 
     def step(j, block, key_block):
         def tile(masked):
@@ -627,39 +649,49 @@
         pl.when(masked)(lambda: tile(True))
         pl.when(jnp.logical_not(masked))(lambda: tile(False))
 
+    def key_pass(j, of_quarter, count):
+        block = query_block(quarter, j)
+
+        @pl.loop(0, count)
+        def _(n):
+            step(j, block, query_block(of_quarter, n))
+
     @pl.loop(0, 4)
     def _(j):
-        block = query_block(quarter, j)
-
-        @pl.loop(0, 2 * j + block % 2 + 1)
-        def _(n):
-            step(j, block, chip_block(x_low, n))
-
-    wait_bytes(kv.at[pl.ds(0, 4)], x_recv)
+        key_pass(j, quarter, j + 1)
+
+    two.stage(2)
+    wait_bytes(kv.at[pl.ds(0, 4)], core_recv)
+    beside = quarter + 1 - 2 * core
+    turn_values(beside)
 
     @pl.loop(0, 4)
     def _(j):
-        block = kv.at[query_block((quarter + 2) % 4, j)]
+        key_pass(j, beside, j + query_block(quarter, j) % 2)
+
+    wait_bytes(kv.at[pl.ds(0, 4)], x_recv)
+    across = (quarter + 2) % 4
+    for_sibling = [kv.at[query_block(across, j)] for j in range(4)]
+    for block in for_sibling:
         remote(block, block, pass_send, pass_recv, sibling).start()
-
+    turn_values(across)
+
+    @pl.loop(0, 4)
+    def _(j):
+        key_pass(j, across, j + (j + x_low) % 2)
+
+    two.relay()
     wait_bytes(kv.at[pl.ds(0, 4)], pass_recv)
     keep = pltpu.make_async_copy(kv, kv_out, kv_sem)
     keep.start()
-
-    @pl.loop(0, 8)
-    def _(n):
-        b = chip_block(1 - x_low, n)
-        value_t[b] = kv[b, :, 128:].T
+    across_beside = across + 1 - 2 * core
+    turn_values(across_beside)
 
     @pl.loop(0, 4)
     def _(i):
         j = 3 - i
         block = query_block(quarter, j)
-
-        @pl.loop(0, 2 * j + 2 * ((j + x_low) % 2))
-        def _(n):
-            step(j, block, chip_block(1 - x_low, n))
-
+        key_pass(j, across_beside, j + (j + x_low) % 2)
         acc = out_t[j]
         result = acc / acc[112:113]
         out_t[j] = result
@@ -682,11 +714,11 @@
                 remote(src, dst, back_send, back_recv, (block, h)).start()
 
     two.finish()
-    unpack(buf, staged, spread, out_w, hidden_w, proj_w, out_sem)
+    unpack(buf, staged, take, out_w, hidden_w, proj_w, out_sem)
     wait_bytes(landed, back_recv)
     attended[...] = landed[...]
     keep.wait()
-    for sem in (core_send, x_send, pass_send):
+    for sem in (core_send, pass_send):
         wait_bytes(kv.at[pl.ds(0, 4)], sem)
     wait_cells(landed, back_send, even, 128)
     wait_bytes(ring_pieces.at[pl.ds(0, 7)], piece_send)
@@ -694,6 +726,7 @@
         wait_bytes(tokens, x_tok_send.at[step_at])
     wait_bytes(ring_tokens.at[pl.ds(0, 2)], c_tok_send)
     wait_ring(kv, send, place)
+    wait_ring(kv, x_send, place)
 
 
 def front(*operands):
@@ -701,10 +734,11 @@
     return pl.pallas_call(
         front_kernel,
         out_shape=(
-            jax.ShapeDtypeStruct((4, 256, D), bf16),
+            jax.ShapeDtypeStruct((4, 4, 2, ROWS, D), bf16),
             jax.ShapeDtypeStruct((4, 2, 128, MINE), bf16),
             jax.ShapeDtypeStruct((D, MINE), bf16),
             jax.ShapeDtypeStruct((16, MINE), f32),
+            jax.ShapeDtypeStruct((4, 1, B), jnp.int32),
             jax.ShapeDtypeStruct((16, B, LANES), bf16),
             jax.ShapeDtypeStruct((4, B, 128), bf16),
             jax.ShapeDtypeStruct((4, 128, B), f32),
@@ -715,21 +749,21 @@
             jax.ShapeDtypeStruct((D, D), bf16),
         ),
         in_specs=[VMEM] * 8,
-        out_specs=(VMEM, VMEM, VMEM, VMEM, HBM, VMEM, VMEM, VMEM, VMEM, HBM, HBM, HBM),
+        out_specs=(VMEM,) * 5 + (HBM,) + (VMEM,) * 4 + (HBM,) * 3,
         scratch_shapes=[
             pltpu.VMEM((4, 2, 128, D), bf16),
             pltpu.VMEM((8, ROWS, MINE), bf16),
-            pltpu.VMEM((4, 4 * CHUNK, MINE), bf16),
+            pltpu.VMEM((4, 4, CHUNK, MINE), bf16),
             pltpu.VMEM((16, B, LANES), bf16),
             pltpu.VMEM((16, 128, B), bf16),
             pltpu.VMEM((4, 1, B), f32),
             pltpu.VMEM((4, 1, B), f32),
             pltpu.VMEM((4, B, 128), bf16),
             pltpu.VMEM((2 * TOK, OUT_WIDE), bf16),
-            pltpu.VMEM((16, 256, D), bf16),
+            pltpu.VMEM((4, 2, 2, 4, 2, ROWS, D), bf16),
             pltpu.VMEM((2, 288, D), bf16),
             dma((3,)), dma((3,)), dma, dma, dma, dma, dma((2, 2)), dma((2, 2)),
-            dma((2, 4)), dma((2, 6)), dma((2,)),
+            dma((3, 4)), dma((3, 6)), dma((2,)),
         ]
         + [dma] * 11
         + [dma((3, 2))],
@@ -741,18 +775,18 @@
         *operands,
         jnp.asarray(JOIN, bf16),
         jnp.asarray(ORDER, bf16),
-        jnp.asarray(SPREAD, bf16),
+        jnp.asarray(TAKE, bf16),
     )
 
 
 def rear_kernel(
     pack, kv, queries, starts, out_t, log_norms,
     attended, d_branch, normed_two, d_pre, activated, upstream,
-    normed, packed, wide_w, vectors, vector_grads, scale_row, take_t, share, order_t,
+    normed, packed, wide_w, vector_grads, scale_row, take_t, share, order_t,
     d_normed, pieces_out, two_out,
     d_out, key_t, deltas, d_query, d_kv, mine_kv, half, half_in, cross, cross_in, final, d_wide,
     attended_t, normed_two_t, activated_t, right,
-    partial_in, sum_in, grad_chunks, first_in, second_in, first_y, first_z,
+    partial_in, sum_in, grad_chunks, first_in, second_in, first_sum,
     joined, shares, shares_in,
     send, recv, core_send, core_recv, x_send, x_recv, back_send, back_recv,
     normed_sem, c_send, c_recv, sum_send, sum_recv, col_send, col_recv, share_send, share_recv,
@@ -811,7 +845,8 @@
         )
         for cell in range(5):
             lanes = slice(cell * LANES, (cell + 1) * LANES)
-            into[number, :, lanes] = nn(left, right[:, lanes]).astype(bf16)
+            block = nn(left, right[:, lanes]).astype(bf16)
+            into[number // 2, number % 2, :, :, :, lanes] = block.reshape(4, 2, ROWS, LANES)
 
     @pl.loop(0, 8)
     def _(number):
@@ -826,13 +861,7 @@
     def _(b):
         key_t[b] = kv[b, :, :128].T
 
-    @pl.loop(0, 8)
-    def _(number):
-        two.add_pair(number)
-
-    load_normed = pltpu.make_async_copy(normed, two.pair.at[pl.ds(0, 4)], normed_sem)
-    load_normed.start()
-    two.start(0)
+    load_normed = pltpu.make_async_copy(normed, two.pair.at[:, 0], normed_sem)
     wait_bytes(d_out, recv)
 
     @pl.loop(0, 4)
@@ -841,7 +870,6 @@
         d_query[j] = jnp.zeros((128, B), f32)
 
     sibling = (blk + 1 - 2 * core, head)
-    partner = (blk + 2 - 4 * x_low, head)
 
     def step(j, block, key_block):
         def tile(masked):
@@ -865,40 +893,38 @@
             half.at[n], half_in.at[n], core_send.at[n], core_recv.at[n], sibling
         )
 
+    shift = shift_matrix(128, LANES, -HD)
+
+    partner = (blk + 2 - 4 * x_low, head)
+
     def cross_swap(z):
         return remote(cross.at[z], cross_in.at[z], x_send.at[z], x_recv.at[z], partner)
 
-    def own_number(z):
-        return 2 * z + (x_low + z) % 2
-
     def core_sum(z):
-        own = own_number(z)
+        own = 2 * z + (x_low + z) % 2
         other = 4 * z + 1 - own
         swap(other).wait()
         cross[z] = (mine_kv[other] + half_in[other].astype(f32)).astype(bf16)
         cross_swap(z).start()
         swap(own).wait()
-        mine_kv[own] = mine_kv[own] + half_in[own].astype(f32)
-
-    shift = shift_matrix(128, LANES, -HD)
+        mine_kv[own] = (
+            mine_kv[own]
+            + half_in[own].astype(f32)
+            + nn(d_query[z].T.astype(bf16), shift)
+        )
 
     def finish(z):
-        block = query_block(quarter, z)
         cross_swap(z).wait()
-        final[z] = (
-            mine_kv[own_number(z)]
-            + cross_in[z].astype(f32)
-            + nn(d_query[z].T.astype(bf16), shift)
-        ).astype(bf16)
+        own = 2 * z + (x_low + z) % 2
+        final[z] = (mine_kv[own] + cross_in[z].astype(f32)).astype(bf16)
+        inner = query_block(quarter, z) % 4
+        dst = d_wide.at[inner, place["z"] // 2, :, pl.ds((my_head % 2) * LANES, LANES)]
 
         @pl.loop(0, 4)
         def _(k):
             y = (place["y"] + k) % 4
             there = {"x": my_head // 4, "y": y, "z": z, "c": (my_head // 2) % 2}
             src = final.at[z, pl.ds(y * 128, 128)]
-            dst = d_wide.at[
-                block % 4, place["z"] // 2, :, pl.ds((my_head % 2) * LANES, LANES)
-            ]
             blk_to, head_to = device_at(there)
             stays = (blk_to == blk) & (head_to == head)
 
@@ -942,29 +968,27 @@
         def _():
             finish(z - 1)
 
-        @pl.when(part == 4)
+        @pl.when(part == 0)
         def _():
-            two.add(0)
-            two.start(1)
-
-        @pl.when(part == 6)
-        def _():
-            two.add(1)
-            two.start(2)
+            @pl.loop(0, 8)
+            def _(number):
+                two.add_pair(number)
+
+            load_normed.start()
+            two.start(0)
 
     core_sum(3)
-    two.add(2, two_out)
+    two.add(0)
+    two.start(1)
     finish(3)
-    two.finish()
     wait_bytes(d_wide, back_recv)
 
     load_normed.wait()
-    partial, normed_here = two.away, two.pair
+    partial, normed_here = two.away.at[:, 0], two.pair.at[:, 0]
+    summed = two.away.at[:, 1]
     scale = scale_row[0:1]
-    gain = jnp.concatenate([vectors[1:2], vectors[2:3], vectors[3:4, :256]], axis=1)
     bias_sum = jnp.zeros((1, MINE), f32)
     scale_sum = jnp.zeros((1, MINE), f32)
-    gain_sum = jnp.zeros((1, D), f32)
     for inner in range(4):
         grad = d_wide[inner].reshape(256, MINE).astype(f32)
         scale_sum = scale_sum + jnp.sum(
@@ -973,120 +997,94 @@
         grad = (grad * scale).astype(bf16)
         d_wide[inner] = grad.reshape(2, 128, MINE)
         bias_sum = bias_sum + jnp.sum(grad.astype(f32), axis=0, keepdims=True)
-        back = nt(grad, wide_w[...])
-        gain_sum = gain_sum + jnp.sum(
-            back * normed_here[inner].astype(f32), axis=0, keepdims=True
-        )
-        partial[inner] = back.astype(bf16)
-    sibling_at = (blk + 1 - 2 * core, head)
-    c_swaps = []
-    for low in range(2):
-        c_swaps.append(
-            remote(
-                partial.at[low * 2 + 1 - core],
-                partial_in.at[low],
-                c_send.at[low],
-                c_recv.at[low],
-                sibling_at,
-            )
-        )
-        c_swaps[-1].start()
-    gain_sum = gain_sum / gain
     scale_sum = scale_sum[:, :LANES] + scale_sum[:, LANES:]
     rows = vector_grads[...] + jnp.concatenate(
-        [
-            bias_sum,
-            gain_sum[:, :512],
-            gain_sum[:, 512:1024],
-            jnp.concatenate([gain_sum[:, 1024:], scale_sum], axis=1),
-            jnp.zeros((12, MINE), f32),
-        ],
+        [bias_sum, jnp.concatenate([scale_sum, scale_sum], axis=1), jnp.zeros((14, MINE), f32)],
         axis=0,
     )
     rows = rows.astype(bf16)
     for z in range(4):
         left = jnp.concatenate(
-            [normed_here[inner, :, z * 320 // 128 * 128 : z * 320 // 128 * 128 + 384]
+            [normed_here[inner, :, :, :, z * 320 // 128 * 128 : z * 320 // 128 * 128 + 384].reshape(256, 384)
              for inner in range(4)],
             axis=0,
         )
         skip = z * 320 % 128
         grads = tn(left, d_wide[...].reshape(1024, MINE))[skip : skip + 320].astype(bf16)
-        grad_chunks[z] = nn(order_t[...], grads).astype(bf16)
+        grad_chunks[z] = nn(order_t[...], grads).astype(bf16).reshape(4, CHUNK, MINE)
         for y in range(4):
-            grad_chunks[z, y * CHUNK + GROUP : y * CHUNK + GROUP + 16] = rows
-
-    def chunk_rows(y):
-        return pl.ds(pl.multiple_of(y * CHUNK, 32), CHUNK)
+            grad_chunks[z, y, GROUP:] = rows
 
     for step_at in (1, 3, 2):
-        z = (place["z"] + step_at) % 4
+        for half, axis in enumerate("zy"):
+            there = moved(place, axis, (place[axis] + step_at) % 4)
+            remote(
+                column_pieces(grad_chunks, half, there, "y" if half == 0 else "z"),
+                first_in.at[half, step_at - 1],
+                col_send.at[half, 0],
+                col_recv.at[half, 0],
+                device_at(there),
+            ).start()
+    sibling_at = (blk + 1 - 2 * core, head)
+    c_swaps = [
         remote(
-            grad_chunks.at[z, :, pl.ds(0, 256)],
-            first_in.at[0, step_at - 1],
-            col_send.at[0, 0],
-            col_recv.at[0, 0],
-            device_at(moved(place, "z", z)),
-        ).start()
-        y = (place["y"] + step_at) % 4
-        for plane in range(4):
-            remote(
-                grad_chunks.at[plane, chunk_rows(y), pl.ds(256, 256)],
-                first_in.at[1, step_at - 1, chunk_rows(plane)],
-                col_send.at[1, 0],
-                col_recv.at[1, 0],
-                device_at(moved(place, "y", y)),
-            ).start()
+            partial.at[low * 2 + 1 - core],
+            partial_in.at[low],
+            c_send.at[low],
+            c_recv.at[low],
+            sibling_at,
+        )
+        for low in range(2)
+    ]
+    for number in range(4):
+        inner = (number % 2) * 2 + (1 - core if number < 2 else core)
+        back = nt(d_wide[inner].reshape(256, MINE), wide_w[...])
+        partial[inner] = back.astype(bf16).reshape(4, 2, ROWS, D)
+        if number < 2:
+            c_swaps[number].start()
     for low in range(2):
         c_swaps[low].wait()
-        partial[4 + low] = (
+        summed[low] = (
             partial[low * 2 + core].astype(f32) + partial_in[low].astype(f32)
         ).astype(bf16)
     for step_at in (1, 3, 2):
         there = moved(place, "x", (place["x"] + step_at) % 4)
         for m in range(2):
             remote(
-                partial.at[4 + there["x"] % 2, pl.ds(m * 128 + (there["x"] // 2) * TOK, TOK)],
-                sum_in.at[step_at - 1, pl.ds(m * TOK, TOK)],
+                summed.at[there["x"] % 2, m * 2 + there["x"] // 2],
+                sum_in.at[step_at - 1, m],
                 sum_send,
                 sum_recv,
                 device_at(there),
             ).start()
-    wait_bytes(first_in.at[0], col_recv.at[0, 0])
-    total = grad_chunks[place["z"], :, 0:256].astype(f32)
-    for source in range(3):
-        total = total + first_in[0, source].astype(f32)
-    first_y[...] = total.astype(bf16)
-    wait_bytes(first_in.at[1], col_recv.at[1, 0])
-    for plane in range(4):
-        total = grad_chunks[plane, chunk_rows(place["y"]), 256:512].astype(f32)
+    two.add(1)
+    two.start(2)
+    for half in range(2):
+        wait_bytes(first_in.at[half], col_recv.at[half, 0])
+        own = column_pieces(grad_chunks, half, place, "y" if half == 0 else "z")
+        for number in range(4):
+            total = own[number].astype(f32)
+            for source in range(3):
+                total = total + first_in[half, source, number].astype(f32)
+            first_sum[half, number] = total.astype(bf16)
+    for step_at in (1, 3, 2):
+        for half, axis in enumerate("yz"):
+            there = moved(place, axis, (place[axis] + step_at) % 4)
+            remote(
+                first_sum.at[half, there[axis]],
+                second_in.at[half, step_at - 1],
+                col_send.at[half, 1],
+                col_recv.at[half, 1],
+                device_at(there),
+            ).start()
+    totals = []
+    for half, axis in enumerate("yz"):
+        wait_bytes(second_in.at[half], col_recv.at[half, 1])
+        total = first_sum[half, place[axis]].astype(f32)
         for source in range(3):
-            total = total + first_in[1, source, chunk_rows(plane)].astype(f32)
-        first_z[plane] = total.astype(bf16)
-    for step_at in (1, 3, 2):
-        y = (place["y"] + step_at) % 4
-        remote(
-            first_y.at[chunk_rows(y)],
-            second_in.at[0, step_at - 1],
-            col_send.at[0, 1],
-            col_recv.at[0, 1],
-            device_at(moved(place, "y", y)),
-        ).start()
-        z = (place["z"] + step_at) % 4
-        remote(
-            first_z.at[z],
-            second_in.at[1, step_at - 1],
-            col_send.at[1, 1],
-            col_recv.at[1, 1],
-            device_at(moved(place, "z", z)),
-        ).start()
-    wait_bytes(second_in.at[0], col_recv.at[0, 1])
-    wait_bytes(second_in.at[1], col_recv.at[1, 1])
-    total_y = first_y[chunk_rows(place["y"])].astype(f32)
-    total_z = first_z[place["z"]].astype(f32)
-    for source in range(3):
-        total_y = total_y + second_in[0, source].astype(f32)
-        total_z = total_z + second_in[1, source].astype(f32)
+            total = total + second_in[half, source].astype(f32)
+        totals.append(total)
+    total_y, total_z = totals
     joined[:, 0:256] = total_y.astype(bf16)
     joined[:, 256:512] = total_z.astype(bf16)
     shares[...] = nn(share[...], joined[...]).astype(bf16).reshape(8, ROWS, MINE)
@@ -1102,23 +1100,18 @@
     pltpu.make_async_copy(
         shares.at[ring_number(place)], shares_in.at[turn], share_recv
     ).start()
+    two.add(2, two_out)
+    two.finish()
     wait_bytes(sum_in, sum_recv)
     for m in range(2):
-        at = pl.multiple_of(m * 128 + (place["x"] // 2) * TOK, TOK)
-        total = partial[4 + x_low, pl.ds(at, TOK)].astype(f32)
+        total = summed[x_low, m * 2 + place["x"] // 2].astype(f32)
         for source in range(3):
-            total = total + sum_in[source, m * TOK : (m + 1) * TOK].astype(f32)
-        d_normed[m * TOK : (m + 1) * TOK] = total
+            total = total + sum_in[source, m].astype(f32)
+        d_normed[m * TOK : (m + 1) * TOK] = total.reshape(TOK, D)
     wait_bytes(shares_in, share_recv)
     pieces_out[...] = shares_in[...]
     wait_cells(pack, send, even, 128)
-    wait_bytes(final.at[pl.ds(0, 3)], back_send)
-    wait_bytes(final.at[0, pl.ds(0, 384)], back_send)
-
-    @pl.when(jnp.logical_not(stays_here(place)))
-    def _():
-        wait_bytes(final.at[0, pl.ds(0, 128)], back_send)
-
+    wait_ring(final, back_send, place)
     wait_bytes(sum_in, sum_send)
     for number in range(2):
         wait_bytes(first_in.at[number], col_send.at[number, 0])
@@ -1135,7 +1128,7 @@
             jax.ShapeDtypeStruct((8, ROWS, MINE), bf16),
             jax.ShapeDtypeStruct((ROWS, D), f32),
         ),
-        in_specs=[VMEM] * 12 + [HBM] + [VMEM] * 8,
+        in_specs=[VMEM] * 12 + [HBM] + [VMEM] * 7,
         out_specs=(VMEM, VMEM, VMEM),
         scratch_shapes=[
             pltpu.VMEM((4, B, 128), bf16),
@@ -1154,13 +1147,12 @@
             pltpu.VMEM((D, 128), bf16),
             pltpu.VMEM((D, 128), bf16),
             pltpu.VMEM((384, D), bf16),
-            pltpu.VMEM((2, 256, D), bf16),
-            pltpu.VMEM((3, 2 * TOK, D), bf16),
-            pltpu.VMEM((4, 4 * CHUNK, MINE), bf16),
-            pltpu.VMEM((2, 3, 4 * CHUNK, 256), bf16),
+            pltpu.VMEM((2, 4, 2, ROWS, D), bf16),
+            pltpu.VMEM((3, 2, 2, ROWS, D), bf16),
+            pltpu.VMEM((4, 4, CHUNK, MINE), bf16),
+            pltpu.VMEM((2, 3, 4, CHUNK, 256), bf16),
             pltpu.VMEM((2, 3, CHUNK, 256), bf16),
-            pltpu.VMEM((4 * CHUNK, 256), bf16),
-            pltpu.VMEM((4, CHUNK, 256), bf16),
+            pltpu.VMEM((2, 4, CHUNK, 256), bf16),
             pltpu.VMEM((CHUNK, MINE), bf16),
             pltpu.VMEM((8, ROWS, MINE), bf16),
             pltpu.VMEM((8, ROWS, MINE), bf16),
@@ -1232,20 +1224,10 @@
     )
     scale_row = jnp.broadcast_to(scale_row, (8, MINE))
 
-    micro = blk // 8
-    segment_row = lax.dynamic_index_in_dim(segment_ids, micro, 0, keepdims=False)
-    starts = jnp.zeros_like(segment_row)
-    for value in range(1, 9):
-        before = jnp.sum((segment_row < value).astype(jnp.int32))
-        starts = jnp.where(segment_row == value, before, starts)
-    quarter = blk % 4
-    starts = starts.reshape(16, 1, B)
-    starts = jnp.stack([starts[query_block(quarter, j)] for j in range(4)])
-
     (
-        ring_normed, packed, wide_w, vectors, kv, queries, out_t, log_norms, attended,
+        ring_normed, packed, wide_w, vectors, starts, kv, queries, out_t, log_norms, attended,
         out_w, hidden_w, proj_w,
-    ) = front(inputs, pieces, pack, scale_row, starts)
+    ) = front(inputs, pieces, pack, scale_row, segment_ids.reshape(2, 16, B))
     every = vectors[1:].reshape(5, 3 * MINE)[:, :D]
     gain_one, out_b, gain_two, hidden_b, proj_b = [every[i] for i in range(5)]
 
@@ -1282,7 +1264,7 @@
     d_normed, shares, two = rear(
         d_attended, kv, queries, starts, out_t, log_norms,
         attended, d_branch, normed_two, d_pre, activated, upstream_low,
-        ring_normed, packed, wide_w, vectors, vector_grads, scale_row,
+        ring_normed, packed, wide_w, vector_grads, scale_row,
     )
     inverse_one = inverse_rms(tokens)
     input_grad = (
@@ -1299,13 +1281,17 @@
         lax.dynamic_slice(by_head, (blk, i * HD + head * 10), (1, 10)).reshape(10) for i in (1, 2)
     ]
     summed = jnp.sum(shares[:, 17:], axis=0)
-    scale_grad = summed[2, LANES + HD : LANES + 2 * HD] / softplus_scale
+    scale_grad = summed[0, HD : 2 * HD] / softplus_scale
     scale_grad = scale_grad * (LOG2E / math.sqrt(HD)) * jax.nn.sigmoid(dim_scale)
     natural = lax.dynamic_slice(summed.reshape(5, 3 * MINE), (0, at), (5, 10))
+    norm1_gain_grad = sum(
+        jnp.sum(w.astype(f32) * grad, axis=1)
+        for w, grad in ((w_query, d_query_w), (w_key, d_key_w), (w_value, d_value_w))
+    ) / norm1_gain.astype(f32)
     return (
         layer_out.reshape(2, TOK, D),
         input_grad.reshape(2, TOK, D),
-        natural[0],
+        norm1_gain_grad,
         d_query_w,
         d_key_w,
         d_value_w,

time: 304 us -> 285 us (0.938); the launches traced: 300 us -> 285 us
  other arithmetic: 19.5 us -> 11.7 us
  Pallas kernels: 253 us -> 246 us
    pallas_call x1, Pallas kernels: 113 us -> 104 us  [front(): pl.pallas_call(front_kernel, out_shape=(jax.ShapeDtypeStruct((4, 4, 2, RO...]
    select_n x1 -> x0, other arithmetic: 6.17 us -> none  [on_device(): starts = jnp.where(segment_row == value, before, starts)]
where the time goes in v2:
time: 285 us
  Pallas kernels  246 us (86%)
  local copies, waits for them, and re-layouts  15.1 us (5%)
  other arithmetic  11.7 us (4%)
  matrix products  11 us (4%)
    pallas_call x1, Pallas kernels, rear(): pl.pallas_call(rear_kernel, out_shape=(jax.ShapeDtypeStruct((2 * TOK, D),...  142 us
    pallas_call x1, Pallas kernels, front(): pl.pallas_call(front_kernel, out_shape=(jax.ShapeDtypeStruct((4, 4, 2, RO...  104 us
    dot_general x3, matrix products, nn(): lax.dot_general(a, b, (((1,), (0,)), ((), ())), preferred_element_type=f32)  5.81 us

profile of v2, /device:TPU:97, one launch (start us, length us, event | category | flops | bytes accessed | tf_op | source)
XLA Modules:
  0.0 284.8 jit_solution(7087630261582036977)
XLA Ops:
  0.7 0.7 fusion.11
  1.4 0.1 pad.17.clone
  1.5 0.1 pad.19.clone
  1.5 0.1 pad.25.clone
  1.6 0.1 concatenate.15
  1.7 1.1 multiply_reduce_fusion.1
  2.8 0.6 rsqrt.27
  3.5 0.7 stack.38
  4.2 1.0 convert_reduce_fusion
  5.3 0.9 dynamic_update_slice.9
  6.2 0.9 dynamic_update_slice.10
  7.0 0.6 broadcast_in_dim.44.scale_row
  7.7 0.2 dynamic_update_slice.11
  7.9 0.9 reshape.139
  8.8 0.9 reshape.138
  9.7 0.9 reshape.140
  10.6 0.1 maximum_maximum_fusion
  10.7 1.5 copy.46
  12.2 1.5 maximum_maximum_fusion.1.pack
  13.8 0.8 pad_maximum_fusion.pieces
  14.6 104.3 %front.1 = (bf16[4,4,2,32,1280]{4,3,2,1,0:T(8,128)(2,1)}, bf16[4,2,128,512]{3,2,1,0:T(8,128)(2,1)}, bf16[1280,512]{1,0:T(8,128)(2,1)}, f32[16,512]{1,0:T(8,128)}...) custom-call(bf16[2,64,1280]{2,1,0:T(8,128)(2,1)} %tokens.1, ...), custom_call_target="tpu_custom_call" | custom-call | tf_op jit(solution)/shard_map/front/pallas_call | solution.py:734
  118.9 0.8 slice.66
  119.7 0.6 slice_reduce_fusion.2
  120.3 3.7 %multiply_reduce_fusion.3 = (f32[128]{0:T(128)S(1)}, f32[128,1280]{1,0:T(8,128)S(1)}) fusion(f32[1280]{0:T(1024)S(1)} %get-tuple-element.54, bf16[128,2048]{1,0:T(8,128)(2,1)} %get-tuple-element.32.attended, bf16[2048,1280]{1,0:T(8,128)(2,1)} %get-tuple-element.33, bf16[128,1280]{1,0:T(8,128)(2,1)S(1)} %bitcast.75), kind=kOutput, calls=%fused_computation.28 | convolution fusion | flops 671907712 | bytes 6755840 | tf_op jit(solution)/shard_map/dot_general | solution.py:48
  124.1 0.1 multiply_convert_fusion.1.normed_two
  124.2 0.7 multiply_convert_fusion
  124.9 1.4 copy-done.1
  126.4 1.3 convert_reduce_fusion.1
  127.7 1.4 fusion.5
  129.1 1.3 multiply_reduce_fusion
  130.4 1.1 convert_reduce_fusion.2
  131.5 2.6 convolution_convert_fusion.pack
  134.2 0.6 pad.9.vector_grads
  134.8 141.6 %rear.1 = (f32[128,1280]{1,0:T(8,128)}, bf16[8,32,512]{2,1,0:T(8,128)(2,1)}, f32[32,1280]{1,0:T(8,128)}) custom-call(bf16[128,2048]{1,0:T(8,128)(2,1)} %convolution_convert_fusion.pack, bf16[16,512,256]{2,1,0:T(8,128)(2,1)} %get-tuple-element.37.kv, bf16[4,512,128]{2,1,0:T(8,128)(2,1)} %get-tuple-element.38.queries, s32[4,1,512]{2,1,0:T(1,128)} %get-tuple-element.39.starts, ...), custom_call_target="tpu_custom_call" | custom-call | tf_op jit(solution)/shard_map/rear/pallas_call | solution.py:1124
  276.5 1.3 fusion.10
  277.9 2.3 fusion.9
  280.2 1.7 fusion.13
  282.0 0.1 copy.41
  282.2 0.6 divide_multiply_fusion
  282.8 0.1 constant_dynamic-slice_fusion
  282.9 0.6 slice_bitcast_fusion.2
  283.5 0.1 fusion.14
  283.6 0.1 reshape.151
  283.7 0.1 reshape.152
  283.8 0.1 multiply_reduce_fusion.4
  284.0 0.1 reshape.150
  284.1 0.1 multiply_reduce_fusion.6
  284.2 0.5 convert_divide_fusion
  (72 shorter events, 0.6 us)
Async XLA Ops:
  0.6 119.6 %copy-start = (bf16[2,64,1280]{2,1,0:T(8,128)(2,1)S(1)}, bf16[2,64,1280]{2,1,0:T(8,128)(2,1)}, u32[]{:S(2)}) copy-start(bf16[2,64,1280]{2,1,0:T(8,128)(2,1)} %tokens.1) | copy-start | bytes 983044
  120.3 3.9 %copy-start.2 = (bf16[1280,1280]{1,0:T(8,128)(2,1)S(1)}, bf16[1280,1280]{1,0:T(8,128)(2,1)}, u32[]{:S(2)}) copy-start(bf16[1280,1280]{1,0:T(8,128)(2,1)} %get-tuple-element.35) | copy-start | bytes 9830404
  124.2 3.5 %copy-start.6 = (bf16[128,1280]{1,0:T(8,128)(2,1)}, bf16[128,1280]{1,0:T(8,128)(2,1)S(1)}, u32[]{:S(2)}) copy-start(bf16[128,1280]{1,0:T(8,128)(2,1)S(1)} %multiply_convert_fusion.1.normed_two) | copy-start | bytes 983044
  124.2 2.2 copy-start.1
  124.2 2.2 copy-start.4
  124.9 2.7 copy-start.5
  127.7 2.7 copy-start.7
  127.7 3.8 %slice-start = ((s8[5242880]{0:T(1024)(128)(4,1)}), s8[4194304]{0:T(1024)(128)(4,1)S(1)}, s32[]{:S(2)}) async-start(s8[5242880]{0:T(1024)(128)(4,1)} %bitcast.73), calls=%async_computation | async-start | bytes 8388608
  129.1 2.5 slice-start.1
  131.5 3.3 %copy-start.3 = (bf16[128,1280]{1,0:T(8,128)(2,1)}, bf16[128,1280]{1,0:T(8,128)(2,1)S(1)}, u32[]{:S(2)}) copy-start(bf16[128,1280]{1,0:T(8,128)(2,1)S(1)} %get-tuple-element.56.d_branch) | copy-start | bytes 983044
  134.8 141.6 %copy-start.15 = (f32[1280]{0:T(1024)S(1)}, f32[1280]{0:T(1024)}, u32[]{:S(2)}) copy-start(f32[1280]{0:T(1024)} %get-tuple-element.50) | copy-start | bytes 15364
  134.8 143.0 %copy-start.17 = (f32[128]{0:T(128)S(1)}, f32[128]{0:T(128)}, u32[]{:S(2)}) copy-start(f32[128]{0:T(128)} %rsqrt.27) | copy-start | bytes 1540
  276.5 5.4 %copy-start.11 = (bf16[8,32,512]{2,1,0:T(8,128)(2,1)S(1)}, bf16[8,32,512]{2,1,0:T(8,128)(2,1)}, u32[]{:S(2)}) copy-start(bf16[8,32,512]{2,1,0:T(8,128)(2,1)} %get-tuple-element.46) | copy-start | bytes 786436
  276.5 5.7 %copy-start.18 = (f32[80]{0:T(128)S(1)}, f32[80]{0:T(128)}, u32[]{:S(2)}) copy-start(f32[80]{0:T(128)} %param.38) | copy-start | bytes 964
  276.5 7.3 %copy-start.13 = (bf16[10,1280]{1,0:T(8,128)(2,1)S(1)}, bf16[10,1280]{1,0:T(8,128)(2,1)}, u32[]{:S(2)}) copy-start(bf16[10,1280]{1,0:T(8,128)(2,1)} %param.28) | copy-start | bytes 76804
  276.5 7.3 %copy-start.14 = (bf16[10,1280]{1,0:T(8,128)(2,1)S(1)}, bf16[10,1280]{1,0:T(8,128)(2,1)}, u32[]{:S(2)}) copy-start(bf16[10,1280]{1,0:T(8,128)(2,1)} %param.27) | copy-start | bytes 76804
  277.8 6.3 %copy-start.12 = (bf16[10,1280]{1,0:T(8,128)(2,1)S(1)}, bf16[10,1280]{1,0:T(8,128)(2,1)}, u32[]{:S(2)}) copy-start(bf16[10,1280]{1,0:T(8,128)(2,1)} %param.26) | copy-start | bytes 76804
  277.8 6.4 %copy-start.16 = (bf16[10]{0:T(256)(128)(2,1)S(1)}, bf16[10]{0:T(256)(128)(2,1)}, u32[]{:S(2)}) copy-start(bf16[10]{0:T(256)(128)(2,1)} %param.25) | copy-start | bytes 64
  283.7 1.1 copy-start.9
  283.8 0.9 copy-start.10
  284.1 0.7 copy-start.8

commit v3 on v2

--- a/solution.py
+++ b/solution.py
@@ -31,7 +31,7 @@
 bf16 = jnp.bfloat16
 
 PARTS = (((0, 512), "xyz"), ((512, 384), "yzx"), ((896, 384), "zxy"))
-PARTS_BACK = (((0, 640), "xyz"), ((640, 640), "xzy"))
+PARTS_BACK = (((0, 512), "xyz"), ((512, 512), "xzy"), ((1024, 256), "yzx"))
 
 
 def inverse_rms(values):
@@ -381,7 +381,7 @@
             lands.append(pltpu.VMEM((3, *lead, ROWS, width), bf16))
             if stage < 2:
                 halves.append(pltpu.VMEM((*lead, ROWS, width), bf16))
-    semaphores = [pltpu.SemaphoreType.DMA((3, 8))] * 2
+    semaphores = [pltpu.SemaphoreType.DMA((4, 8))] * 2
     return [whole] * 3 + lands + halves + semaphores
 
 
@@ -501,9 +501,9 @@
 
 def front_kernel(
     tokens, pieces, pack, scale_row, segments, join, order, take,
-    normed_out, packed_out, wide_w, vectors, starts, kv_out, queries, out_t, log_norms, attended,
+    normed_hbm, packed_hbm, wide_hbm, vectors, starts, kv_out, queries, out_t, log_norms, attended,
     out_w, hidden_w, proj_w,
-    ring_tokens, ring_pieces, chunks, kv, value_t, tops, totals, rounded, landed, buf, staged,
+    normed_out, normed_t, packed_out, wide_w, keep_sems, ring_tokens, ring_pieces, chunks, kv, value_t, tops, totals, rounded, landed, buf, staged,
     x_tok_send, x_tok_recv, c_tok_send, c_tok_recv, piece_send, piece_recv, col_send, col_recv,
     two_send, two_recv, own_sem, send, recv, core_send, core_recv, x_send, x_recv,
     pass_send, pass_recv, back_send, back_recv, kv_sem, out_sem,
@@ -562,9 +562,14 @@
         remote(arrived, arrived, c_tok_send, c_tok_recv, sibling).start()
     own_tokens.wait()
     finish_columns(chunks, col_send, col_recv)
+
+    @pl.loop(0, 4)
+    def _(z):
+        rows = pl.ds(pl.multiple_of(z * 4 * GROUP, 64), 4 * GROUP)
+        wide_w[rows] = nn(order[...], chunks[z].reshape(4 * CHUNK, MINE)).astype(bf16)
+
     vector_rows = jnp.zeros((16, MINE), f32)
     for z in range(4):
-        wide_w[z * 4 * GROUP : (z + 1) * 4 * GROUP] = nn(order[...], chunks[z].reshape(4 * CHUNK, MINE)).astype(bf16)
         for y in range(4):
             vector_rows = vector_rows + chunks[z, y, GROUP:].astype(f32)
     vectors[...] = vector_rows
@@ -597,7 +602,7 @@
     def _(inner):
         values = ring_tokens[inner].reshape(256, D).astype(f32)
         normed = (values * inverse_rms(values) * gain).astype(bf16)
-        normed_out[inner] = normed.reshape(4, 2, ROWS, D)
+        normed_out[inner] = normed
         full = nn(normed, wide_w[...])
         packed = ((full + bias) * scale_row[0:1] + one_lane).astype(bf16)
         packed_out[inner] = packed.reshape(2, 128, MINE)
@@ -608,18 +613,28 @@
         deliver(inner, 2, x_send, x_recv)
 
     two.stage(1)
+
+    @pl.loop(0, 4)
+    def _(inner):
+        @pl.loop(0, D // 128)
+        def _(n):
+            lanes = pl.ds(pl.multiple_of(n * 128, 128), 128)
+            normed_t[inner, lanes] = normed_out[inner, :, lanes].T
+
+    keeps = [
+        pltpu.make_async_copy(ref, out, keep_sems.at[i])
+        for i, (ref, out) in enumerate(
+            ((normed_t, normed_hbm), (packed_out, packed_hbm), (wide_w, wide_hbm))
+        )
+    ]
+    for keep in keeps:
+        keep.start()
     wait_bytes(kv.at[pl.ds(0, 4)], recv)
 
     @pl.loop(0, 4)
     def _(j):
         block = kv.at[query_block(quarter, j)]
         remote(block, block, core_send, core_recv, sibling).start()
-
-    def turn_values(of_quarter):
-        @pl.loop(0, 4)
-        def _(j):
-            b = query_block(of_quarter, j)
-            value_t[b] = kv[b, :, 128:].T
 
     pick = shift_matrix(LANES, 128, HD)
 
@@ -630,68 +645,49 @@
         totals[j] = jnp.zeros((1, B), f32)
         out_t[j] = jnp.zeros((128, B), f32)
 
-    turn_values(quarter)
-
-    def step(j, block, key_block):
-        def tile(masked):
-            s = nt(kv[key_block, :, :128], queries[j])
-            if masked:
-                s = jnp.where(mask_of(key_block, block, starts[j]), s, NEGATIVE)
+
+    def step(j, block, key_blocks):
+        def tiles(masked):
+            scores = []
+            for key_block in key_blocks:
+                s = nt(kv[key_block, :, :128], queries[j])
+                if masked:
+                    s = jnp.where(mask_of(key_block, block, starts[j]), s, NEGATIVE)
+                scores.append(s)
             top = tops[j]
-            new_top = jnp.maximum(top, jnp.max(s, axis=0, keepdims=True))
-            p = jnp.exp(s - new_top)
+            new_top = top
+            for s in scores:
+                new_top = jnp.maximum(new_top, jnp.max(s, axis=0, keepdims=True))
             scale = jnp.exp(top - new_top)
+            total = totals[j] * scale
+            acc = out_t[j] * scale
+            for key_block, s in zip(key_blocks, scores):
+                p = jnp.exp(s - new_top)
+                total = total + jnp.sum(p, axis=0, keepdims=True)
+                acc = acc + nn(value_t[key_block], p.astype(bf16))
             tops[j] = new_top
-            totals[j] = totals[j] * scale + jnp.sum(p, axis=0, keepdims=True)
-            out_t[j] = out_t[j] * scale + nn(value_t[key_block], p.astype(bf16))
-
-        masked = has_mask(key_block, block)
-        pl.when(masked)(lambda: tile(True))
-        pl.when(jnp.logical_not(masked))(lambda: tile(False))
+            totals[j] = total
+            out_t[j] = acc
+
+        masked = has_mask(key_blocks[0], block)
+        for key_block in key_blocks[1:]:
+            masked = masked | has_mask(key_block, block)
+        pl.when(masked)(lambda: tiles(True))
+        pl.when(jnp.logical_not(masked))(lambda: tiles(False))
 
     def key_pass(j, of_quarter, count):
         block = query_block(quarter, j)
 
-        @pl.loop(0, count)
+        @pl.loop(0, count // 2)
         def _(n):
-            step(j, block, query_block(of_quarter, n))
-
-    @pl.loop(0, 4)
-    def _(j):
-        key_pass(j, quarter, j + 1)
-
-    two.stage(2)
-    wait_bytes(kv.at[pl.ds(0, 4)], core_recv)
-    beside = quarter + 1 - 2 * core
-    turn_values(beside)
-
-    @pl.loop(0, 4)
-    def _(j):
-        key_pass(j, beside, j + query_block(quarter, j) % 2)
-
-    wait_bytes(kv.at[pl.ds(0, 4)], x_recv)
-    across = (quarter + 2) % 4
-    for_sibling = [kv.at[query_block(across, j)] for j in range(4)]
-    for block in for_sibling:
-        remote(block, block, pass_send, pass_recv, sibling).start()
-    turn_values(across)
-
-    @pl.loop(0, 4)
-    def _(j):
-        key_pass(j, across, j + (j + x_low) % 2)
-
-    two.relay()
-    wait_bytes(kv.at[pl.ds(0, 4)], pass_recv)
-    keep = pltpu.make_async_copy(kv, kv_out, kv_sem)
-    keep.start()
-    across_beside = across + 1 - 2 * core
-    turn_values(across_beside)
-
-    @pl.loop(0, 4)
-    def _(i):
-        j = 3 - i
-        block = query_block(quarter, j)
-        key_pass(j, across_beside, j + (j + x_low) % 2)
+            last = count - 1 - 2 * n
+            step(j, block, (query_block(of_quarter, last), query_block(of_quarter, last - 1)))
+
+        @pl.when(count % 2 == 1)
+        def _():
+            step(j, block, (query_block(of_quarter, 0),))
+
+    def give(j, block):
         acc = out_t[j]
         result = acc / acc[112:113]
         out_t[j] = result
@@ -713,11 +709,53 @@
             def _():
                 remote(src, dst, back_send, back_recv, (block, h)).start()
 
+    keep_kv = pltpu.make_async_copy(kv, kv_out, kv_sem)
+
+    @pl.loop(0, 4)
+    def _(turn_at):
+        of_quarter = (quarter + 2 * (turn_at // 2)) % 4 + (turn_at % 2) * (1 - 2 * core)
+
+        @pl.when(turn_at == 1)
+        def _():
+            two.stage(2)
+            wait_bytes(kv.at[pl.ds(0, 4)], core_recv)
+
+        @pl.when(turn_at == 2)
+        def _():
+            wait_bytes(kv.at[pl.ds(0, 4)], x_recv)
+
+            @pl.loop(0, 4)
+            def _(j):
+                block = kv.at[query_block(of_quarter, j)]
+                remote(block, block, pass_send, pass_recv, sibling).start()
+
+        @pl.when(turn_at == 3)
+        def _():
+            two.relay()
+            wait_bytes(kv.at[pl.ds(0, 4)], pass_recv)
+            keep_kv.start()
+
+        @pl.loop(0, 4)
+        def _(j):
+            b = query_block(of_quarter, j)
+            value_t[b] = kv[b, :, 128:].T
+
+        @pl.loop(0, 4)
+        def _(i):
+            j = 3 - i
+            block = query_block(quarter, j)
+            more = jnp.where(
+                turn_at == 0, 1, jnp.where(turn_at == 1, block % 2, (j + x_low) % 2)
+            )
+            key_pass(j, of_quarter, j + more)
+            pl.when(turn_at == 3)(lambda: give(j, block))
+
     two.finish()
     unpack(buf, staged, take, out_w, hidden_w, proj_w, out_sem)
     wait_bytes(landed, back_recv)
     attended[...] = landed[...]
-    keep.wait()
+    for keep in keeps + [keep_kv]:
+        keep.wait()
     for sem in (core_send, pass_send):
         wait_bytes(kv.at[pl.ds(0, 4)], sem)
     wait_cells(landed, back_send, even, 128)
@@ -734,7 +772,7 @@
     return pl.pallas_call(
         front_kernel,
         out_shape=(
-            jax.ShapeDtypeStruct((4, 4, 2, ROWS, D), bf16),
+            jax.ShapeDtypeStruct((4, D, 256), bf16),
             jax.ShapeDtypeStruct((4, 2, 128, MINE), bf16),
             jax.ShapeDtypeStruct((D, MINE), bf16),
             jax.ShapeDtypeStruct((16, MINE), f32),
@@ -749,8 +787,13 @@
             jax.ShapeDtypeStruct((D, D), bf16),
         ),
         in_specs=[VMEM] * 8,
-        out_specs=(VMEM,) * 5 + (HBM,) + (VMEM,) * 4 + (HBM,) * 3,
+        out_specs=(HBM,) * 3 + (VMEM,) * 2 + (HBM,) + (VMEM,) * 4 + (HBM,) * 3,
         scratch_shapes=[
+            pltpu.VMEM((4, 256, D), bf16),
+            pltpu.VMEM((4, D, 256), bf16),
+            pltpu.VMEM((4, 2, 128, MINE), bf16),
+            pltpu.VMEM((D, MINE), bf16),
+            dma((3,)),
             pltpu.VMEM((4, 2, 128, D), bf16),
             pltpu.VMEM((8, ROWS, MINE), bf16),
             pltpu.VMEM((4, 4, CHUNK, MINE), bf16),
@@ -780,16 +823,17 @@
 
 
 def rear_kernel(
-    pack, kv, queries, starts, out_t, log_norms,
+    pack, kv_hbm, queries, starts, out_t, log_norms,
     attended, d_branch, normed_two, d_pre, activated, upstream,
-    normed, packed, wide_w, vector_grads, scale_row, take_t, share, order_t,
+    normed_hbm, packed_hbm, wide_hbm, vector_grads, scale_row, take_t, share, order_t,
     d_normed, pieces_out, two_out,
+    kv, packed, wide_w, load_sems,
     d_out, key_t, deltas, d_query, d_kv, mine_kv, half, half_in, cross, cross_in, final, d_wide,
     attended_t, normed_two_t, activated_t, right,
-    partial_in, sum_in, grad_chunks, first_in, second_in, first_sum,
+    sum_in, grad_chunks, first_in, second_in, first_sum,
     joined, shares, shares_in,
     send, recv, core_send, core_recv, x_send, x_recv, back_send, back_recv,
-    normed_sem, c_send, c_recv, sum_send, sum_recv, col_send, col_recv, share_send, share_recv,
+    c_send, c_recv, sum_send, sum_recv, col_send, col_recv, share_send, share_recv,
     *scratch,
 ):
     blk = lax.axis_index("blk")
@@ -803,6 +847,14 @@
     to_quarter = quarter_of(blk)
     even = (blk // 4) % 2 == 0
     two = scatter_of(scratch, place)
+    loads = [
+        pltpu.make_async_copy(src, dst, load_sems.at[i])
+        for i, (src, dst) in enumerate(
+            ((kv_hbm, kv), (packed_hbm, packed), (wide_hbm, wide_w))
+        )
+    ]
+    for load in loads:
+        load.start()
     greet_all()
 
     @pl.loop(0, PAIRS)
@@ -820,13 +872,18 @@
         def _():
             remote(src, dst, send, recv, pair_device(p, to_quarter)).start()
 
-    for n in range(D // 128):
-        lanes = slice(n * 128, n * 128 + 128)
+
+    @pl.loop(0, D // 128)
+    def _(n):
+        lanes = pl.ds(pl.multiple_of(n * 128, 128), 128)
         normed_two_t[lanes] = normed_two[:, lanes].T
         activated_t[lanes] = activated[:, lanes].T
-    for n in range(H):
-        lanes = slice(n * 128, n * 128 + 128)
+
+    @pl.loop(0, H)
+    def _(n):
+        lanes = pl.ds(pl.multiple_of(n * 128, 128), 128)
         attended_t[lanes] = attended[:, lanes].T
+
     right[0:128] = d_branch[...]
     right[128:256] = d_pre[...]
     right[256:384] = upstream[...]
@@ -857,11 +914,20 @@
     def _(number):
         produce(number, core, two.mine)
 
+    loads[0].wait()
+
+    def keys_at(block, lane):
+        return kv[pl.ds(pl.multiple_of(block * B, B), B), lane : lane + 128]
+
     @pl.loop(0, 16)
     def _(b):
-        key_t[b] = kv[b, :, :128].T
-
-    load_normed = pltpu.make_async_copy(normed, two.pair.at[:, 0], normed_sem)
+        key_t[b] = keys_at(b, 0).T
+
+    @pl.loop(0, 8)
+    def _(number):
+        two.add_pair(number)
+
+    two.start(0)
     wait_bytes(d_out, recv)
 
     @pl.loop(0, 4)
@@ -871,22 +937,28 @@
 
     sibling = (blk + 1 - 2 * core, head)
 
-    def step(j, block, key_block):
-        def tile(masked):
-            q = queries[j]
-            do = d_out[j]
-            p = jnp.exp(nt(kv[key_block, :, :128], q) - log_norms[j])
-            if masked:
-                p = jnp.where(mask_of(key_block, block, starts[j]), p, 0.0)
-            dp = nt(kv[key_block, :, 128:], do)
-            ds = (p * (dp - deltas[j])).astype(bf16)
-            d_kv[:, :128] += nn(ds, q)
-            d_kv[:, 128:] += nn(p.astype(bf16), do)
-            d_query[j] += nn(key_t[key_block], ds)
-
-        masked = has_mask(key_block, block)
-        pl.when(masked)(lambda: tile(True))
-        pl.when(jnp.logical_not(masked))(lambda: tile(False))
+    def step(numbers, key_block):
+        def tiles(masked):
+            found = []
+            for j in numbers:
+                q = queries[j]
+                do = d_out[j]
+                p = jnp.exp(nt(keys_at(key_block, 0), q) - log_norms[j])
+                if masked:
+                    allowed = mask_of(key_block, query_block(quarter, j), starts[j])
+                    p = jnp.where(allowed, p, 0.0)
+                dp = nt(keys_at(key_block, 128), do)
+                found.append((q, do, p.astype(bf16), (p * (dp - deltas[j])).astype(bf16)))
+            d_kv[:, :128] += sum(nn(ds, q) for q, do, p, ds in found)
+            d_kv[:, 128:] += sum(nn(p, do) for q, do, p, ds in found)
+            for j, (q, do, p, ds) in zip(numbers, found):
+                d_query[j] += nn(key_t[key_block], ds)
+
+        masked = has_mask(key_block, query_block(quarter, numbers[0]))
+        for j in numbers[1:]:
+            masked = masked | has_mask(key_block, query_block(quarter, j))
+        pl.when(masked)(lambda: tiles(True))
+        pl.when(jnp.logical_not(masked))(lambda: tiles(False))
 
     def swap(n):
         return remote(
@@ -936,29 +1008,45 @@
             def _():
                 remote(src, dst, back_send, back_recv, (blk_to, head_to)).start()
 
-    @pl.loop(0, 8)
+    load_normed = pltpu.make_async_copy(normed_hbm, kv.at[pl.ds(0, 4 * D)], load_sems.at[3])
+
+    def key_steps(key_block):
+        z = key_block // 4
+        d_kv[...] = jnp.zeros((B, LANES), f32)
+        first = z + (query_block(quarter, z) < key_block).astype(jnp.int32)
+
+        @pl.when(first % 2 == 1)
+        def _():
+            step((first,), key_block)
+
+        @pl.loop((first + 1) // 2, 2)
+        def _(n):
+            step((2 * n, 2 * n + 1), key_block)
+
+        n = 2 * z + (key_block % 4) // 2
+
+        @pl.when((key_block + z + core) % 2 == 0)
+        def _():
+            mine_kv[n] = d_kv[...]
+
+        @pl.when((key_block + z + core) % 2 == 1)
+        def _():
+            half[n] = d_kv[...].astype(bf16)
+            swap(n).start()
+
+    @pl.loop(0, 10)
     def _(part):
         z = part // 2
 
-        @pl.loop(2 * part, 2 * part + 2)
-        def _(key_block):
-            d_kv[...] = jnp.zeros((B, LANES), f32)
-            first = z + (query_block(quarter, z) < key_block).astype(jnp.int32)
-
-            @pl.loop(first, 4)
-            def _(j):
-                step(j, query_block(quarter, j), key_block)
-
-            n = 2 * z + (key_block % 4) // 2
-
-            @pl.when((key_block + z + core) % 2 == 0)
-            def _():
-                mine_kv[n] = d_kv[...]
-
-            @pl.when((key_block + z + core) % 2 == 1)
-            def _():
-                half[n] = d_kv[...].astype(bf16)
-                swap(n).start()
+        @pl.when(part < 8)
+        def _():
+            @pl.loop(2 * part, 2 * part + 2)
+            def _(key_block):
+                key_steps(key_block)
+
+        @pl.when(part == 8)
+        def _():
+            load_normed.start()
 
         @pl.when((part % 2 == 0) & (part > 0))
         def _():
@@ -968,63 +1056,41 @@
         def _():
             finish(z - 1)
 
-        @pl.when(part == 0)
+        @pl.when(part == 6)
         def _():
-            @pl.loop(0, 8)
-            def _(number):
-                two.add_pair(number)
-
-            load_normed.start()
-            two.start(0)
-
-    core_sum(3)
-    two.add(0)
-    two.start(1)
-    finish(3)
+            two.add(0)
+            two.start(1)
+
+    two.add(1)
+    two.start(2)
     wait_bytes(d_wide, back_recv)
 
+    for load in loads[1:]:
+        load.wait()
     load_normed.wait()
-    partial, normed_here = two.away.at[:, 0], two.pair.at[:, 0]
-    summed = two.away.at[:, 1]
+    partial = two.away.at[:, 0]
+    summed, partial_in = two.away.at[pl.ds(0, 2), 1], two.away.at[pl.ds(2, 2), 1]
     scale = scale_row[0:1]
     bias_sum = jnp.zeros((1, MINE), f32)
     scale_sum = jnp.zeros((1, MINE), f32)
-    for inner in range(4):
+
+    def scaled_grads(inner, sums):
+        bias_sum, scale_sum = sums
         grad = d_wide[inner].reshape(256, MINE).astype(f32)
         scale_sum = scale_sum + jnp.sum(
             grad * packed[inner].reshape(256, MINE).astype(f32), axis=0, keepdims=True
         )
         grad = (grad * scale).astype(bf16)
         d_wide[inner] = grad.reshape(2, 128, MINE)
-        bias_sum = bias_sum + jnp.sum(grad.astype(f32), axis=0, keepdims=True)
+        return bias_sum + jnp.sum(grad.astype(f32), axis=0, keepdims=True), scale_sum
+
+    bias_sum, scale_sum = lax.fori_loop(0, 4, scaled_grads, (bias_sum, scale_sum))
     scale_sum = scale_sum[:, :LANES] + scale_sum[:, LANES:]
     rows = vector_grads[...] + jnp.concatenate(
         [bias_sum, jnp.concatenate([scale_sum, scale_sum], axis=1), jnp.zeros((14, MINE), f32)],
         axis=0,
     )
     rows = rows.astype(bf16)
-    for z in range(4):
-        left = jnp.concatenate(
-            [normed_here[inner, :, :, :, z * 320 // 128 * 128 : z * 320 // 128 * 128 + 384].reshape(256, 384)
-             for inner in range(4)],
-            axis=0,
-        )
-        skip = z * 320 % 128
-        grads = tn(left, d_wide[...].reshape(1024, MINE))[skip : skip + 320].astype(bf16)
-        grad_chunks[z] = nn(order_t[...], grads).astype(bf16).reshape(4, CHUNK, MINE)
-        for y in range(4):
-            grad_chunks[z, y, GROUP:] = rows
-
-    for step_at in (1, 3, 2):
-        for half, axis in enumerate("zy"):
-            there = moved(place, axis, (place[axis] + step_at) % 4)
-            remote(
-                column_pieces(grad_chunks, half, there, "y" if half == 0 else "z"),
-                first_in.at[half, step_at - 1],
-                col_send.at[half, 0],
-                col_recv.at[half, 0],
-                device_at(there),
-            ).start()
     sibling_at = (blk + 1 - 2 * core, head)
     c_swaps = [
         remote(
@@ -1036,12 +1102,45 @@
         )
         for low in range(2)
     ]
-    for number in range(4):
-        inner = (number % 2) * 2 + (1 - core if number < 2 else core)
+
+    def token_grads(inner):
         back = nt(d_wide[inner].reshape(256, MINE), wide_w[...])
         partial[inner] = back.astype(bf16).reshape(4, 2, ROWS, D)
-        if number < 2:
-            c_swaps[number].start()
+
+    @pl.loop(0, 2)
+    def _(low):
+        token_grads(low * 2 + 1 - core)
+
+    for low in range(2):
+        c_swaps[low].start()
+
+    @pl.loop(0, 4)
+    def _(z):
+        def part(inner):
+            at = pl.ds(pl.multiple_of(inner * D + z * 320, 64), 320)
+            return nn(kv[at], d_wide[inner].reshape(256, MINE))
+
+        grads = sum(part(inner) for inner in range(4)).astype(bf16)
+        grad_chunks[z] = nn(order_t[...], grads).astype(bf16).reshape(4, CHUNK, MINE)
+        for y in range(4):
+            grad_chunks[z, y, GROUP:] = rows
+
+
+    for step_at in (1, 3, 2):
+        for half, axis in enumerate("zy"):
+            there = moved(place, axis, (place[axis] + step_at) % 4)
+            remote(
+                column_pieces(grad_chunks, half, there, "y" if half == 0 else "z"),
+                first_in.at[half, step_at - 1],
+                col_send.at[half, 0],
+                col_recv.at[half, 0],
+                device_at(there),
+            ).start()
+
+    @pl.loop(0, 2)
+    def _(low):
+        token_grads(low * 2 + core)
+
     for low in range(2):
         c_swaps[low].wait()
         summed[low] = (
@@ -1057,8 +1156,6 @@
                 sum_recv,
                 device_at(there),
             ).start()
-    two.add(1)
-    two.start(2)
     for half in range(2):
         wait_bytes(first_in.at[half], col_recv.at[half, 0])
         own = column_pieces(grad_chunks, half, place, "y" if half == 0 else "z")
@@ -1128,9 +1225,13 @@
             jax.ShapeDtypeStruct((8, ROWS, MINE), bf16),
             jax.ShapeDtypeStruct((ROWS, D), f32),
         ),
-        in_specs=[VMEM] * 12 + [HBM] + [VMEM] * 7,
+        in_specs=[VMEM] + [HBM] + [VMEM] * 10 + [HBM] * 3 + [VMEM] * 5,
         out_specs=(VMEM, VMEM, VMEM),
         scratch_shapes=[
+            pltpu.VMEM((16 * B, LANES), bf16),
+            pltpu.VMEM((4, 2, 128, MINE), bf16),
+            pltpu.VMEM((D, MINE), bf16),
+            dma((4,)),
             pltpu.VMEM((4, B, 128), bf16),
             pltpu.VMEM((16, 128, B), bf16),
             pltpu.VMEM((4, 1, B), f32),
@@ -1147,7 +1248,6 @@
             pltpu.VMEM((D, 128), bf16),
             pltpu.VMEM((D, 128), bf16),
             pltpu.VMEM((384, D), bf16),
-            pltpu.VMEM((2, 4, 2, ROWS, D), bf16),
             pltpu.VMEM((3, 2, 2, ROWS, D), bf16),
             pltpu.VMEM((4, 4, CHUNK, MINE), bf16),
             pltpu.VMEM((2, 3, 4, CHUNK, 256), bf16),
@@ -1157,7 +1257,7 @@
             pltpu.VMEM((8, ROWS, MINE), bf16),
             pltpu.VMEM((8, ROWS, MINE), bf16),
             dma, dma, dma((8,)), dma((8,)), dma((4,)), dma((4,)), dma, dma,
-            dma, dma((2,)), dma((2,)), dma, dma, dma((2, 2)), dma((2, 2)), dma, dma,
+            dma((2,)), dma((2,)), dma, dma, dma((2, 2)), dma((2, 2)), dma, dma,
         ]
         + scatter_scratch(),
         compiler_params=pltpu.CompilerParams(
@@ -1195,10 +1295,8 @@
     head = lax.axis_index("head")
     at = (blk * 8 + head) * 10
     spread_heads = jnp.zeros((H, LANES), bf16)
-    for i, vector in ((1, query_bias), (2, value_bias)):
-        spread_heads = lax.dynamic_update_slice(
-            spread_heads, vector[None], (blk, i * HD + head * 10)
-        )
+    biases = jnp.concatenate([query_bias, jnp.zeros((HD - 10,), bf16), value_bias])
+    spread_heads = lax.dynamic_update_slice(spread_heads, biases[None], (blk, HD + head * 10))
     natural = jnp.stack([norm1_gain, out_bias, norm2_gain, hidden_bias, proj_bias])
     natural = lax.dynamic_update_slice(jnp.zeros((5, 3 * MINE), bf16), natural, (0, at))
     columns = jnp.concatenate(
@@ -1262,9 +1360,9 @@
     vector_grads = jnp.pad(vector_grads, ((0, 0), (0, 3 * MINE - D))).reshape(12, MINE)
     vector_grads = jnp.pad(vector_grads, ((4, 0), (0, 0)))
     d_normed, shares, two = rear(
-        d_attended, kv, queries, starts, out_t, log_norms,
+        d_attended, kv.reshape(16 * B, LANES), queries, starts, out_t, log_norms,
         attended, d_branch, normed_two, d_pre, activated, upstream_low,
-        ring_normed, packed, wide_w, vector_grads, scale_row,
+        ring_normed.reshape(4 * D, 256), packed, wide_w, vector_grads, scale_row,
     )
     inverse_one = inverse_rms(tokens)
     input_grad = (

time: 285 us -> 275 us (0.965); the launches traced: 285 us -> 271 us
  Pallas kernels: 246 us -> 233 us
    pallas_call x1, Pallas kernels: 142 us -> 129 us  [rear(): pl.pallas_call(rear_kernel, out_shape=(jax.ShapeDtypeStruct((2 * TOK, D),...]
where the time goes in v3:
time: 275 us; the launch traced here: 271 us
  Pallas kernels  233 us (85%)
  local copies, waits for them, and re-layouts  13.6 us (5%)
  other arithmetic  12.4 us (5%)
  matrix products  11 us (4%)
    pallas_call x1, Pallas kernels, rear(): pl.pallas_call(rear_kernel, out_shape=(jax.ShapeDtypeStruct((2 * TOK, D),...  129 us
    pallas_call x1, Pallas kernels, front(): pl.pallas_call(front_kernel, out_shape=(jax.ShapeDtypeStruct((4, D, 256),...  104 us
    dot_general x3, matrix products, nn(): lax.dot_general(a, b, (((1,), (0,)), ((), ())), preferred_element_type=f32)  5.82 us

profile of v3, /device:TPU:97, one launch (start us, length us, event | category | flops | bytes accessed | tf_op | source)
XLA Modules:
  0.0 271.2 jit_solution(17571183861029931296)
XLA Ops:
  0.7 0.7 fusion.11
  1.4 0.1 pad.17.clone
  1.5 0.8 maximum_bitcast_fusion
  2.2 0.1 pad.19.clone
  2.3 0.1 pad.28.clone
  2.4 0.1 concatenate.19
  2.5 1.1 multiply_reduce_fusion.1
  3.6 0.6 rsqrt.27
  4.2 0.7 stack.38
  4.9 1.0 convert_reduce_fusion
  6.0 0.3 dynamic_update_slice.6
  6.3 0.6 broadcast_in_dim.44.scale_row
  6.9 0.2 dynamic_update_slice.7
  7.2 0.9 reshape.145
  8.0 0.9 reshape.144
  8.9 0.9 reshape.146
  9.8 0.1 maximum_maximum_fusion
  10.0 1.5 copy.46
  11.5 1.5 maximum_maximum_fusion.1.pack
  13.1 0.8 pad_maximum_fusion.pieces
  13.9 103.9 %front.1 = (bf16[4,1280,256]{2,1,0:T(8,128)(2,1)}, bf16[4,2,128,512]{3,2,1,0:T(8,128)(2,1)}, bf16[1280,512]{1,0:T(8,128)(2,1)}, f32[16,512]{1,0:T(8,128)}, s32[4...) custom-call(bf16[2,64,1280]{2,1,0:T(8,128)(2,1)} %tokens.1, ...), custom_call_target="tpu_custom_call" | custom-call | tf_op jit(solution)/shard_map/front/pallas_call | solution.py:772
  117.7 0.8 slice.66
  118.5 0.6 slice_reduce_fusion.2
  119.2 3.7 %multiply_reduce_fusion.3 = (f32[128]{0:T(128)S(1)}, f32[128,1280]{1,0:T(8,128)S(1)}) fusion(f32[1280]{0:T(1024)S(1)} %get-tuple-element.54, bf16[128,2048]{1,0:T(8,128)(2,1)} %get-tuple-element.32.attended, bf16[2048,1280]{1,0:T(8,128)(2,1)} %get-tuple-element.33, bf16[128,1280]{1,0:T(8,128)(2,1)S(1)} %bitcast.77), kind=kOutput, calls=%fused_computation.28 | convolution fusion | flops 671907712 | bytes 6755840 | tf_op jit(solution)/shard_map/dot_general | solution.py:48
  122.9 0.1 multiply_convert_fusion.1.normed_two
  123.1 0.7 multiply_convert_fusion
  123.8 1.4 copy-done.1
  125.3 1.3 convert_reduce_fusion.1
  126.6 1.4 fusion.5
  128.0 1.3 multiply_reduce_fusion
  129.3 1.1 convert_reduce_fusion.2
  130.4 2.6 convolution_convert_fusion.pack
  133.1 0.6 pad.9.vector_grads
  133.7 129.2 %rear.1 = (f32[128,1280]{1,0:T(8,128)}, bf16[8,32,512]{2,1,0:T(8,128)(2,1)}, f32[32,1280]{1,0:T(8,128)}) custom-call(bf16[128,2048]{1,0:T(8,128)(2,1)} %convolution_convert_fusion.pack, bf16[8192,256]{1,0:T(8,128)(2,1)} %bitcast.78, bf16[4,512,128]{2,1,0:T(8,128)(2,1)} %get-tuple-element.38.queries, s32[4,1,512]{2,1,0:T(1,128)} %get-tuple-element.39.starts, ...), custom_call_target="tpu_custom_call" | custom-call | tf_op jit(solution)/shard_map/rear/pallas_call | solution.py:1221
  263.0 1.3 fusion.10
  264.3 2.3 fusion.9
  266.6 1.7 fusion.13
  268.5 0.1 copy.41
  268.6 0.6 divide_multiply_fusion
  269.2 0.1 constant_dynamic-slice_fusion
  269.3 0.6 slice_bitcast_fusion.2
  269.9 0.1 fusion.14
  270.0 0.1 reshape.159
  270.1 0.1 reshape.160
  270.3 0.1 multiply_reduce_fusion.4
  270.4 0.1 reshape.158
  270.5 0.1 multiply_reduce_fusion.6
  270.7 0.5 convert_divide_fusion
  (73 shorter events, 0.6 us)
Async XLA Ops:
  0.6 118.5 %copy-start = (bf16[2,64,1280]{2,1,0:T(8,128)(2,1)S(1)}, bf16[2,64,1280]{2,1,0:T(8,128)(2,1)}, u32[]{:S(2)}) copy-start(bf16[2,64,1280]{2,1,0:T(8,128)(2,1)} %tokens.1) | copy-start | bytes 983044
  119.2 3.9 %copy-start.2 = (bf16[1280,1280]{1,0:T(8,128)(2,1)S(1)}, bf16[1280,1280]{1,0:T(8,128)(2,1)}, u32[]{:S(2)}) copy-start(bf16[1280,1280]{1,0:T(8,128)(2,1)} %get-tuple-element.35) | copy-start | bytes 9830404
  123.1 3.5 %copy-start.6 = (bf16[128,1280]{1,0:T(8,128)(2,1)}, bf16[128,1280]{1,0:T(8,128)(2,1)S(1)}, u32[]{:S(2)}) copy-start(bf16[128,1280]{1,0:T(8,128)(2,1)S(1)} %multiply_convert_fusion.1.normed_two) | copy-start | bytes 983044
  123.1 2.2 copy-start.1
  123.1 2.2 copy-start.4
  123.8 2.7 %copy-start.5 = (bf16[128,1280]{1,0:T(8,128)(2,1)}, bf16[128,1280]{1,0:T(8,128)(2,1)S(1)}, u32[]{:S(2)}) copy-start(bf16[128,1280]{1,0:T(8,128)(2,1)S(1)} %get-tuple-element.74.activated) | copy-start | bytes 983044
  126.6 2.7 copy-start.7
  126.6 3.8 %slice-start = ((s8[5242880]{0:T(1024)(128)(4,1)}), s8[4194304]{0:T(1024)(128)(4,1)S(1)}, s32[]{:S(2)}) async-start(s8[5242880]{0:T(1024)(128)(4,1)} %bitcast.75), calls=%async_computation | async-start | bytes 8388608
  128.0 2.5 slice-start.1
  130.4 3.3 %copy-start.3 = (bf16[128,1280]{1,0:T(8,128)(2,1)}, bf16[128,1280]{1,0:T(8,128)(2,1)S(1)}, u32[]{:S(2)}) copy-start(bf16[128,1280]{1,0:T(8,128)(2,1)S(1)} %get-tuple-element.56.d_branch) | copy-start | bytes 983044
  133.7 129.2 %copy-start.15 = (f32[1280]{0:T(1024)S(1)}, f32[1280]{0:T(1024)}, u32[]{:S(2)}) copy-start(f32[1280]{0:T(1024)} %get-tuple-element.50) | copy-start | bytes 15364
  133.7 130.6 %copy-start.17 = (f32[128]{0:T(128)S(1)}, f32[128]{0:T(128)}, u32[]{:S(2)}) copy-start(f32[128]{0:T(128)} %rsqrt.27) | copy-start | bytes 1540
  262.9 5.4 %copy-start.11 = (bf16[8,32,512]{2,1,0:T(8,128)(2,1)S(1)}, bf16[8,32,512]{2,1,0:T(8,128)(2,1)}, u32[]{:S(2)}) copy-start(bf16[8,32,512]{2,1,0:T(8,128)(2,1)} %get-tuple-element.46) | copy-start | bytes 786436
  262.9 5.7 %copy-start.18 = (f32[80]{0:T(128)S(1)}, f32[80]{0:T(128)}, u32[]{:S(2)}) copy-start(f32[80]{0:T(128)} %param.38) | copy-start | bytes 964
  262.9 7.3 %copy-start.13 = (bf16[10,1280]{1,0:T(8,128)(2,1)S(1)}, bf16[10,1280]{1,0:T(8,128)(2,1)}, u32[]{:S(2)}) copy-start(bf16[10,1280]{1,0:T(8,128)(2,1)} %param.28) | copy-start | bytes 76804
  262.9 7.3 %copy-start.14 = (bf16[10,1280]{1,0:T(8,128)(2,1)S(1)}, bf16[10,1280]{1,0:T(8,128)(2,1)}, u32[]{:S(2)}) copy-start(bf16[10,1280]{1,0:T(8,128)(2,1)} %param.27) | copy-start | bytes 76804
  264.3 6.3 %copy-start.12 = (bf16[10,1280]{1,0:T(8,128)(2,1)S(1)}, bf16[10,1280]{1,0:T(8,128)(2,1)}, u32[]{:S(2)}) copy-start(bf16[10,1280]{1,0:T(8,128)(2,1)} %param.26) | copy-start | bytes 76804
  264.3 6.4 %copy-start.16 = (bf16[10]{0:T(256)(128)(2,1)S(1)}, bf16[10]{0:T(256)(128)(2,1)}, u32[]{:S(2)}) copy-start(bf16[10]{0:T(256)(128)(2,1)} %param.25) | copy-start | bytes 64
  270.1 1.1 copy-start.9
  270.3 0.9 copy-start.10
  270.5 0.7 copy-start.8

commit v4 on v3

--- a/solution.py
+++ b/solution.py
@@ -139,25 +139,20 @@
 
 
 def selections():
-    take = np.zeros((240, 256), np.float32)
     join = np.zeros((CHUNK, 256), np.float32)
-    order = np.zeros((4 * GROUP, 4 * CHUNK), np.float32)
     for i in range(8):
         for j in range(10):
-            for w in range(3):
-                take[w * GROUP + i * 10 + j, i * ROWS + w * 10 + j] = 1
             join[i * 10 + j, i * ROWS + j] = 1
-            inner, x_high = i // 2, i % 2
-            for y in range(4):
-                order[inner * GROUP + (y * 2 + x_high) * 10 + j, y * CHUNK + i * 10 + j] = 1
         for v in range(16):
             join[GROUP + v, i * ROWS + 16 + v] = 1
-    share = join.T.copy()
-    return take, join, share, order
-
-
-TAKE, JOIN, SHARE, ORDER = selections()
-TAKE_T = TAKE.reshape(3, GROUP, 256).transpose(0, 2, 1)
+    return join, join.T.copy()
+
+
+JOIN, SHARE = selections()
+
+
+def rows_of(values, size, starts):
+    return jnp.concatenate([values[at : at + size] for at in starts], axis=0)
 
 
 def row_block(ref, g, count):
@@ -258,7 +253,7 @@
 HBM = pl.BlockSpec(memory_space=pl.ANY)
 
 
-def unpack(buf, staged, take, out_w, hidden_w, proj_w, out_sem):
+def unpack(buf, staged, out_w, hidden_w, proj_w, out_sem):
     spans = ((0, 128, out_w), (128, GROUP, hidden_w), (208, GROUP, proj_w))
     staged[:, 0:32] = jnp.zeros((2, 32, D), bf16)
     staged[:, 112:128] = jnp.zeros((2, 16, D), bf16)
@@ -278,9 +273,10 @@
             for out in outs:
                 out.wait()
 
-        rows = nn(take[...], buf[g // 4, (g // 2) % 2, g % 2].reshape(256, D)).astype(bf16)
-        staged[slot, 32:112] = rows[0:80]
-        staged[slot, 128:288] = rows[80:240]
+        packed = buf[g // 4, (g // 2) % 2, g % 2].reshape(256, D).astype(f32)
+        for w, at in enumerate((32, 128, 208)):
+            rows = rows_of(packed, 10, range(w * 10, 256, ROWS))
+            staged[slot, at : at + GROUP] = rows.astype(bf16)
         for out in outs:
             out.start()
 
@@ -500,7 +496,7 @@
 
 
 def front_kernel(
-    tokens, pieces, pack, scale_row, segments, join, order, take,
+    tokens, pieces, pack, scale_row, segments, join,
     normed_hbm, packed_hbm, wide_hbm, vectors, starts, kv_out, queries, out_t, log_norms, attended,
     out_w, hidden_w, proj_w,
     normed_out, normed_t, packed_out, wide_w, keep_sems, ring_tokens, ring_pieces, chunks, kv, value_t, tops, totals, rounded, landed, buf, staged,
@@ -566,15 +562,19 @@
     @pl.loop(0, 4)
     def _(z):
         rows = pl.ds(pl.multiple_of(z * 4 * GROUP, 64), 4 * GROUP)
-        wide_w[rows] = nn(order[...], chunks[z].reshape(4 * CHUNK, MINE)).astype(bf16)
+        found = chunks[z].reshape(4 * CHUNK, MINE).astype(f32)
+        starts_at = [y * CHUNK + inner * 20 for inner in range(4) for y in range(4)]
+        wide_w[rows] = rows_of(found, 20, starts_at).astype(bf16)
 
     vector_rows = jnp.zeros((16, MINE), f32)
     for z in range(4):
         for y in range(4):
             vector_rows = vector_rows + chunks[z, y, GROUP:].astype(f32)
-    vectors[...] = vector_rows
+    for i in range(5):
+        three = [vector_rows[1 + 3 * i + k : 2 + 3 * i + k] for k in range(3)]
+        vectors[i : i + 1] = jnp.concatenate(three[:2] + [three[2][:, :256]], axis=1)
     bias = vector_rows[0:1]
-    gain = jnp.concatenate([vector_rows[1:2], vector_rows[2:3], vector_rows[3:4, :256]], axis=1)
+    gain = vectors[0:1]
     one_lane = jnp.where(
         lax.broadcasted_iota(jnp.int32, (1, MINE), 1) % LANES == 3 * HD, 1.0, 0.0
     )
@@ -751,7 +751,7 @@
             pl.when(turn_at == 3)(lambda: give(j, block))
 
     two.finish()
-    unpack(buf, staged, take, out_w, hidden_w, proj_w, out_sem)
+    unpack(buf, staged, out_w, hidden_w, proj_w, out_sem)
     wait_bytes(landed, back_recv)
     attended[...] = landed[...]
     for keep in keeps + [keep_kv]:
@@ -775,7 +775,7 @@
             jax.ShapeDtypeStruct((4, D, 256), bf16),
             jax.ShapeDtypeStruct((4, 2, 128, MINE), bf16),
             jax.ShapeDtypeStruct((D, MINE), bf16),
-            jax.ShapeDtypeStruct((16, MINE), f32),
+            jax.ShapeDtypeStruct((8, D), f32),
             jax.ShapeDtypeStruct((4, 1, B), jnp.int32),
             jax.ShapeDtypeStruct((16, B, LANES), bf16),
             jax.ShapeDtypeStruct((4, B, 128), bf16),
@@ -786,7 +786,7 @@
             jax.ShapeDtypeStruct((D, D), bf16),
             jax.ShapeDtypeStruct((D, D), bf16),
         ),
-        in_specs=[VMEM] * 8,
+        in_specs=[VMEM] * 6,
         out_specs=(HBM,) * 3 + (VMEM,) * 2 + (HBM,) + (VMEM,) * 4 + (HBM,) * 3,
         scratch_shapes=[
             pltpu.VMEM((4, 256, D), bf16),
@@ -817,19 +817,18 @@
     )(
         *operands,
         jnp.asarray(JOIN, bf16),
-        jnp.asarray(ORDER, bf16),
-        jnp.asarray(TAKE, bf16),
     )
 
 
 def rear_kernel(
     pack, kv_hbm, queries, starts, out_t, log_norms,
     attended, d_branch, normed_two, d_pre, activated, upstream,
-    normed_hbm, packed_hbm, wide_hbm, vector_grads, scale_row, take_t, share, order_t,
-    d_normed, pieces_out, two_out,
+    normed_hbm, packed_hbm, wide_hbm, vector_grads, scale_row, tokens, vectors,
+    share,
+    input_grad, pieces_out, two_out,
     kv, packed, wide_w, load_sems,
     d_out, key_t, deltas, d_query, d_kv, mine_kv, half, half_in, cross, cross_in, final, d_wide,
-    attended_t, normed_two_t, activated_t, right,
+    attended_t, normed_two_t, activated_t,
     sum_in, grad_chunks, first_in, second_in, first_sum,
     joined, shares, shares_in,
     send, recv, core_send, core_recv, x_send, x_recv, back_send, back_recv,
@@ -884,35 +883,41 @@
         lanes = pl.ds(pl.multiple_of(n * 128, 128), 128)
         attended_t[lanes] = attended[:, lanes].T
 
-    right[0:128] = d_branch[...]
-    right[128:256] = d_pre[...]
-    right[256:384] = upstream[...]
-
-    def produce(number, of_core, into):
-        group = number * 2 + of_core
-        rows = pl.ds(pl.multiple_of(group * GROUP, 16), GROUP)
-        out_rows = pl.ds(pl.multiple_of(group * 128 + 32, 16), GROUP)
-        left = jnp.concatenate(
-            [
-                nn(take_t[0], attended_t[out_rows]).astype(bf16),
-                nn(take_t[1], normed_two_t[rows]).astype(bf16),
-                nn(take_t[2], activated_t[rows]).astype(bf16),
-            ],
-            axis=1,
-        )
-        for cell in range(5):
-            lanes = slice(cell * LANES, (cell + 1) * LANES)
-            block = nn(left, right[:, lanes]).astype(bf16)
-            into[number // 2, number % 2, :, :, :, lanes] = block.reshape(4, 2, ROWS, LANES)
 
     @pl.loop(0, 8)
     def _(number):
-        produce(number, 1 - core, two.away)
+        rows = pl.ds(pl.multiple_of(number * 2 * GROUP, 32), 2 * GROUP)
+        heads = [
+            attended_t[pl.ds(pl.multiple_of((number * 2 + k) * 128 + 32, 32), GROUP)]
+            for k in range(2)
+        ]
+        found = [
+            nn(jnp.concatenate(heads, axis=0), d_branch[...]),
+            nn(normed_two_t[rows], d_pre[...]),
+            nn(activated_t[rows], upstream[...]),
+        ]
+        spare = jnp.zeros((2, D), f32)
+        for k in range(2):
+            block = jnp.concatenate(
+                [
+                    part
+                    for i in range(8)
+                    for part in [w[k * GROUP + i * 10 : k * GROUP + i * 10 + 10] for w in found]
+                    + [spare]
+                ],
+                axis=0,
+            )
+            block = block.astype(bf16).reshape(4, 2, ROWS, D)
+
+            @pl.when(core == k)
+            def _():
+                two.mine[number // 2, number % 2] = block
+
+            @pl.when(core != k)
+            def _():
+                two.away[number // 2, number % 2] = block
+
         two.swap(number).start()
-
-    @pl.loop(0, 8)
-    def _(number):
-        produce(number, core, two.mine)
 
     loads[0].wait()
 
@@ -1120,9 +1125,10 @@
             at = pl.ds(pl.multiple_of(inner * D + z * 320, 64), 320)
             return nn(kv[at], d_wide[inner].reshape(256, MINE))
 
-        grads = sum(part(inner) for inner in range(4)).astype(bf16)
-        grad_chunks[z] = nn(order_t[...], grads).astype(bf16).reshape(4, CHUNK, MINE)
+        grads = sum(part(inner) for inner in range(4))
         for y in range(4):
+            found = rows_of(grads, 20, [inner * GROUP + y * 20 for inner in range(4)])
+            grad_chunks[z, y, :GROUP] = found.astype(bf16)
             grad_chunks[z, y, GROUP:] = rows
 
 
@@ -1204,7 +1210,12 @@
         total = summed[x_low, m * 2 + place["x"] // 2].astype(f32)
         for source in range(3):
             total = total + sum_in[source, m].astype(f32)
-        d_normed[m * TOK : (m + 1) * TOK] = total.reshape(TOK, D)
+        values = tokens[m].astype(f32)
+        upward = total.reshape(TOK, D) * vectors[0:1]
+        input_grad[m] = (
+            d_branch[m * TOK : (m + 1) * TOK].astype(f32)
+            + norm_back(upward, values, inverse_rms(values))
+        ).astype(bf16)
     wait_bytes(shares_in, share_recv)
     pieces_out[...] = shares_in[...]
     wait_cells(pack, send, even, 128)
@@ -1221,7 +1232,7 @@
     return pl.pallas_call(
         rear_kernel,
         out_shape=(
-            jax.ShapeDtypeStruct((2 * TOK, D), f32),
+            jax.ShapeDtypeStruct((2, TOK, D), bf16),
             jax.ShapeDtypeStruct((8, ROWS, MINE), bf16),
             jax.ShapeDtypeStruct((ROWS, D), f32),
         ),
@@ -1247,7 +1258,6 @@
             pltpu.VMEM((OUT_WIDE, 128), bf16),
             pltpu.VMEM((D, 128), bf16),
             pltpu.VMEM((D, 128), bf16),
-            pltpu.VMEM((384, D), bf16),
             pltpu.VMEM((3, 2, 2, ROWS, D), bf16),
             pltpu.VMEM((4, 4, CHUNK, MINE), bf16),
             pltpu.VMEM((2, 3, 4, CHUNK, 256), bf16),
@@ -1266,9 +1276,7 @@
         name="rear",
     )(
         *operands,
-        jnp.asarray(TAKE_T, bf16),
         jnp.asarray(SHARE, bf16),
-        jnp.asarray(ORDER.T, bf16),
     )
 
 
@@ -1320,14 +1328,13 @@
     scale_row = jnp.concatenate(
         [ones, softplus_scale, ones, jnp.zeros((LANES - 3 * HD,), f32)] * 2
     )
-    scale_row = jnp.broadcast_to(scale_row, (8, MINE))
+    scale_row = scale_row[None]
 
     (
         ring_normed, packed, wide_w, vectors, starts, kv, queries, out_t, log_norms, attended,
         out_w, hidden_w, proj_w,
     ) = front(inputs, pieces, pack, scale_row, segment_ids.reshape(2, 16, B))
-    every = vectors[1:].reshape(5, 3 * MINE)[:, :D]
-    gain_one, out_b, gain_two, hidden_b, proj_b = [every[i] for i in range(5)]
+    out_b, gain_two, hidden_b, proj_b = [vectors[i] for i in range(1, 5)]
 
     tokens = inputs.reshape(2 * TOK, D).astype(f32)
     residual = tokens + nn(attended, out_w) + out_b
@@ -1359,16 +1366,12 @@
     )
     vector_grads = jnp.pad(vector_grads, ((0, 0), (0, 3 * MINE - D))).reshape(12, MINE)
     vector_grads = jnp.pad(vector_grads, ((4, 0), (0, 0)))
-    d_normed, shares, two = rear(
+    input_grad, shares, two = rear(
         d_attended, kv.reshape(16 * B, LANES), queries, starts, out_t, log_norms,
         attended, d_branch, normed_two, d_pre, activated, upstream_low,
         ring_normed.reshape(4 * D, 256), packed, wide_w, vector_grads, scale_row,
+        inputs, vectors,
     )
-    inverse_one = inverse_rms(tokens)
-    input_grad = (
-        d_residual + norm_back(d_normed * gain_one, tokens, inverse_one)
-    ).astype(bf16)
-
     shares = shares.astype(f32)
     columns = shares[:, :10].transpose(1, 0, 2).reshape(10, H, LANES)
     d_key_w, d_query_w, d_value_w = [
@@ -1388,7 +1391,7 @@
     ) / norm1_gain.astype(f32)
     return (
         layer_out.reshape(2, TOK, D),
-        input_grad.reshape(2, TOK, D),
+        input_grad,
         norm1_gain_grad,
         d_query_w,
         d_key_w,

time: 275 us -> 261 us (0.949)
  Pallas kernels: 233 us -> 225 us
  other arithmetic: 12.4 us -> 7.79 us
    pallas_call x1, Pallas kernels: 129 us -> 123 us  [rear(): pl.pallas_call(rear_kernel, out_shape=(jax.ShapeDtypeStruct((2, TOK, D),...]
where the time goes in v4:
time: 261 us; the launch traced here: 258 us
  Pallas kernels  225 us (86%)
  local copies, waits for them, and re-layouts  13.4 us (5%)
  matrix products  11 us (4%)
  other arithmetic  7.79 us (3%)
    pallas_call x1, Pallas kernels, rear(): pl.pallas_call(rear_kernel, out_shape=(jax.ShapeDtypeStruct((2, TOK, D),...  123 us
    pallas_call x1, Pallas kernels, front(): pl.pallas_call(front_kernel, out_shape=(jax.ShapeDtypeStruct((4, D, 256),...  101 us
    dot_general x3, matrix products, nn(): lax.dot_general(a, b, (((1,), (0,)), ((), ())), preferred_element_type=f32)  5.79 us

profile of v4, /device:TPU:97, one launch (start us, length us, event | category | flops | bytes accessed | tf_op | source)
XLA Modules:
  0.0 258.1 jit_solution(8899046655145921978)
XLA Ops:
  0.7 0.7 fusion.6
  1.4 0.1 pad.17.clone
  1.5 0.8 maximum_bitcast_fusion
  2.2 0.1 pad.19.clone
  2.3 0.1 pad.28.clone
  2.4 0.7 concatenate.19
  3.1 0.7 stack.38
  3.8 1.0 convert_reduce_fusion
  4.9 0.3 dynamic_update_slice.6
  5.2 0.3 dynamic_update_slice.7
  5.5 0.9 reshape.110
  6.4 0.9 reshape.109
  7.3 0.9 reshape.111
  8.2 0.1 maximum_maximum_fusion
  8.3 1.5 copy.42
  9.8 1.5 maximum_maximum_fusion.1.pack
  11.4 0.8 pad_maximum_fusion.pieces
  12.2 101.5 %front.1 = (bf16[4,1280,256]{2,1,0:T(8,128)(2,1)}, bf16[4,2,128,512]{3,2,1,0:T(8,128)(2,1)}, bf16[1280,512]{1,0:T(8,128)(2,1)}, f32[8,1280]{1,0:T(8,128)}, s32[4...) custom-call(bf16[2,64,1280]{2,1,0:T(8,128)(2,1)} %tokens.3, ...), custom_call_target="tpu_custom_call" | custom-call | tf_op jit(solution)/shard_map/front/pallas_call | solution.py:772
  113.7 1.0 slice_reduce_fusion.2
  114.7 3.7 %multiply_reduce_fusion.2 = (f32[128]{0:T(128)S(1)}, f32[128,1280]{1,0:T(8,128)S(1)}) fusion(f32[1280]{0:T(1024)S(1)} %get-tuple-element.53, bf16[128,2048]{1,0:T(8,128)(2,1)} %get-tuple-element.32.attended, bf16[2048,1280]{1,0:T(8,128)(2,1)} %get-tuple-element.33, bf16[128,1280]{1,0:T(8,128)(2,1)S(1)} %bitcast.68), kind=kOutput, calls=%fused_computation.20 | convolution fusion | flops 671907712 | bytes 6755840 | tf_op jit(solution)/shard_map/dot_general | solution.py:48
  118.4 0.1 multiply_convert_fusion.1.normed_two
  118.6 0.7 multiply_convert_fusion
  119.3 1.4 copy-done
  120.8 0.0 copy-done.3
  120.8 1.2 convert_reduce_fusion.1
  122.1 1.4 fusion.5
  123.4 1.3 multiply_reduce_fusion
  124.8 0.3 convert_reduce_fusion.2
  125.1 2.6 %convolution_convert_fusion.pack = bf16[128,2048]{1,0:T(8,128)(2,1)} fusion(bf16[128,1280]{1,0:T(8,128)(2,1)S(1)} %get-tuple-element.55.d_branch, bf16[2048,1280]{1,0:T(8,128)(2,1)S(1)} %bitcast.64), kind=kOutput, calls=%fused_computation.10 | convolution fusion | flops 671350784 | bytes 6094848 | tf_op jit(solution)/shard_map/dot_general | solution.py:52
  127.8 0.6 pad.9.vector_grads
  128.4 123.3 %rear.1 = (bf16[2,64,1280]{2,1,0:T(8,128)(2,1)}, bf16[8,32,512]{2,1,0:T(8,128)(2,1)}, f32[32,1280]{1,0:T(8,128)}) custom-call(bf16[128,2048]{1,0:T(8,128)(2,1)} %convolution_convert_fusion.pack, bf16[8192,256]{1,0:T(8,128)(2,1)} %bitcast.65, bf16[4,512,128]{2,1,0:T(8,128)(2,1)} %get-tuple-element.38.queries, s32[4,1,512]{2,1,0:T(1,128)} %get-tuple-element.39.starts, ...), custom_call_target="tpu_custom_call" | custom-call | tf_op jit(solution)/shard_map/rear/pallas_call | solution.py:1232
  251.7 1.7 fusion.8
  253.5 1.0 convert_element_type.68
  254.6 0.1 copy.37
  254.8 0.6 divide_multiply_fusion
  255.4 0.1 constant_dynamic-slice_fusion
  255.4 0.6 slice_bitcast_fusion.2
  256.0 0.1 fusion.9
  256.1 0.1 reshape.122
  256.3 0.0 copy-start.10
  256.3 0.1 reshape.123
  256.4 0.0 copy-start.11
  256.4 0.1 multiply_reduce_fusion.3
  256.6 0.1 reshape.121
  256.7 0.0 copy-start.9
  256.7 0.1 multiply_reduce_fusion.5
  256.8 0.5 convert_divide_fusion
  257.3 0.7 copy.46
  (61 shorter events, 0.4 us)
Async XLA Ops:
  0.6 114.0 %copy-start.4 = (bf16[2,64,1280]{2,1,0:T(8,128)(2,1)S(1)}, bf16[2,64,1280]{2,1,0:T(8,128)(2,1)}, u32[]{:S(2)}) copy-start(bf16[2,64,1280]{2,1,0:T(8,128)(2,1)} %tokens.3) | copy-start | bytes 983044
  114.7 3.9 %copy-start.1 = (bf16[1280,1280]{1,0:T(8,128)(2,1)S(1)}, bf16[1280,1280]{1,0:T(8,128)(2,1)}, u32[]{:S(2)}) copy-start(bf16[1280,1280]{1,0:T(8,128)(2,1)} %get-tuple-element.35) | copy-start | bytes 9830404
  118.6 3.5 %copy-start.6 = (bf16[128,1280]{1,0:T(8,128)(2,1)}, bf16[128,1280]{1,0:T(8,128)(2,1)S(1)}, u32[]{:S(2)}) copy-start(bf16[128,1280]{1,0:T(8,128)(2,1)S(1)} %multiply_convert_fusion.1.normed_two) | copy-start | bytes 983044
  118.6 2.2 copy-start
  118.6 2.2 copy-start.3
  119.3 2.8 %copy-start.5 = (bf16[128,1280]{1,0:T(8,128)(2,1)}, bf16[128,1280]{1,0:T(8,128)(2,1)S(1)}, u32[]{:S(2)}) copy-start(bf16[128,1280]{1,0:T(8,128)(2,1)S(1)} %get-tuple-element.72.activated) | copy-start | bytes 983044
  120.8 4.3 %slice-start = ((s8[5242880]{0:T(1024)(128)(4,1)}), s8[4194304]{0:T(1024)(128)(4,1)S(1)}, s32[]{:S(2)}) async-start(s8[5242880]{0:T(1024)(128)(4,1)} %bitcast.63), calls=%async_computation | async-start | bytes 8388608
  122.1 2.7 %copy-start.7 = (bf16[128,1280]{1,0:T(8,128)(2,1)}, bf16[128,1280]{1,0:T(8,128)(2,1)S(1)}, u32[]{:S(2)}) copy-start(bf16[128,1280]{1,0:T(8,128)(2,1)S(1)} %get-tuple-element.76.d_pre) | copy-start | bytes 983044
  122.1 3.0 %slice-start.1 = ((s8[5242880]{0:T(1024)(128)(4,1)}), s8[1048576]{0:T(1024)(128)(4,1)S(1)}, s32[]{:S(2)}) async-start(s8[5242880]{0:T(1024)(128)(4,1)} %bitcast.63), calls=%async_computation.1 | async-start | bytes 2097152
  125.1 3.3 %copy-start.2 = (bf16[128,1280]{1,0:T(8,128)(2,1)}, bf16[128,1280]{1,0:T(8,128)(2,1)S(1)}, u32[]{:S(2)}) copy-start(bf16[128,1280]{1,0:T(8,128)(2,1)S(1)} %get-tuple-element.55.d_branch) | copy-start | bytes 983044
  128.4 126.4 %copy-start.16 = (f32[80]{0:T(128)S(1)}, f32[80]{0:T(128)}, u32[]{:S(2)}) copy-start(f32[80]{0:T(128)} %param.34) | copy-start | bytes 964
  251.7 4.7 %copy-start.13 = (bf16[10,1280]{1,0:T(8,128)(2,1)S(1)}, bf16[10,1280]{1,0:T(8,128)(2,1)}, u32[]{:S(2)}) copy-start(bf16[10,1280]{1,0:T(8,128)(2,1)} %param.24) | copy-start | bytes 76804
  251.7 4.7 %copy-start.14 = (bf16[10,1280]{1,0:T(8,128)(2,1)S(1)}, bf16[10,1280]{1,0:T(8,128)(2,1)}, u32[]{:S(2)}) copy-start(bf16[10,1280]{1,0:T(8,128)(2,1)} %param.23) | copy-start | bytes 76804
  251.7 4.9 %copy-start.12 = (bf16[10,1280]{1,0:T(8,128)(2,1)S(1)}, bf16[10,1280]{1,0:T(8,128)(2,1)}, u32[]{:S(2)}) copy-start(bf16[10,1280]{1,0:T(8,128)(2,1)} %param.22) | copy-start | bytes 76804
  251.7 5.1 %copy-start.15 = (bf16[10]{0:T(256)(128)(2,1)S(1)}, bf16[10]{0:T(256)(128)(2,1)}, u32[]{:S(2)}) copy-start(bf16[10]{0:T(256)(128)(2,1)} %param.21) | copy-start | bytes 64
  251.7 5.6 %copy-start.8 = (bf16[2,64,1280]{2,1,0:T(8,128)(2,1)S(1)}, bf16[2,64,1280]{2,1,0:T(8,128)(2,1)}, u32[]{:S(2)}) copy-start(bf16[2,64,1280]{2,1,0:T(8,128)(2,1)} %get-tuple-element.98) | copy-start | bytes 983044
  256.3 1.8 copy-start.10
  256.4 1.7 copy-start.11
  256.7 1.4 copy-start.9

commit v5 on v4

--- a/solution.py
+++ b/solution.py
@@ -30,7 +30,7 @@
 f32 = jnp.float32
 bf16 = jnp.bfloat16
 
-PARTS = (((0, 512), "xyz"), ((512, 384), "yzx"), ((896, 384), "zxy"))
+PARTS = (((0, 384), "xyz"), ((384, 512), "yzx"), ((896, 384), "zxy"))
 PARTS_BACK = (((0, 512), "xyz"), ((512, 512), "xzy"), ((1024, 256), "yzx"))
 
 
@@ -165,10 +165,10 @@
         self.buf, self.send, self.recv = buf, send, recv
         self.sibling = device_at(moved(place, "c", 1 - place["c"]))
 
-    def begin(self, pack, sem):
-        own = pltpu.make_async_copy(pack, self.buf.at[span(self.place, "")], sem)
-        own.start()
-        return own
+    def begin(self, matrices):
+        spare = jnp.zeros((2, D), f32)
+        own = [matrix[...].astype(f32) for matrix in matrices] + [spare]
+        self.buf[span(self.place, "")] = jnp.concatenate(own, axis=0).astype(bf16)
 
     def piece(self, part, where, free):
         first, width = PARTS[part][0]
@@ -496,7 +496,7 @@
 
 
 def front_kernel(
-    tokens, pieces, pack, scale_row, segments, join,
+    tokens, pieces, w_out, w_hidden, w_proj, scale_row, segments, join,
     normed_hbm, packed_hbm, wide_hbm, vectors, starts, kv_out, queries, out_t, log_norms, attended,
     out_w, hidden_w, proj_w,
     normed_out, normed_t, packed_out, wide_w, keep_sems, ring_tokens, ring_pieces, chunks, kv, value_t, tops, totals, rounded, landed, buf, staged,
@@ -515,8 +515,7 @@
     turn = place["x"] * 2 + core
     sibling = (blk + 1 - 2 * core, head)
     two = Gather(buf, two_send, two_recv, place)
-    own = two.begin(pack, own_sem.at[0])
-    own_tokens = pltpu.make_async_copy(tokens, tokens_of(ring_tokens, place), own_sem.at[1])
+    own_tokens = pltpu.make_async_copy(tokens, tokens_of(ring_tokens, place), own_sem)
     own_tokens.start()
     number = ring_number(place)
     pltpu.make_async_copy(pieces.at[turn], ring_pieces.at[number], piece_recv).start()
@@ -536,7 +535,7 @@
             tokens, mine, x_tok_send.at[step - 1], x_tok_recv.at[step - 1], device_at(there)
         ).start()
     remote(tokens, mine, c_tok_send, c_tok_recv, sibling).start()
-    own.wait()
+    two.begin((w_out, w_hidden, w_proj))
     two.stage(0)
     ids = segments[place["z"] // 2]
     before = [jnp.sum((ids < value).astype(jnp.int32)) for value in range(1, 9)]
@@ -678,7 +677,11 @@
     def key_pass(j, of_quarter, count):
         block = query_block(quarter, j)
 
-        @pl.loop(0, count // 2)
+        @pl.when(count == 4)
+        def _():
+            step(j, block, tuple(query_block(of_quarter, n) for n in range(4)))
+
+        @pl.loop(0, jnp.where(count == 4, 0, count // 2))
         def _(n):
             last = count - 1 - 2 * n
             step(j, block, (query_block(of_quarter, last), query_block(of_quarter, last - 1)))
@@ -786,7 +789,7 @@
             jax.ShapeDtypeStruct((D, D), bf16),
             jax.ShapeDtypeStruct((D, D), bf16),
         ),
-        in_specs=[VMEM] * 6,
+        in_specs=[VMEM] * 8,
         out_specs=(HBM,) * 3 + (VMEM,) * 2 + (HBM,) + (VMEM,) * 4 + (HBM,) * 3,
         scratch_shapes=[
             pltpu.VMEM((4, 256, D), bf16),
@@ -806,7 +809,7 @@
             pltpu.VMEM((4, 2, 2, 4, 2, ROWS, D), bf16),
             pltpu.VMEM((2, 288, D), bf16),
             dma((3,)), dma((3,)), dma, dma, dma, dma, dma((2, 2)), dma((2, 2)),
-            dma((3, 4)), dma((3, 6)), dma((2,)),
+            dma((3, 4)), dma((3, 6)), dma,
         ]
         + [dma] * 11
         + [dma((3, 2))],
@@ -821,12 +824,12 @@
 
 
 def rear_kernel(
-    pack, kv_hbm, queries, starts, out_t, log_norms,
+    pack, kv_hbm, queries_hbm, starts, out_t_hbm, log_norms,
     attended, d_branch, normed_two, d_pre, activated, upstream,
     normed_hbm, packed_hbm, wide_hbm, vector_grads, scale_row, tokens, vectors,
     share,
     input_grad, pieces_out, two_out,
-    kv, packed, wide_w, load_sems,
+    kv, queries, out_t, packed, wide_w, load_sems,
     d_out, key_t, deltas, d_query, d_kv, mine_kv, half, half_in, cross, cross_in, final, d_wide,
     attended_t, normed_two_t, activated_t,
     sum_in, grad_chunks, first_in, second_in, first_sum,
@@ -849,7 +852,13 @@
     loads = [
         pltpu.make_async_copy(src, dst, load_sems.at[i])
         for i, (src, dst) in enumerate(
-            ((kv_hbm, kv), (packed_hbm, packed), (wide_hbm, wide_w))
+            (
+                (kv_hbm, kv),
+                (queries_hbm, queries),
+                (out_t_hbm, out_t),
+                (packed_hbm, packed),
+                (wide_hbm, wide_w),
+            )
         )
     ]
     for load in loads:
@@ -919,7 +928,8 @@
 
         two.swap(number).start()
 
-    loads[0].wait()
+    for load in loads[:3]:
+        load.wait()
 
     def keys_at(block, lane):
         return kv[pl.ds(pl.multiple_of(block * B, B), B), lane : lane + 128]
@@ -1013,7 +1023,7 @@
             def _():
                 remote(src, dst, back_send, back_recv, (blk_to, head_to)).start()
 
-    load_normed = pltpu.make_async_copy(normed_hbm, kv.at[pl.ds(0, 4 * D)], load_sems.at[3])
+    load_normed = pltpu.make_async_copy(normed_hbm, kv.at[pl.ds(0, 4 * D)], load_sems.at[5])
 
     def key_steps(key_block):
         z = key_block // 4
@@ -1070,7 +1080,7 @@
     two.start(2)
     wait_bytes(d_wide, back_recv)
 
-    for load in loads[1:]:
+    for load in loads[3:]:
         load.wait()
     load_normed.wait()
     partial = two.away.at[:, 0]
@@ -1236,13 +1246,15 @@
             jax.ShapeDtypeStruct((8, ROWS, MINE), bf16),
             jax.ShapeDtypeStruct((ROWS, D), f32),
         ),
-        in_specs=[VMEM] + [HBM] + [VMEM] * 10 + [HBM] * 3 + [VMEM] * 5,
+        in_specs=[HBM] * 3 + [VMEM, HBM] + [VMEM] * 7 + [HBM] * 3 + [VMEM] * 5,
         out_specs=(VMEM, VMEM, VMEM),
         scratch_shapes=[
             pltpu.VMEM((16 * B, LANES), bf16),
+            pltpu.VMEM((4, B, 128), bf16),
+            pltpu.VMEM((4, 128, B), f32),
             pltpu.VMEM((4, 2, 128, MINE), bf16),
             pltpu.VMEM((D, MINE), bf16),
-            dma((4,)),
+            dma((6,)),
             pltpu.VMEM((4, B, 128), bf16),
             pltpu.VMEM((16, 128, B), bf16),
             pltpu.VMEM((4, 1, B), f32),
@@ -1322,7 +1334,6 @@
         ],
         axis=1,
     )
-    pack = jnp.concatenate([w_out, w_hidden, w_proj, jnp.zeros((2, D), bf16)], axis=0)
     softplus_scale = LOG2E / math.sqrt(HD) * jax.nn.softplus(dim_scale)
     ones = jnp.ones((HD,), f32)
     scale_row = jnp.concatenate(
@@ -1333,7 +1344,9 @@
     (
         ring_normed, packed, wide_w, vectors, starts, kv, queries, out_t, log_norms, attended,
         out_w, hidden_w, proj_w,
-    ) = front(inputs, pieces, pack, scale_row, segment_ids.reshape(2, 16, B))
+    ) = front(
+        inputs, pieces, w_out, w_hidden, w_proj, scale_row, segment_ids.reshape(2, 16, B)
+    )
     out_b, gain_two, hidden_b, proj_b = [vectors[i] for i in range(1, 5)]
 
     tokens = inputs.reshape(2 * TOK, D).astype(f32)

time: 261 us -> 256 us (0.981)
  Pallas kernels: 225 us -> 221 us
    pallas_call x1, Pallas kernels: 123 us -> 120 us  [rear(): pl.pallas_call(rear_kernel, out_shape=(jax.ShapeDtypeStruct((2, TOK, D),...]
where the time goes in v5:
time: 256 us; the launch traced here: 253 us
  Pallas kernels  221 us (86%)
  local copies, waits for them, and re-layouts  13.4 us (5%)
  matrix products  11 us (4%)
  other arithmetic  6.26 us (2%)
    pallas_call x1, Pallas kernels, rear(): pl.pallas_call(rear_kernel, out_shape=(jax.ShapeDtypeStruct((2, TOK, D),...  120 us
    pallas_call x1, Pallas kernels, front(): pl.pallas_call(front_kernel, out_shape=(jax.ShapeDtypeStruct((4, D, 256),...  101 us
    dot_general x3, matrix products, nn(): lax.dot_general(a, b, (((1,), (0,)), ((), ())), preferred_element_type=f32)  5.79 us
    dot_general x3, matrix products, nt(): lax.dot_general(a, b, (((1,), (1,)), ((), ())), preferred_element_type=f32)  5.17 us

profile of v5, /device:TPU:97, one launch (start us, length us, event | category | flops | bytes accessed | tf_op | source)
XLA Modules:
  0.0 252.7 jit_solution(18243235503350317516)
XLA Ops:
  0.7 0.7 fusion.6
  1.4 0.8 maximum_bitcast_fusion
  2.1 0.1 pad.15.clone
  2.2 0.1 pad.24.clone
  2.3 0.7 concatenate.15
  3.0 0.7 stack.38
  3.7 1.0 convert_reduce_fusion
  4.8 0.3 dynamic_update_slice.6
  5.1 0.3 dynamic_update_slice.7
  5.4 0.9 reshape.110
  6.3 0.9 reshape.109
  7.2 0.9 reshape.111
  8.1 0.1 maximum_maximum_fusion
  8.3 1.5 copy.42
  9.8 0.8 pad_maximum_fusion.pieces
  10.6 101.3 %front.1 = (bf16[4,1280,256]{2,1,0:T(8,128)(2,1)}, bf16[4,2,128,512]{3,2,1,0:T(8,128)(2,1)}, bf16[1280,512]{1,0:T(8,128)(2,1)}, f32[8,1280]{1,0:T(8,128)}, s32[4...) custom-call(bf16[2,64,1280]{2,1,0:T(8,128)(2,1)} %tokens.3, ...), custom_call_target="tpu_custom_call" | custom-call | tf_op jit(solution)/shard_map/front/pallas_call | solution.py:775
  111.9 1.0 slice_reduce_fusion.2
  112.9 3.7 %multiply_reduce_fusion.2 = (f32[128]{0:T(128)S(1)}, f32[128,1280]{1,0:T(8,128)S(1)}) fusion(f32[1280]{0:T(1024)S(1)} %get-tuple-element.53, bf16[128,2048]{1,0:T(8,128)(2,1)} %get-tuple-element.32.attended, bf16[2048,1280]{1,0:T(8,128)(2,1)} %get-tuple-element.33, bf16[128,1280]{1,0:T(8,128)(2,1)S(1)} %bitcast.68), kind=kOutput, calls=%fused_computation.20 | convolution fusion | flops 671907712 | bytes 6755840 | tf_op jit(solution)/shard_map/dot_general | solution.py:48
  116.6 0.1 multiply_convert_fusion.1.normed_two
  116.8 0.0 copy-start.3
  116.8 0.7 multiply_convert_fusion
  117.5 1.4 copy-done
  119.0 0.0 copy-done.3
  119.0 1.2 convert_reduce_fusion.1
  120.3 1.4 fusion.5
  121.7 1.3 multiply_reduce_fusion
  123.0 0.3 convert_reduce_fusion.2
  123.3 2.6 %convolution_convert_fusion.pack = bf16[128,2048]{1,0:T(8,128)(2,1)} fusion(bf16[128,1280]{1,0:T(8,128)(2,1)S(1)} %get-tuple-element.55.d_branch, bf16[2048,1280]{1,0:T(8,128)(2,1)S(1)} %bitcast.64), kind=kOutput, calls=%fused_computation.10 | convolution fusion | flops 671350784 | bytes 6094848 | tf_op jit(solution)/shard_map/dot_general | solution.py:52
  126.0 0.6 pad.9.vector_grads
  126.6 119.7 %rear.1 = (bf16[2,64,1280]{2,1,0:T(8,128)(2,1)}, bf16[8,32,512]{2,1,0:T(8,128)(2,1)}, f32[32,1280]{1,0:T(8,128)}) custom-call(bf16[128,2048]{1,0:T(8,128)(2,1)} %convolution_convert_fusion.pack, bf16[8192,256]{1,0:T(8,128)(2,1)} %bitcast.65, bf16[4,512,128]{2,1,0:T(8,128)(2,1)} %get-tuple-element.38.queries_hbm, s32[4,1,512]{2,1,0:T(1,128)} %get-tuple-element.39.starts, ...), custom_call_target="tpu_custom_call" | custom-call | tf_op jit(solution)/shard_map/rear/pallas_call | solution.py:1242
  246.3 0.0 copy-start.12
  246.4 1.7 fusion.8
  248.1 1.0 convert_element_type.68
  249.2 0.1 copy.37
  249.4 0.6 divide_multiply_fusion
  250.0 0.1 constant_dynamic-slice_fusion
  250.1 0.6 slice_bitcast_fusion.2
  250.7 0.1 fusion.9
  250.8 0.1 reshape.122
  250.9 0.0 copy-start.10
  250.9 0.1 reshape.123
  251.0 0.0 copy-start.11
  251.0 0.1 multiply_reduce_fusion.3
  251.2 0.1 reshape.121
  251.3 0.0 copy-start.9
  251.3 0.1 multiply_reduce_fusion.5
  251.4 0.5 convert_divide_fusion
  252.0 0.7 copy.46
  (58 shorter events, 0.4 us)
Async XLA Ops:
  0.6 112.2 %copy-start.4 = (bf16[2,64,1280]{2,1,0:T(8,128)(2,1)S(1)}, bf16[2,64,1280]{2,1,0:T(8,128)(2,1)}, u32[]{:S(2)}) copy-start(bf16[2,64,1280]{2,1,0:T(8,128)(2,1)} %tokens.3) | copy-start | bytes 983044
  112.9 3.9 %copy-start.1 = (bf16[1280,1280]{1,0:T(8,128)(2,1)S(1)}, bf16[1280,1280]{1,0:T(8,128)(2,1)}, u32[]{:S(2)}) copy-start(bf16[1280,1280]{1,0:T(8,128)(2,1)} %get-tuple-element.35) | copy-start | bytes 9830404
  116.8 3.5 %copy-start.6 = (bf16[128,1280]{1,0:T(8,128)(2,1)}, bf16[128,1280]{1,0:T(8,128)(2,1)S(1)}, u32[]{:S(2)}) copy-start(bf16[128,1280]{1,0:T(8,128)(2,1)S(1)} %multiply_convert_fusion.1.normed_two) | copy-start | bytes 983044
  116.8 2.2 copy-start
  116.8 2.2 copy-start.3
  117.5 2.8 %copy-start.5 = (bf16[128,1280]{1,0:T(8,128)(2,1)}, bf16[128,1280]{1,0:T(8,128)(2,1)S(1)}, u32[]{:S(2)}) copy-start(bf16[128,1280]{1,0:T(8,128)(2,1)S(1)} %get-tuple-element.72.activated) | copy-start | bytes 983044
  119.0 4.3 %slice-start = ((s8[5242880]{0:T(1024)(128)(4,1)}), s8[4194304]{0:T(1024)(128)(4,1)S(1)}, s32[]{:S(2)}) async-start(s8[5242880]{0:T(1024)(128)(4,1)} %bitcast.63), calls=%async_computation | async-start | bytes 8388608
  120.3 2.7 %copy-start.7 = (bf16[128,1280]{1,0:T(8,128)(2,1)}, bf16[128,1280]{1,0:T(8,128)(2,1)S(1)}, u32[]{:S(2)}) copy-start(bf16[128,1280]{1,0:T(8,128)(2,1)S(1)} %get-tuple-element.76.d_pre) | copy-start | bytes 983044
  120.3 3.0 %slice-start.1 = ((s8[5242880]{0:T(1024)(128)(4,1)}), s8[1048576]{0:T(1024)(128)(4,1)S(1)}, s32[]{:S(2)}) async-start(s8[5242880]{0:T(1024)(128)(4,1)} %bitcast.63), calls=%async_computation.1 | async-start | bytes 2097152
  123.3 3.3 %copy-start.2 = (bf16[128,1280]{1,0:T(8,128)(2,1)}, bf16[128,1280]{1,0:T(8,128)(2,1)S(1)}, u32[]{:S(2)}) copy-start(bf16[128,1280]{1,0:T(8,128)(2,1)S(1)} %get-tuple-element.55.d_branch) | copy-start | bytes 983044
  126.6 122.8 %copy-start.16 = (f32[80]{0:T(128)S(1)}, f32[80]{0:T(128)}, u32[]{:S(2)}) copy-start(f32[80]{0:T(128)} %param.34) | copy-start | bytes 964
  246.3 4.7 %copy-start.13 = (bf16[10,1280]{1,0:T(8,128)(2,1)S(1)}, bf16[10,1280]{1,0:T(8,128)(2,1)}, u32[]{:S(2)}) copy-start(bf16[10,1280]{1,0:T(8,128)(2,1)} %param.24) | copy-start | bytes 76804
  246.3 4.7 %copy-start.14 = (bf16[10,1280]{1,0:T(8,128)(2,1)S(1)}, bf16[10,1280]{1,0:T(8,128)(2,1)}, u32[]{:S(2)}) copy-start(bf16[10,1280]{1,0:T(8,128)(2,1)} %param.23) | copy-start | bytes 76804
  246.3 4.9 %copy-start.12 = (bf16[10,1280]{1,0:T(8,128)(2,1)S(1)}, bf16[10,1280]{1,0:T(8,128)(2,1)}, u32[]{:S(2)}) copy-start(bf16[10,1280]{1,0:T(8,128)(2,1)} %param.22) | copy-start | bytes 76804
  246.4 5.1 %copy-start.15 = (bf16[10]{0:T(256)(128)(2,1)S(1)}, bf16[10]{0:T(256)(128)(2,1)}, u32[]{:S(2)}) copy-start(bf16[10]{0:T(256)(128)(2,1)} %param.21) | copy-start | bytes 64
  246.4 5.6 %copy-start.8 = (bf16[2,64,1280]{2,1,0:T(8,128)(2,1)S(1)}, bf16[2,64,1280]{2,1,0:T(8,128)(2,1)}, u32[]{:S(2)}) copy-start(bf16[2,64,1280]{2,1,0:T(8,128)(2,1)} %get-tuple-element.98) | copy-start | bytes 983044
  250.9 1.8 copy-start.10
  251.0 1.7 copy-start.11
  251.3 1.4 copy-start.9

commit v6 on v5

--- a/solution.py
+++ b/solution.py
@@ -100,14 +100,17 @@
 
 def greet_all():
     barrier = pltpu.get_barrier_semaphore()
-    me = lax.axis_index("blk") * 8 + lax.axis_index("head")
-
-    @pl.loop(1, 128)
-    def _(k):
-        other = (me + k) % 128
-        pl.semaphore_signal(
-            barrier, inc=1, device_id=(other // 8, other % 8), device_id_type=MESH
-        )
+    blk = lax.axis_index("blk")
+    head = lax.axis_index("head")
+    heads = [(head + h) % 8 for h in range(8)]
+    for h in range(1, 8):
+        pl.semaphore_signal(barrier, inc=1, device_id=(blk, heads[h]), device_id_type=MESH)
+
+    @pl.loop(1, 16)
+    def _(b):
+        other = (blk + b) % 16
+        for h in range(8):
+            pl.semaphore_signal(barrier, inc=1, device_id=(other, heads[h]), device_id_type=MESH)
 
     pl.semaphore_wait(barrier, 127)
 

time: 256 us -> 252 us (0.984)
  Pallas kernels: 221 us -> 218 us
    pallas_call x1, Pallas kernels: 101 us -> 98.7 us  [front(): pl.pallas_call(front_kernel, out_shape=(jax.ShapeDtypeStruct((4, D, 256),...]
where the time goes in v6:
time: 252 us; the launch traced here: 249 us
  Pallas kernels  218 us (87%)
  local copies, waits for them, and re-layouts  13.4 us (5%)
  matrix products  11 us (4%)
  other arithmetic  6.26 us (2%)
    pallas_call x1, Pallas kernels, rear(): pl.pallas_call(rear_kernel, out_shape=(jax.ShapeDtypeStruct((2, TOK, D),...  119 us
    pallas_call x1, Pallas kernels, front(): pl.pallas_call(front_kernel, out_shape=(jax.ShapeDtypeStruct((4, D, 256),...  98.7 us
    dot_general x3, matrix products, nn(): lax.dot_general(a, b, (((1,), (0,)), ((), ())), preferred_element_type=f32)  5.79 us
    dot_general x3, matrix products, nt(): lax.dot_general(a, b, (((1,), (1,)), ((), ())), preferred_element_type=f32)  5.17 us

profile of v6, /device:TPU:97, one launch (start us, length us, event | category | flops | bytes accessed | tf_op | source)
XLA Modules:
  0.0 249.3 jit_solution(7536490216538012585)
XLA Ops:
  0.6 0.0 copy-start.4
  0.7 0.7 fusion.6
  1.4 0.8 maximum_bitcast_fusion
  2.1 0.1 pad.15.clone
  2.2 0.1 pad.24.clone
  2.3 0.7 concatenate.15
  3.0 0.7 stack.38
  3.7 1.0 convert_reduce_fusion
  4.8 0.3 dynamic_update_slice.6
  5.1 0.3 dynamic_update_slice.7
  5.4 0.9 reshape.110
  6.3 0.9 reshape.109
  7.2 0.9 reshape.111
  8.1 0.1 maximum_maximum_fusion
  8.3 1.5 copy.42
  9.8 0.8 pad_maximum_fusion.pieces
  10.6 98.7 %front.1 = (bf16[4,1280,256]{2,1,0:T(8,128)(2,1)}, bf16[4,2,128,512]{3,2,1,0:T(8,128)(2,1)}, bf16[1280,512]{1,0:T(8,128)(2,1)}, f32[8,1280]{1,0:T(8,128)}, s32[4...) custom-call(bf16[2,64,1280]{2,1,0:T(8,128)(2,1)} %tokens.3, ...), custom_call_target="tpu_custom_call" | custom-call | tf_op jit(solution)/shard_map/front/pallas_call | solution.py:778
  109.3 1.0 slice_reduce_fusion.2
  110.3 3.7 %multiply_reduce_fusion.2 = (f32[128]{0:T(128)S(1)}, f32[128,1280]{1,0:T(8,128)S(1)}) fusion(f32[1280]{0:T(1024)S(1)} %get-tuple-element.53, bf16[128,2048]{1,0:T(8,128)(2,1)} %get-tuple-element.32.attended, bf16[2048,1280]{1,0:T(8,128)(2,1)} %get-tuple-element.33, bf16[128,1280]{1,0:T(8,128)(2,1)S(1)} %bitcast.68), kind=kOutput, calls=%fused_computation.20 | convolution fusion | flops 671907712 | bytes 6755840 | tf_op jit(solution)/shard_map/dot_general | solution.py:48
  114.1 0.1 multiply_convert_fusion.1.normed_two
  114.2 0.7 multiply_convert_fusion
  114.9 1.4 copy-done
  116.4 0.0 copy-done.3
  116.4 1.2 convert_reduce_fusion.1
  117.7 1.4 fusion.5
  119.1 1.3 multiply_reduce_fusion
  120.4 0.3 convert_reduce_fusion.2
  120.7 0.0 copy-start.2
  120.7 2.6 %convolution_convert_fusion.pack = bf16[128,2048]{1,0:T(8,128)(2,1)} fusion(bf16[128,1280]{1,0:T(8,128)(2,1)S(1)} %get-tuple-element.55.d_branch, bf16[2048,1280]{1,0:T(8,128)(2,1)S(1)} %bitcast.64), kind=kOutput, calls=%fused_computation.10 | convolution fusion | flops 671350784 | bytes 6094848 | tf_op jit(solution)/shard_map/dot_general | solution.py:52
  123.4 0.6 pad.9.vector_grads
  124.0 118.9 %rear.1 = (bf16[2,64,1280]{2,1,0:T(8,128)(2,1)}, bf16[8,32,512]{2,1,0:T(8,128)(2,1)}, f32[32,1280]{1,0:T(8,128)}) custom-call(bf16[128,2048]{1,0:T(8,128)(2,1)} %convolution_convert_fusion.pack, bf16[8192,256]{1,0:T(8,128)(2,1)} %bitcast.65, bf16[4,512,128]{2,1,0:T(8,128)(2,1)} %get-tuple-element.38.queries_hbm, s32[4,1,512]{2,1,0:T(1,128)} %get-tuple-element.39.starts, ...), custom_call_target="tpu_custom_call" | custom-call | tf_op jit(solution)/shard_map/rear/pallas_call | solution.py:1245
  243.0 1.7 fusion.8
  244.8 1.0 convert_element_type.68
  245.9 0.1 copy.37
  246.0 0.6 divide_multiply_fusion
  246.6 0.1 constant_dynamic-slice_fusion
  246.7 0.6 slice_bitcast_fusion.2
  247.3 0.1 fusion.9
  247.4 0.1 reshape.122
  247.5 0.0 copy-start.10
  247.5 0.1 reshape.123
  247.7 0.0 copy-start.11
  247.7 0.1 multiply_reduce_fusion.3
  247.8 0.1 reshape.121
  247.9 0.0 copy-start.9
  248.0 0.1 multiply_reduce_fusion.5
  248.1 0.5 convert_divide_fusion
  248.6 0.7 copy.46
  (58 shorter events, 0.4 us)
Async XLA Ops:
  0.6 109.6 %copy-start.4 = (bf16[2,64,1280]{2,1,0:T(8,128)(2,1)S(1)}, bf16[2,64,1280]{2,1,0:T(8,128)(2,1)}, u32[]{:S(2)}) copy-start(bf16[2,64,1280]{2,1,0:T(8,128)(2,1)} %tokens.3) | copy-start | bytes 983044
  110.3 3.9 %copy-start.1 = (bf16[1280,1280]{1,0:T(8,128)(2,1)S(1)}, bf16[1280,1280]{1,0:T(8,128)(2,1)}, u32[]{:S(2)}) copy-start(bf16[1280,1280]{1,0:T(8,128)(2,1)} %get-tuple-element.35) | copy-start | bytes 9830404
  114.2 3.5 %copy-start.6 = (bf16[128,1280]{1,0:T(8,128)(2,1)}, bf16[128,1280]{1,0:T(8,128)(2,1)S(1)}, u32[]{:S(2)}) copy-start(bf16[128,1280]{1,0:T(8,128)(2,1)S(1)} %multiply_convert_fusion.1.normed_two) | copy-start | bytes 983044
  114.2 2.2 copy-start
  114.2 2.2 copy-start.3
  114.9 2.8 %copy-start.5 = (bf16[128,1280]{1,0:T(8,128)(2,1)}, bf16[128,1280]{1,0:T(8,128)(2,1)S(1)}, u32[]{:S(2)}) copy-start(bf16[128,1280]{1,0:T(8,128)(2,1)S(1)} %get-tuple-element.72.activated) | copy-start | bytes 983044
  116.4 4.3 %slice-start = ((s8[5242880]{0:T(1024)(128)(4,1)}), s8[4194304]{0:T(1024)(128)(4,1)S(1)}, s32[]{:S(2)}) async-start(s8[5242880]{0:T(1024)(128)(4,1)} %bitcast.63), calls=%async_computation | async-start | bytes 8388608
  117.7 2.7 %copy-start.7 = (bf16[128,1280]{1,0:T(8,128)(2,1)}, bf16[128,1280]{1,0:T(8,128)(2,1)S(1)}, u32[]{:S(2)}) copy-start(bf16[128,1280]{1,0:T(8,128)(2,1)S(1)} %get-tuple-element.76.d_pre) | copy-start | bytes 983044
  117.7 3.0 %slice-start.1 = ((s8[5242880]{0:T(1024)(128)(4,1)}), s8[1048576]{0:T(1024)(128)(4,1)S(1)}, s32[]{:S(2)}) async-start(s8[5242880]{0:T(1024)(128)(4,1)} %bitcast.63), calls=%async_computation.1 | async-start | bytes 2097152
  120.7 3.3 %copy-start.2 = (bf16[128,1280]{1,0:T(8,128)(2,1)}, bf16[128,1280]{1,0:T(8,128)(2,1)S(1)}, u32[]{:S(2)}) copy-start(bf16[128,1280]{1,0:T(8,128)(2,1)S(1)} %get-tuple-element.55.d_branch) | copy-start | bytes 983044
  124.0 122.0 %copy-start.16 = (f32[80]{0:T(128)S(1)}, f32[80]{0:T(128)}, u32[]{:S(2)}) copy-start(f32[80]{0:T(128)} %param.34) | copy-start | bytes 964
  243.0 4.7 %copy-start.13 = (bf16[10,1280]{1,0:T(8,128)(2,1)S(1)}, bf16[10,1280]{1,0:T(8,128)(2,1)}, u32[]{:S(2)}) copy-start(bf16[10,1280]{1,0:T(8,128)(2,1)} %param.24) | copy-start | bytes 76804
  243.0 4.7 %copy-start.14 = (bf16[10,1280]{1,0:T(8,128)(2,1)S(1)}, bf16[10,1280]{1,0:T(8,128)(2,1)}, u32[]{:S(2)}) copy-start(bf16[10,1280]{1,0:T(8,128)(2,1)} %param.23) | copy-start | bytes 76804
  243.0 4.9 %copy-start.12 = (bf16[10,1280]{1,0:T(8,128)(2,1)S(1)}, bf16[10,1280]{1,0:T(8,128)(2,1)}, u32[]{:S(2)}) copy-start(bf16[10,1280]{1,0:T(8,128)(2,1)} %param.22) | copy-start | bytes 76804
  243.0 5.1 %copy-start.15 = (bf16[10]{0:T(256)(128)(2,1)S(1)}, bf16[10]{0:T(256)(128)(2,1)}, u32[]{:S(2)}) copy-start(bf16[10]{0:T(256)(128)(2,1)} %param.21) | copy-start | bytes 64
  243.0 5.6 %copy-start.8 = (bf16[2,64,1280]{2,1,0:T(8,128)(2,1)S(1)}, bf16[2,64,1280]{2,1,0:T(8,128)(2,1)}, u32[]{:S(2)}) copy-start(bf16[2,64,1280]{2,1,0:T(8,128)(2,1)} %get-tuple-element.98) | copy-start | bytes 983044
  247.5 1.8 copy-start.10
  247.7 1.7 copy-start.11
  247.9 1.4 copy-start.9

commit v7 on v6

--- a/solution.py
+++ b/solution.py
@@ -868,20 +868,23 @@
         load.start()
     greet_all()
 
-    @pl.loop(0, PAIRS)
-    def _(k):
-        p = (pair + k) % PAIRS
-        src = cell_of(pack, p, 128)
-        dst = d_out.at[blk // 4, pl.ds(head * TOK, TOK)]
-        mine = (k == 0) & even
-
-        @pl.when(mine)
-        def _():
-            pltpu.make_async_copy(src, dst, recv).start()
-
-        @pl.when(jnp.logical_not(mine))
-        def _():
-            remote(src, dst, send, recv, pair_device(p, to_quarter)).start()
+    dst = d_out.at[blk // 4, pl.ds(head * TOK, TOK)]
+    heads = [(head + k) % 8 for k in range(8)]
+    places_of = [(to % 2) * 8 + to // 2 for to in heads]
+
+    @pl.loop(0, 4)
+    def _(step_at):
+        z = (place["z"] + step_at) % 4
+        rows = pl.ds(z // 2 * TOK, TOK)
+        for k in range(8):
+            src = pack.at[rows, pl.ds(((z % 2) * 4 + places_of[k]) * 128, 128)]
+            copy = remote(src, dst, send, recv, (z * 4 + to_quarter, heads[k]))
+            if k:
+                copy.start()
+                continue
+            mine = (step_at == 0) & even
+            pl.when(mine)(lambda src=src: pltpu.make_async_copy(src, dst, recv).start())
+            pl.when(jnp.logical_not(mine))(copy.start)
 
 
     @pl.loop(0, D // 128)

time: 252 us -> 253 us (level)
  no operation moved by 1% of the time
where the time goes in v7:
time: 253 us; the launch traced here: 249 us
  Pallas kernels  217 us (86%)
  local copies, waits for them, and re-layouts  13.4 us (5%)
  matrix products  11 us (4%)
  other arithmetic  6.26 us (2%)
    pallas_call x1, Pallas kernels, rear(): pl.pallas_call(rear_kernel, out_shape=(jax.ShapeDtypeStruct((2, TOK, D),...  118 us
    pallas_call x1, Pallas kernels, front(): pl.pallas_call(front_kernel, out_shape=(jax.ShapeDtypeStruct((4, D, 256),...  98.7 us
    dot_general x3, matrix products, nn(): lax.dot_general(a, b, (((1,), (0,)), ((), ())), preferred_element_type=f32)  5.79 us
    dot_general x3, matrix products, nt(): lax.dot_general(a, b, (((1,), (1,)), ((), ())), preferred_element_type=f32)  5.17 us

profile of v7, /device:TPU:97, one launch (start us, length us, event | category | flops | bytes accessed | tf_op | source)
XLA Modules:
  0.0 248.7 jit_solution(17021013842030971072)
XLA Ops:
  0.7 0.7 fusion.6
  1.4 0.8 maximum_bitcast_fusion
  2.1 0.1 pad.15.clone
  2.2 0.1 pad.24.clone
  2.3 0.7 concatenate.15
  3.0 0.7 stack.38
  3.7 1.0 convert_reduce_fusion
  4.8 0.3 dynamic_update_slice.6
  5.1 0.3 dynamic_update_slice.7
  5.4 0.9 reshape.110
  6.3 0.9 reshape.109
  7.2 0.9 reshape.111
  8.1 0.1 maximum_maximum_fusion
  8.3 1.5 copy.42
  9.8 0.8 pad_maximum_fusion.pieces
  10.6 98.7 %front.1 = (bf16[4,1280,256]{2,1,0:T(8,128)(2,1)}, bf16[4,2,128,512]{3,2,1,0:T(8,128)(2,1)}, bf16[1280,512]{1,0:T(8,128)(2,1)}, f32[8,1280]{1,0:T(8,128)}, s32[4...) custom-call(bf16[2,64,1280]{2,1,0:T(8,128)(2,1)} %tokens.3, ...), custom_call_target="tpu_custom_call" | custom-call | tf_op jit(solution)/shard_map/front/pallas_call | solution.py:778
  109.3 1.0 slice_reduce_fusion.2
  110.3 3.7 %multiply_reduce_fusion.2 = (f32[128]{0:T(128)S(1)}, f32[128,1280]{1,0:T(8,128)S(1)}) fusion(f32[1280]{0:T(1024)S(1)} %get-tuple-element.53, bf16[128,2048]{1,0:T(8,128)(2,1)} %get-tuple-element.32.attended, bf16[2048,1280]{1,0:T(8,128)(2,1)} %get-tuple-element.33, bf16[128,1280]{1,0:T(8,128)(2,1)S(1)} %bitcast.68), kind=kOutput, calls=%fused_computation.20 | convolution fusion | flops 671907712 | bytes 6755840 | tf_op jit(solution)/shard_map/dot_general | solution.py:48
  114.1 0.1 multiply_convert_fusion.1.normed_two
  114.2 0.7 multiply_convert_fusion
  114.9 1.4 copy-done
  116.4 0.0 copy-done.3
  116.4 1.2 convert_reduce_fusion.1
  117.7 1.4 fusion.5
  119.1 1.3 multiply_reduce_fusion
  120.4 0.3 convert_reduce_fusion.2
  120.7 0.0 copy-start.2
  120.7 2.6 %convolution_convert_fusion.pack = bf16[128,2048]{1,0:T(8,128)(2,1)} fusion(bf16[128,1280]{1,0:T(8,128)(2,1)S(1)} %get-tuple-element.55.d_branch, bf16[2048,1280]{1,0:T(8,128)(2,1)S(1)} %bitcast.64), kind=kOutput, calls=%fused_computation.10 | convolution fusion | flops 671350784 | bytes 6094848 | tf_op jit(solution)/shard_map/dot_general | solution.py:52
  123.4 0.6 pad.9.vector_grads
  124.0 118.3 %rear.1 = (bf16[2,64,1280]{2,1,0:T(8,128)(2,1)}, bf16[8,32,512]{2,1,0:T(8,128)(2,1)}, f32[32,1280]{1,0:T(8,128)}) custom-call(bf16[128,2048]{1,0:T(8,128)(2,1)} %convolution_convert_fusion.pack, bf16[8192,256]{1,0:T(8,128)(2,1)} %bitcast.65, bf16[4,512,128]{2,1,0:T(8,128)(2,1)} %get-tuple-element.38.queries_hbm, s32[4,1,512]{2,1,0:T(1,128)} %get-tuple-element.39.starts, ...), custom_call_target="tpu_custom_call" | custom-call | tf_op jit(solution)/shard_map/rear/pallas_call | solution.py:1248
  242.4 0.0 copy-start.12
  242.4 1.7 fusion.8
  244.2 1.0 convert_element_type.68
  245.3 0.1 copy.37
  245.4 0.6 divide_multiply_fusion
  246.0 0.1 constant_dynamic-slice_fusion
  246.1 0.6 slice_bitcast_fusion.2
  246.7 0.1 fusion.9
  246.8 0.1 reshape.122
  246.9 0.0 copy-start.10
  246.9 0.1 reshape.123
  247.1 0.0 copy-start.11
  247.1 0.1 multiply_reduce_fusion.3
  247.2 0.1 reshape.121
  247.3 0.0 copy-start.9
  247.3 0.1 multiply_reduce_fusion.5
  247.5 0.5 convert_divide_fusion
  248.0 0.7 copy.46
  (58 shorter events, 0.4 us)
Async XLA Ops:
  0.6 109.6 %copy-start.4 = (bf16[2,64,1280]{2,1,0:T(8,128)(2,1)S(1)}, bf16[2,64,1280]{2,1,0:T(8,128)(2,1)}, u32[]{:S(2)}) copy-start(bf16[2,64,1280]{2,1,0:T(8,128)(2,1)} %tokens.3) | copy-start | bytes 983044
  110.3 3.9 %copy-start.1 = (bf16[1280,1280]{1,0:T(8,128)(2,1)S(1)}, bf16[1280,1280]{1,0:T(8,128)(2,1)}, u32[]{:S(2)}) copy-start(bf16[1280,1280]{1,0:T(8,128)(2,1)} %get-tuple-element.35) | copy-start | bytes 9830404
  114.2 3.5 %copy-start.6 = (bf16[128,1280]{1,0:T(8,128)(2,1)}, bf16[128,1280]{1,0:T(8,128)(2,1)S(1)}, u32[]{:S(2)}) copy-start(bf16[128,1280]{1,0:T(8,128)(2,1)S(1)} %multiply_convert_fusion.1.normed_two) | copy-start | bytes 983044
  114.2 2.2 copy-start
  114.2 2.2 copy-start.3
  114.9 2.8 %copy-start.5 = (bf16[128,1280]{1,0:T(8,128)(2,1)}, bf16[128,1280]{1,0:T(8,128)(2,1)S(1)}, u32[]{:S(2)}) copy-start(bf16[128,1280]{1,0:T(8,128)(2,1)S(1)} %get-tuple-element.72.activated) | copy-start | bytes 983044
  116.4 4.3 %slice-start = ((s8[5242880]{0:T(1024)(128)(4,1)}), s8[4194304]{0:T(1024)(128)(4,1)S(1)}, s32[]{:S(2)}) async-start(s8[5242880]{0:T(1024)(128)(4,1)} %bitcast.63), calls=%async_computation | async-start | bytes 8388608
  117.7 2.7 %copy-start.7 = (bf16[128,1280]{1,0:T(8,128)(2,1)}, bf16[128,1280]{1,0:T(8,128)(2,1)S(1)}, u32[]{:S(2)}) copy-start(bf16[128,1280]{1,0:T(8,128)(2,1)S(1)} %get-tuple-element.76.d_pre) | copy-start | bytes 983044
  117.7 3.0 %slice-start.1 = ((s8[5242880]{0:T(1024)(128)(4,1)}), s8[1048576]{0:T(1024)(128)(4,1)S(1)}, s32[]{:S(2)}) async-start(s8[5242880]{0:T(1024)(128)(4,1)} %bitcast.63), calls=%async_computation.1 | async-start | bytes 2097152
  120.7 3.3 %copy-start.2 = (bf16[128,1280]{1,0:T(8,128)(2,1)}, bf16[128,1280]{1,0:T(8,128)(2,1)S(1)}, u32[]{:S(2)}) copy-start(bf16[128,1280]{1,0:T(8,128)(2,1)S(1)} %get-tuple-element.55.d_branch) | copy-start | bytes 983044
  124.0 121.4 %copy-start.16 = (f32[80]{0:T(128)S(1)}, f32[80]{0:T(128)}, u32[]{:S(2)}) copy-start(f32[80]{0:T(128)} %param.34) | copy-start | bytes 964
  242.4 4.7 %copy-start.13 = (bf16[10,1280]{1,0:T(8,128)(2,1)S(1)}, bf16[10,1280]{1,0:T(8,128)(2,1)}, u32[]{:S(2)}) copy-start(bf16[10,1280]{1,0:T(8,128)(2,1)} %param.24) | copy-start | bytes 76804
  242.4 4.7 %copy-start.14 = (bf16[10,1280]{1,0:T(8,128)(2,1)S(1)}, bf16[10,1280]{1,0:T(8,128)(2,1)}, u32[]{:S(2)}) copy-start(bf16[10,1280]{1,0:T(8,128)(2,1)} %param.23) | copy-start | bytes 76804
  242.4 4.9 %copy-start.12 = (bf16[10,1280]{1,0:T(8,128)(2,1)S(1)}, bf16[10,1280]{1,0:T(8,128)(2,1)}, u32[]{:S(2)}) copy-start(bf16[10,1280]{1,0:T(8,128)(2,1)} %param.22) | copy-start | bytes 76804
  242.4 5.1 %copy-start.15 = (bf16[10]{0:T(256)(128)(2,1)S(1)}, bf16[10]{0:T(256)(128)(2,1)}, u32[]{:S(2)}) copy-start(bf16[10]{0:T(256)(128)(2,1)} %param.21) | copy-start | bytes 64
  242.4 5.6 %copy-start.8 = (bf16[2,64,1280]{2,1,0:T(8,128)(2,1)S(1)}, bf16[2,64,1280]{2,1,0:T(8,128)(2,1)}, u32[]{:S(2)}) copy-start(bf16[2,64,1280]{2,1,0:T(8,128)(2,1)} %get-tuple-element.98) | copy-start | bytes 983044
  246.9 1.8 copy-start.10
  247.1 1.7 copy-start.11
  247.3 1.4 copy-start.9
